TPU v7x, 512 devices: a whole 4x8x8 slice. The times are simulated.
512 devices in a mesh: tm: 128 (over z_lo, x, y), rows: 4 (over z_hi, core).
Axes of the slice: x: 4, y: 8, z: 8 (z_hi: 2, z_lo: 4; z = z_hi * 4 + z_lo), core: 2. Of those that a mesh axis runs over, the one named last changes fastest.
Arguments:
- trajectory: bfloat16 [128, 2, 64, 128], P('tm', None, 'rows'), may hold values from -6 to 6
- observed: float32 [128, 2, 1024], P('tm'), may hold values from -6 to 6
- station_rows: int32 [1024], replicated, may hold values from 0 to 63
- station_cols: int32 [1024], replicated, may hold values from 0 to 127
- step_index: int32 [1], replicated, may hold values from 32 to 223
- w_in: bfloat16 [96, 10, 3, 3], replicated, may hold values from -0.625 to 0.625
- w_mid: bfloat16 [3, 3, 9216], replicated, may hold values from -0.21875 to 0.21875
- w_out: bfloat16 [2, 96, 3, 3], replicated, may hold values from -0.21875 to 0.21875
- noise_gain: float32 [96], replicated, may hold values from -4 to 4
Outputs:
- posterior: float32 [128, 2, 64, 128], P('tm', None, 'rows')
All inputs are finite; a program needn't handle non-finite values.
Results may differ from a plain program's by a relative error of at most 0.009.
Values may be sent and summed in bfloat16 or wider, within the bound.
No kernel may reach another device: no remote copies, remote signals or barrier semaphores. Data moves between devices by JAX's collectives and lax.ppermute only.
A program may use at most 64 MiB of HBM per device.

v0:
```python
import math

import jax
import jax.numpy as jnp
from jax import lax
from jax.sharding import PartitionSpec as P

NSTEPS = 256


def from_behind(value, axis, steps):
    count = lax.axis_size(axis)
    leading, last = (max(0, -steps), min(count, count - steps))
    return lax.ppermute(value, axis, [(source, source + steps) for source in range(leading, last)])


def extended(block, sides, width):
    for axis, dim in sides:
        count = lax.axis_size(axis)
        forward = [(i, i + 1) for i in range(count - 1)]
        forward.append((count - 1, 0))
        backward = [(target, source) for source, target in forward]
        low = lax.ppermute(
            lax.slice_in_dim(block, block.shape[dim] - width, None, axis=dim), axis, forward
        )
        high = lax.ppermute(lax.slice_in_dim(block, 0, width, axis=dim), axis, backward)
        block = jnp.concatenate([low, block, high], axis=dim)
    return block


def noise_level(step_index):
    phase_time = (step_index[0].astype(jnp.float32) + 0.5) / NSTEPS
    noise_alpha = jnp.cos(0.5 * math.pi * phase_time)
    noise_sigma = jnp.sin(0.5 * math.pi * phase_time)
    obs_kappa = 1.0 + (noise_sigma / noise_alpha) ** 2
    return (noise_alpha, noise_sigma, obs_kappa)


def conv_rows(inputs, weight):
    padded = jnp.concatenate([inputs[:, :, -1:], inputs, inputs[:, :, :1]], axis=2)
    result = lax.conv_general_dilated(
        padded[None],
        weight,
        (1, 1),
        "VALID",
        dimension_numbers=("NCHW", "OIHW", "NCHW"),
        preferred_element_type=jnp.float32,
    )
    return result[0]


def adjoint(weight):
    return jnp.transpose(jnp.flip(weight, (2, 3)), (1, 0, 2, 3))


def silu_slope(values):
    logistic = jax.nn.sigmoid(values)
    return logistic * (1.0 + values * (1.0 - logistic))


def station_field(denoised, obs_row, station_rows, station_cols, first_row, total_rows, obs_kappa):
    height = denoised.shape[1]
    offset = jnp.mod(station_rows - first_row, total_rows)
    inside = offset < height
    safe_rows = jnp.where(inside, offset, 0)
    picked = denoised[:, safe_rows, station_cols]
    misfit = jnp.where(inside[None, :], (obs_row - picked) / obs_kappa, 0.0)
    return jnp.zeros_like(denoised).at[:, safe_rows, station_cols].add(misfit)


def on_device(
    trajectory, observed, station_rows, station_cols, step_index, w_in, w_mid, w_out, noise_gain
):
    noise_alpha, noise_sigma, obs_kappa = noise_level(step_index)
    channels = w_in.shape[0]
    mid_kernel = jnp.transpose(w_mid.reshape(3, 3, channels, channels), (2, 3, 0, 1))
    own_state = trajectory[0]
    obs_row = observed[0]
    rows_dev = own_state.shape[1]
    total_rows = rows_dev * lax.axis_size("rows")
    first_row = lax.axis_index("rows") * rows_dev
    prev_one = from_behind(own_state, "tm", 1)
    next_one = from_behind(own_state, "tm", -1)
    prev_two = from_behind(own_state, "tm", 2)
    next_two = from_behind(own_state, "tm", -2)
    blanket = jnp.concatenate([prev_two, prev_one, own_state, next_one, next_two], axis=0)
    shift_bias = (noise_sigma * noise_gain)[:, None, None]
    w_in_adj = adjoint(w_in)
    w_mid_adj = adjoint(mid_kernel)
    w_out_adj = adjoint(w_out)
    padded_in = extended(blanket, (("rows", 1),), 1)
    pre_one = conv_rows(padded_in, w_in) + shift_bias
    hidden_one = jax.nn.silu(pre_one).astype(jnp.bfloat16)
    pre_two = conv_rows(extended(hidden_one, (("rows", 1),), 1), mid_kernel)
    hidden_two = (hidden_one.astype(jnp.float32) + jax.nn.silu(pre_two)).astype(jnp.bfloat16)
    noise_pred = conv_rows(extended(hidden_two, (("rows", 1),), 1), w_out)
    denoised = (own_state.astype(jnp.float32) - noise_sigma * noise_pred) / noise_alpha
    obs_pull = station_field(
        denoised, obs_row, station_rows, station_cols, first_row, total_rows, obs_kappa
    )
    pull_low = obs_pull.astype(jnp.bfloat16)
    grad_two = conv_rows(extended(pull_low, (("rows", 1),), 1), w_out_adj)
    slope_two = (grad_two * silu_slope(pre_two)).astype(jnp.bfloat16)
    grad_one = grad_two + conv_rows(extended(slope_two, (("rows", 1),), 1), w_mid_adj)
    slope_one = (grad_one * silu_slope(pre_one)).astype(jnp.bfloat16)
    grad_in = conv_rows(extended(slope_one, (("rows", 1),), 1), w_in_adj)
    grad_far_back = grad_in[0:2]
    grad_near_back = grad_in[2:4]
    grad_own = grad_in[4:6]
    grad_near_on = grad_in[6:8]
    grad_far_on = grad_in[8:10]
    one_later = from_behind(grad_near_back, "tm", -1)
    two_later = from_behind(grad_far_back, "tm", -2)
    one_earlier = from_behind(grad_near_on, "tm", 1)
    two_earlier = from_behind(grad_far_on, "tm", 2)
    summed = grad_own + one_later + two_later + one_earlier + two_earlier
    posterior = -noise_pred / noise_sigma + (obs_pull - noise_sigma * summed) / noise_alpha
    return posterior[None]


def solution(mesh):
    return jax.shard_map(
        on_device,
        mesh=mesh,
        in_specs=(
            P("tm", None, "rows", None),
            P("tm", None, None),
            P(),
            P(),
            P(),
            P(),
            P(),
            P(),
            P(),
        ),
        out_specs=P("tm", None, "rows", None),
        check_vma=False,
    )
```

profile of v0, /device:TPU:63, one launch (start us, length us, event | category | flops | bytes accessed | tf_op | source)
XLA Modules:
  0.0 177.6 jit_solution(597541084487714057)
XLA Ops:
  0.0 3.9 %collective-permute-start.3 = (bf16[2,16,128]{2,1,0:T(8,128)(2,1)}, bf16[2,16,128]{2,1,0:T(8,128)(2,1)S(1)}, u32[]{:S(2)}, u32[]{:S(2)}) collective-permute-start(bf16[2,16,128]{2,1,0:T(8,128)(2,1)} %bitcast.213), channel_id=1, source_target_pairs={{8,0},{12,4},{16,8},{20,12},{24,16},{28,20},{32,24},{36,28},{40,32... | collective-permute-start | bytes 24584 | tf_op jit(solution)/shard_map/ppermute | solution.py:14
  3.9 3.0 %collective-permute-start.2 = (bf16[2,16,128]{2,1,0:T(8,128)(2,1)}, bf16[2,16,128]{2,1,0:T(8,128)(2,1)S(1)}, u32[]{:S(2)}, u32[]{:S(2)}) collective-permute-start(bf16[2,16,128]{2,1,0:T(8,128)(2,1)} %bitcast.214), channel_id=1, source_target_pairs={{4,0},{8,4},{12,8},{16,12},{20,16},{24,20},{28,24},{32,28},{36,32}... | collective-permute-start | bytes 24584 | tf_op jit(solution)/shard_map/ppermute | solution.py:14
  6.9 6.5 %collective-permute-start.1 = (bf16[2,16,128]{2,1,0:T(8,128)(2,1)}, bf16[2,16,128]{2,1,0:T(8,128)(2,1)S(1)}, u32[]{:S(2)}, u32[]{:S(2)}) collective-permute-start(bf16[2,16,128]{2,1,0:T(8,128)(2,1)} %bitcast.215), channel_id=1, source_target_pairs={{0,4},{4,8},{8,12},{12,16},{16,20},{20,24},{24,28},{28,32},{32,36}... | collective-permute-start | bytes 24584 | tf_op jit(solution)/shard_map/ppermute | solution.py:14
  13.4 2.4 %collective-permute-start = (bf16[2,16,128]{2,1,0:T(8,128)(2,1)}, bf16[2,16,128]{2,1,0:T(8,128)(2,1)S(1)}, u32[]{:S(2)}, u32[]{:S(2)}) collective-permute-start(bf16[2,16,128]{2,1,0:T(8,128)(2,1)} %bitcast.216), channel_id=1, source_target_pairs={{0,8},{4,12},{8,16},{12,20},{16,24},{20,28},{24,32},{28,36},{32,40... | collective-permute-start | bytes 24584 | tf_op jit(solution)/shard_map/ppermute | solution.py:14
  20.2 12.7 %collective-permute-start.4 = (bf16[10,1,128]{2,1,0:T(2,128)(2,1)S(1)}, bf16[10,1,128]{2,1,0:T(2,128)(2,1)S(1)}, u32[]{:S(2)}, u32[]{:S(2)}) collective-permute-start(bf16[10,1,128]{2,1,0:T(2,128)(2,1)S(1)} %get-tuple-element.22), channel_id=1, source_target_pairs={{0,1},{1,2},{2,3},{3,0},{4,5},{5,6},{6,7},{7,4},{8,9},{9,10},{10,1... | collective-permute-start | bytes 7688 | tf_op jit(solution)/shard_map/ppermute | solution.py:23
  32.9 1.9 %collective-permute-start.5 = (bf16[10,1,128]{2,1,0:T(2,128)(2,1)S(1)}, bf16[10,1,128]{2,1,0:T(2,128)(2,1)S(1)}, u32[]{:S(2)}, u32[]{:S(2)}) collective-permute-start(bf16[10,1,128]{2,1,0:T(2,128)(2,1)S(1)} %get-tuple-element.23), channel_id=1, source_target_pairs={{1,0},{2,1},{3,2},{0,3},{5,4},{6,5},{7,6},{4,7},{9,8},{10,9},{11,1... | collective-permute-start | bytes 7688 | tf_op jit(solution)/shard_map/ppermute | solution.py:26
  35.6 6.2 %collective-permute-done.5 = bf16[10,1,128]{2,1,0:T(2,128)(2,1)S(1)} collective-permute-done((bf16[10,1,128]{2,1,0:T(2,128)(2,1)S(1)}, bf16[10,1,128]{2,1,0:T(2,128)(2,1)S(1)}, u32[]{:S(2)}, u32[]{:S(2)}) %collective-permute-start.5) | collective-permute-done | bytes 2592 | tf_op jit(solution)/shard_map/ppermute | solution.py:26
  45.3 1.9 %collective-permute-start.6 = (bf16[96,1,128]{0,1,2:T(2,128)(2,1)S(1)}, bf16[96,1,128]{0,1,2:T(2,128)(2,1)S(1)}, u32[]{:S(2)}, u32[]{:S(2)}) collective-permute-start(bf16[96,1,128]{0,1,2:T(2,128)(2,1)S(1)} %get-tuple-element.16), channel_id=1, source_target_pairs={{0,1},{1,2},{2,3},{3,0},{4,5},{5,6},{6,7},{7,4},{8,9},{9,10},{10,1... | collective-permute-start | bytes 73736 | tf_op jit(solution)/shard_map/ppermute | solution.py:23
  47.3 2.4 %collective-permute-start.7 = (bf16[96,1,128]{0,1,2:T(2,128)(2,1)S(1)}, bf16[96,1,128]{0,1,2:T(2,128)(2,1)S(1)}, u32[]{:S(2)}, u32[]{:S(2)}) collective-permute-start(bf16[96,1,128]{0,1,2:T(2,128)(2,1)S(1)} %get-tuple-element.17), channel_id=1, source_target_pairs={{1,0},{2,1},{3,2},{0,3},{5,4},{6,5},{7,6},{4,7},{9,8},{10,9},{11,1... | collective-permute-start | bytes 73736 | tf_op jit(solution)/shard_map/ppermute | solution.py:26
  50.5 7.0 %collective-permute-done.7 = bf16[96,1,128]{0,1,2:T(2,128)(2,1)S(1)} collective-permute-done((bf16[96,1,128]{0,1,2:T(2,128)(2,1)S(1)}, bf16[96,1,128]{0,1,2:T(2,128)(2,1)S(1)}, u32[]{:S(2)}, u32[]{:S(2)}) %collective-permute-start.7) | collective-permute-done | bytes 24608 | tf_op jit(solution)/shard_map/ppermute | solution.py:26
  60.6 1.9 %collective-permute-start.8 = (bf16[96,1,128]{0,1,2:T(2,128)(2,1)S(1)}, bf16[96,1,128]{0,1,2:T(2,128)(2,1)S(1)}, u32[]{:S(2)}, u32[]{:S(2)}) collective-permute-start(bf16[96,1,128]{0,1,2:T(2,128)(2,1)S(1)} %get-tuple-element.14), channel_id=1, source_target_pairs={{0,1},{1,2},{2,3},{3,0},{4,5},{5,6},{6,7},{7,4},{8,9},{9,10},{10,1... | collective-permute-start | bytes 73736 | tf_op jit(solution)/shard_map/ppermute | solution.py:23
  62.5 2.6 %collective-permute-start.9 = (bf16[96,1,128]{0,1,2:T(2,128)(2,1)S(1)}, bf16[96,1,128]{0,1,2:T(2,128)(2,1)S(1)}, u32[]{:S(2)}, u32[]{:S(2)}) collective-permute-start(bf16[96,1,128]{0,1,2:T(2,128)(2,1)S(1)} %get-tuple-element.15), channel_id=1, source_target_pairs={{1,0},{2,1},{3,2},{0,3},{5,4},{6,5},{7,6},{4,7},{9,8},{10,9},{11,1... | collective-permute-start | bytes 73736 | tf_op jit(solution)/shard_map/ppermute | solution.py:26
  66.9 5.8 %collective-permute-done.9 = bf16[96,1,128]{0,1,2:T(2,128)(2,1)S(1)} collective-permute-done((bf16[96,1,128]{0,1,2:T(2,128)(2,1)S(1)}, bf16[96,1,128]{0,1,2:T(2,128)(2,1)S(1)}, u32[]{:S(2)}, u32[]{:S(2)}) %collective-permute-start.9) | collective-permute-done | bytes 24608 | tf_op jit(solution)/shard_map/ppermute | solution.py:26
  74.0 12.3 %fusion.47 = f32[16,8,17,2]{1,3,2,0:T(2,128)S(1)} fusion(bf16[2,96,3,3]{1,0,3,2:T(2,128)(2,1)S(1)} %copy-done.7, bf16[96,18,1,7,2]{0,3,4,1,2:T(8,128)(2,1)S(1)} %slice.172, bf16[96,18,1,8,17]{0,3,4,1,2:T(8,128)(2,1)S(1)} %copy.164), kind=kOutput, calls=%fused_computation.77 | convolution fusion | flops 9096192 | bytes 539264 | tf_op jit(solution)/shard_map/conv_general_dilated | solution.py:41
  87.8 13.3 %scatter_custom_fusion = f32[2,2048]{0,1:T(8,128)} fusion(s32[1024]{0:T(1024)} %broadcast_select_fusion, f32[1,2,1024]{1,2,0:T(8,128)} %copy.167, f32[]{:T(128)} %constant.19.clone.1, f32[]{:T(128)S(6)} %add.76, pred[1024]{0:T(1024)(128)(4,1)} %broadcast_compare_fusion, f32[2,16,128]{0,2,1:T(8,128)S(1)} %copy.169, s32[1024]{0:T(1024)S(1)} %bitcast.217), kind=kCustom, calls=%fused_computation.79 | custom fusion | flops 8192 | bytes 563204
  102.7 1.9 %collective-permute-start.10 = (bf16[2,1,128]{2,1,0:T(2,128)(2,1)S(1)}, bf16[2,1,128]{2,1,0:T(2,128)(2,1)S(1)}, u32[]{:S(2)}, u32[]{:S(2)}) collective-permute-start(bf16[2,1,128]{2,1,0:T(2,128)(2,1)S(1)} %get-tuple-element.27), channel_id=1, source_target_pairs={{0,1},{1,2},{2,3},{3,0},{4,5},{5,6},{6,7},{7,4},{8,9},{9,10},{10,1... | collective-permute-start | bytes 1544 | tf_op jit(solution)/shard_map/ppermute | solution.py:23
  104.6 2.6 %collective-permute-start.11 = (bf16[2,1,128]{2,1,0:T(2,128)(2,1)S(1)}, bf16[2,1,128]{2,1,0:T(2,128)(2,1)S(1)}, u32[]{:S(2)}, u32[]{:S(2)}) collective-permute-start(bf16[2,1,128]{2,1,0:T(2,128)(2,1)S(1)} %get-tuple-element.26), channel_id=1, source_target_pairs={{1,0},{2,1},{3,2},{0,3},{5,4},{6,5},{7,6},{4,7},{9,8},{10,9},{11,1... | collective-permute-start | bytes 1544 | tf_op jit(solution)/shard_map/ppermute | solution.py:26
  107.3 6.1 %collective-permute-done.11 = bf16[2,1,128]{2,1,0:T(2,128)(2,1)S(1)} collective-permute-done((bf16[2,1,128]{2,1,0:T(2,128)(2,1)S(1)}, bf16[2,1,128]{2,1,0:T(2,128)(2,1)S(1)}, u32[]{:S(2)}, u32[]{:S(2)}) %collective-permute-start.11) | collective-permute-done | bytes 544 | tf_op jit(solution)/shard_map/ppermute | solution.py:26
  115.8 2.0 %collective-permute-start.12 = (bf16[96,1,128]{0,1,2:T(2,128)(2,1)S(1)}, bf16[96,1,128]{0,1,2:T(2,128)(2,1)S(1)}, u32[]{:S(2)}, u32[]{:S(2)}) collective-permute-start(bf16[96,1,128]{0,1,2:T(2,128)(2,1)S(1)} %get-tuple-element.12), channel_id=1, source_target_pairs={{0,1},{1,2},{2,3},{3,0},{4,5},{5,6},{6,7},{7,4},{8,9},{9,10},{10,1... | collective-permute-start | bytes 73736 | tf_op jit(solution)/shard_map/ppermute | solution.py:23
  117.8 2.4 %collective-permute-start.13 = (bf16[96,1,128]{0,1,2:T(2,128)(2,1)S(1)}, bf16[96,1,128]{0,1,2:T(2,128)(2,1)S(1)}, u32[]{:S(2)}, u32[]{:S(2)}) collective-permute-start(bf16[96,1,128]{0,1,2:T(2,128)(2,1)S(1)} %get-tuple-element.13), channel_id=1, source_target_pairs={{1,0},{2,1},{3,2},{0,3},{5,4},{6,5},{7,6},{4,7},{9,8},{10,9},{11,1... | collective-permute-start | bytes 73736 | tf_op jit(solution)/shard_map/ppermute | solution.py:26
  120.2 7.8 %collective-permute-done.13 = bf16[96,1,128]{0,1,2:T(2,128)(2,1)S(1)} collective-permute-done((bf16[96,1,128]{0,1,2:T(2,128)(2,1)S(1)}, bf16[96,1,128]{0,1,2:T(2,128)(2,1)S(1)}, u32[]{:S(2)}, u32[]{:S(2)}) %collective-permute-start.13) | collective-permute-done | bytes 24608 | tf_op jit(solution)/shard_map/ppermute | solution.py:26
  130.8 1.9 %collective-permute-start.14 = (bf16[96,1,128]{0,1,2:T(2,128)(2,1)S(1)}, bf16[96,1,128]{0,1,2:T(2,128)(2,1)S(1)}, u32[]{:S(2)}, u32[]{:S(2)}) collective-permute-start(bf16[96,1,128]{0,1,2:T(2,128)(2,1)S(1)} %get-tuple-element.10), channel_id=1, source_target_pairs={{0,1},{1,2},{2,3},{3,0},{4,5},{5,6},{6,7},{7,4},{8,9},{9,10},{10,1... | collective-permute-start | bytes 73736 | tf_op jit(solution)/shard_map/ppermute | solution.py:23
  132.7 2.4 %collective-permute-start.15 = (bf16[96,1,128]{0,1,2:T(2,128)(2,1)S(1)}, bf16[96,1,128]{0,1,2:T(2,128)(2,1)S(1)}, u32[]{:S(2)}, u32[]{:S(2)}) collective-permute-start(bf16[96,1,128]{0,1,2:T(2,128)(2,1)S(1)} %get-tuple-element.11), channel_id=1, source_target_pairs={{1,0},{2,1},{3,2},{0,3},{5,4},{6,5},{7,6},{4,7},{9,8},{10,9},{11,1... | collective-permute-start | bytes 73736 | tf_op jit(solution)/shard_map/ppermute | solution.py:26
  135.1 7.8 %collective-permute-done.15 = bf16[96,1,128]{0,1,2:T(2,128)(2,1)S(1)} collective-permute-done((bf16[96,1,128]{0,1,2:T(2,128)(2,1)S(1)}, bf16[96,1,128]{0,1,2:T(2,128)(2,1)S(1)}, u32[]{:S(2)}, u32[]{:S(2)}) %collective-permute-start.15) | collective-permute-done | bytes 24608 | tf_op jit(solution)/shard_map/ppermute | solution.py:26
  145.1 2.6 %fusion.101 = (f32[16,8,17,2]{3,1,2,0:T(8,128)S(1)}, f32[16,8,17,2]{3,1,2,0:T(8,128)}, f32[16,8,17,2]{3,1,2,0:T(8,128)}, f32[16,8,17,2]{3,1,2,0:T(8,128)S(1)}, f32[16,8,17,2]{3,1,2,0:T(8,128)S(1)}) fusion(f32[16,8,17,10]{3,1,2,0:T(8,128)S(1)} %convolution_select_fusion), kind=kLoop, calls=%fused_computation.162 | loop fusion | bytes 174080 | tf_op jit(solution)/shard_map/conv_general_dilated | solution.py:41
  147.7 2.2 %copy.190 = f32[16,8,17,2]{2,1,0,3:T(8,128)S(1)} copy(f32[16,8,17,2]{3,1,2,0:T(8,128)} %get-tuple-element.6) | data formatting | bytes 34816 | tf_op jit(solution)/shard_map/conv_general_dilated | solution.py:41
  151.3 3.9 %collective-permute-start.19 = (f32[2,16,128]{2,1,0:T(8,128)S(1)}, f32[2,16,128]{2,1,0:T(8,128)}, u32[]{:S(2)}, u32[]{:S(2)}) collective-permute-start(f32[2,16,128]{2,1,0:T(8,128)S(1)} %slice_bitcast_fusion.4), channel_id=1, source_target_pairs={{0,8},{4,12},{8,16},{12,20},{16,24},{20,28},{24,32},{28,36},{32,40... | collective-permute-start | bytes 49160 | tf_op jit(solution)/shard_map/ppermute | solution.py:14
  155.2 2.2 %copy.189 = f32[16,8,17,2]{2,1,0,3:T(8,128)S(1)} copy(f32[16,8,17,2]{3,1,2,0:T(8,128)} %get-tuple-element.7) | data formatting | bytes 34816 | tf_op jit(solution)/shard_map/conv_general_dilated | solution.py:41
  159.4 1.9 %collective-permute-start.18 = (f32[2,16,128]{2,1,0:T(8,128)}, f32[2,16,128]{2,1,0:T(8,128)}, u32[]{:S(2)}, u32[]{:S(2)}) collective-permute-start(f32[2,16,128]{2,1,0:T(8,128)} %slice_bitcast_fusion.5), channel_id=1, source_target_pairs={{0,4},{4,8},{8,12},{12,16},{16,20},{20,24},{24,28},{28,32},{32,36}... | collective-permute-start | bytes 49160 | tf_op jit(solution)/shard_map/ppermute | solution.py:14
  162.4 4.1 %collective-permute-start.17 = (f32[2,16,128]{2,1,0:T(8,128)S(1)}, f32[2,16,128]{2,1,0:T(8,128)S(1)}, u32[]{:S(2)}, u32[]{:S(2)}) collective-permute-start(f32[2,16,128]{2,1,0:T(8,128)S(1)} %slice_bitcast_fusion.6), channel_id=1, source_target_pairs={{8,0},{12,4},{16,8},{20,12},{24,16},{28,20},{32,24},{36,28},{40,32... | collective-permute-start | bytes 49160 | tf_op jit(solution)/shard_map/ppermute | solution.py:14
  167.6 1.9 %collective-permute-start.16 = (f32[2,16,128]{2,1,0:T(8,128)S(1)}, f32[2,16,128]{2,1,0:T(8,128)S(1)}, u32[]{:S(2)}, u32[]{:S(2)}) collective-permute-start(f32[2,16,128]{2,1,0:T(8,128)S(1)} %slice_bitcast_fusion.7), channel_id=1, source_target_pairs={{4,0},{8,4},{12,8},{16,12},{20,16},{24,20},{28,24},{32,28},{36,32}... | collective-permute-start | bytes 49160 | tf_op jit(solution)/shard_map/ppermute | solution.py:14
  172.0 4.3 %collective-permute-done.16 = f32[2,16,128]{2,1,0:T(8,128)S(1)} collective-permute-done((f32[2,16,128]{2,1,0:T(8,128)S(1)}, f32[2,16,128]{2,1,0:T(8,128)S(1)}, u32[]{:S(2)}, u32[]{:S(2)}) %collective-permute-start.16) | collective-permute-done | bytes 16416 | tf_op jit(solution)/shard_map/ppermute | solution.py:14
  (124 shorter events, 34.3 us)
Async XLA Ops:
  0.0 43.4 %copy-start = (bf16[96,10,3,3]{0,3,2,1:T(4,128)(2,1)S(1)}, bf16[96,10,3,3]{0,3,2,1:T(4,128)(2,1)}, u32[]{:S(2)}) copy-start(bf16[96,10,3,3]{0,3,2,1:T(4,128)(2,1)} %param.14) | copy-start | bytes 51844
  0.0 20.2 %collective-permute-start.3 = (bf16[2,16,128]{2,1,0:T(8,128)(2,1)}, bf16[2,16,128]{2,1,0:T(8,128)(2,1)S(1)}, u32[]{:S(2)}, u32[]{:S(2)}) collective-permute-start(bf16[2,16,128]{2,1,0:T(8,128)(2,1)} %bitcast.213), channel_id=1, source_target_pairs={{8,0},{12,4},{16,8},{20,12},{24,16},{28,20},{32,24},{36,28},{40,32... | collective-permute-start | bytes 24584 | tf_op jit(solution)/shard_map/ppermute | solution.py:14
  3.9 16.2 %collective-permute-start.2 = (bf16[2,16,128]{2,1,0:T(8,128)(2,1)}, bf16[2,16,128]{2,1,0:T(8,128)(2,1)S(1)}, u32[]{:S(2)}, u32[]{:S(2)}) collective-permute-start(bf16[2,16,128]{2,1,0:T(8,128)(2,1)} %bitcast.214), channel_id=1, source_target_pairs={{4,0},{8,4},{12,8},{16,12},{20,16},{24,20},{28,24},{32,28},{36,32}... | collective-permute-start | bytes 24584 | tf_op jit(solution)/shard_map/ppermute | solution.py:14
  6.9 12.5 %collective-permute-start.1 = (bf16[2,16,128]{2,1,0:T(8,128)(2,1)}, bf16[2,16,128]{2,1,0:T(8,128)(2,1)S(1)}, u32[]{:S(2)}, u32[]{:S(2)}) collective-permute-start(bf16[2,16,128]{2,1,0:T(8,128)(2,1)} %bitcast.215), channel_id=1, source_target_pairs={{0,4},{4,8},{8,12},{12,16},{16,20},{20,24},{24,28},{28,32},{32,36}... | collective-permute-start | bytes 24584 | tf_op jit(solution)/shard_map/ppermute | solution.py:14
  13.4 6.0 %collective-permute-start = (bf16[2,16,128]{2,1,0:T(8,128)(2,1)}, bf16[2,16,128]{2,1,0:T(8,128)(2,1)S(1)}, u32[]{:S(2)}, u32[]{:S(2)}) collective-permute-start(bf16[2,16,128]{2,1,0:T(8,128)(2,1)} %bitcast.216), channel_id=1, source_target_pairs={{0,8},{4,12},{8,16},{12,20},{16,24},{20,28},{24,32},{28,36},{32,40... | collective-permute-start | bytes 24584 | tf_op jit(solution)/shard_map/ppermute | solution.py:14
  20.2 15.4 %collective-permute-start.4 = (bf16[10,1,128]{2,1,0:T(2,128)(2,1)S(1)}, bf16[10,1,128]{2,1,0:T(2,128)(2,1)S(1)}, u32[]{:S(2)}, u32[]{:S(2)}) collective-permute-start(bf16[10,1,128]{2,1,0:T(2,128)(2,1)S(1)} %get-tuple-element.22), channel_id=1, source_target_pairs={{0,1},{1,2},{2,3},{3,0},{4,5},{5,6},{6,7},{7,4},{8,9},{9,10},{10,1... | collective-permute-start | bytes 7688 | tf_op jit(solution)/shard_map/ppermute | solution.py:23
  32.9 8.8 %collective-permute-start.5 = (bf16[10,1,128]{2,1,0:T(2,128)(2,1)S(1)}, bf16[10,1,128]{2,1,0:T(2,128)(2,1)S(1)}, u32[]{:S(2)}, u32[]{:S(2)}) collective-permute-start(bf16[10,1,128]{2,1,0:T(2,128)(2,1)S(1)} %get-tuple-element.23), channel_id=1, source_target_pairs={{1,0},{2,1},{3,2},{0,3},{5,4},{6,5},{7,6},{4,7},{9,8},{10,9},{11,1... | collective-permute-start | bytes 7688 | tf_op jit(solution)/shard_map/ppermute | solution.py:26
  41.9 1.6 copy-start.9
  44.9 5.4 %copy-start.2 = (bf16[3,3,9216]{2,1,0:T(4,128)(2,1)S(1)}, bf16[3,3,9216]{2,1,0:T(4,128)(2,1)}, u32[]{:S(2)}) copy-start(bf16[3,3,9216]{2,1,0:T(4,128)(2,1)} %param.15) | copy-start | bytes 497668
  45.3 5.2 %collective-permute-start.6 = (bf16[96,1,128]{0,1,2:T(2,128)(2,1)S(1)}, bf16[96,1,128]{0,1,2:T(2,128)(2,1)S(1)}, u32[]{:S(2)}, u32[]{:S(2)}) collective-permute-start(bf16[96,1,128]{0,1,2:T(2,128)(2,1)S(1)} %get-tuple-element.16), channel_id=1, source_target_pairs={{0,1},{1,2},{2,3},{3,0},{4,5},{5,6},{6,7},{7,4},{8,9},{9,10},{10,1... | collective-permute-start | bytes 73736 | tf_op jit(solution)/shard_map/ppermute | solution.py:23
  47.3 10.2 %collective-permute-start.7 = (bf16[96,1,128]{0,1,2:T(2,128)(2,1)S(1)}, bf16[96,1,128]{0,1,2:T(2,128)(2,1)S(1)}, u32[]{:S(2)}, u32[]{:S(2)}) collective-permute-start(bf16[96,1,128]{0,1,2:T(2,128)(2,1)S(1)} %get-tuple-element.17), channel_id=1, source_target_pairs={{1,0},{2,1},{3,2},{0,3},{5,4},{6,5},{7,6},{4,7},{9,8},{10,9},{11,1... | collective-permute-start | bytes 73736 | tf_op jit(solution)/shard_map/ppermute | solution.py:26
  59.9 5.2 %copy-start.4 = (s32[1024]{0:T(1024)S(1)}, s32[1024]{0:T(1024)}, u32[]{:S(2)}) copy-start(s32[1024]{0:T(1024)} %param.11) | copy-start | bytes 12292
  59.9 5.9 %copy-start.5 = (f32[1,2,1024]{2,1,0:T(2,128)S(1)}, f32[1,2,1024]{2,1,0:T(2,128)}, u32[]{:S(2)}) copy-start(f32[1,2,1024]{2,1,0:T(2,128)} %param.10) | copy-start | bytes 24580
  60.6 6.3 %collective-permute-start.8 = (bf16[96,1,128]{0,1,2:T(2,128)(2,1)S(1)}, bf16[96,1,128]{0,1,2:T(2,128)(2,1)S(1)}, u32[]{:S(2)}, u32[]{:S(2)}) collective-permute-start(bf16[96,1,128]{0,1,2:T(2,128)(2,1)S(1)} %get-tuple-element.14), channel_id=1, source_target_pairs={{0,1},{1,2},{2,3},{3,0},{4,5},{5,6},{6,7},{7,4},{8,9},{9,10},{10,1... | collective-permute-start | bytes 73736 | tf_op jit(solution)/shard_map/ppermute | solution.py:23
  62.5 10.2 %collective-permute-start.9 = (bf16[96,1,128]{0,1,2:T(2,128)(2,1)S(1)}, bf16[96,1,128]{0,1,2:T(2,128)(2,1)S(1)}, u32[]{:S(2)}, u32[]{:S(2)}) collective-permute-start(bf16[96,1,128]{0,1,2:T(2,128)(2,1)S(1)} %get-tuple-element.15), channel_id=1, source_target_pairs={{1,0},{2,1},{3,2},{0,3},{5,4},{6,5},{7,6},{4,7},{9,8},{10,9},{11,1... | collective-permute-start | bytes 73736 | tf_op jit(solution)/shard_map/ppermute | solution.py:26
  73.4 0.7 copy-start.7
  74.0 12.6 %copy-start.6 = (pred[8,17]{1,0:T(8,128)(4,1)S(1)}, pred[8,17]{1,0:T(8,128)(4,1)}, u32[]{:S(2)}) copy-start(pred[8,17]{1,0:T(8,128)(4,1)} %constant.77) | copy-start | bytes 412
  74.0 13.4 %copy-start.3 = (bf16[1,2,16,128]{3,2,1,0:T(8,128)(2,1)S(1)}, bf16[1,2,16,128]{3,2,1,0:T(8,128)(2,1)}, u32[]{:S(2)}) copy-start(bf16[1,2,16,128]{3,2,1,0:T(8,128)(2,1)} %param.9) | copy-start | bytes 24580
  101.1 13.1 %copy-start.8 = (bf16[2,96,3,3]{1,0,3,2:T(2,128)(2,1)S(1)}, bf16[2,96,3,3]{1,0,3,2:T(2,128)(2,1)}, u32[]{:S(2)}) copy-start(bf16[2,96,3,3]{1,0,3,2:T(2,128)(2,1)} %param.16) | copy-start | bytes 10372
  101.1 13.1 %copy-start.10 = (pred[8,17]{0,1:T(8,128)(4,1)S(1)}, pred[8,17]{0,1:T(8,128)(4,1)}, u32[]{:S(2)}) copy-start(pred[8,17]{0,1:T(8,128)(4,1)} %constant.97) | copy-start | bytes 412
  102.7 4.6 %collective-permute-start.10 = (bf16[2,1,128]{2,1,0:T(2,128)(2,1)S(1)}, bf16[2,1,128]{2,1,0:T(2,128)(2,1)S(1)}, u32[]{:S(2)}, u32[]{:S(2)}) collective-permute-start(bf16[2,1,128]{2,1,0:T(2,128)(2,1)S(1)} %get-tuple-element.27), channel_id=1, source_target_pairs={{0,1},{1,2},{2,3},{3,0},{4,5},{5,6},{6,7},{7,4},{8,9},{9,10},{10,1... | collective-permute-start | bytes 1544 | tf_op jit(solution)/shard_map/ppermute | solution.py:23
  104.6 8.8 %collective-permute-start.11 = (bf16[2,1,128]{2,1,0:T(2,128)(2,1)S(1)}, bf16[2,1,128]{2,1,0:T(2,128)(2,1)S(1)}, u32[]{:S(2)}, u32[]{:S(2)}) collective-permute-start(bf16[2,1,128]{2,1,0:T(2,128)(2,1)S(1)} %get-tuple-element.26), channel_id=1, source_target_pairs={{1,0},{2,1},{3,2},{0,3},{5,4},{6,5},{7,6},{4,7},{9,8},{10,9},{11,1... | collective-permute-start | bytes 1544 | tf_op jit(solution)/shard_map/ppermute | solution.py:26
  115.8 4.3 %collective-permute-start.12 = (bf16[96,1,128]{0,1,2:T(2,128)(2,1)S(1)}, bf16[96,1,128]{0,1,2:T(2,128)(2,1)S(1)}, u32[]{:S(2)}, u32[]{:S(2)}) collective-permute-start(bf16[96,1,128]{0,1,2:T(2,128)(2,1)S(1)} %get-tuple-element.12), channel_id=1, source_target_pairs={{0,1},{1,2},{2,3},{3,0},{4,5},{5,6},{6,7},{7,4},{8,9},{9,10},{10,1... | collective-permute-start | bytes 73736 | tf_op jit(solution)/shard_map/ppermute | solution.py:23
  117.8 10.2 %collective-permute-start.13 = (bf16[96,1,128]{0,1,2:T(2,128)(2,1)S(1)}, bf16[96,1,128]{0,1,2:T(2,128)(2,1)S(1)}, u32[]{:S(2)}, u32[]{:S(2)}) collective-permute-start(bf16[96,1,128]{0,1,2:T(2,128)(2,1)S(1)} %get-tuple-element.13), channel_id=1, source_target_pairs={{1,0},{2,1},{3,2},{0,3},{5,4},{6,5},{7,6},{4,7},{9,8},{10,9},{11,1... | collective-permute-start | bytes 73736 | tf_op jit(solution)/shard_map/ppermute | solution.py:26
  130.8 4.3 %collective-permute-start.14 = (bf16[96,1,128]{0,1,2:T(2,128)(2,1)S(1)}, bf16[96,1,128]{0,1,2:T(2,128)(2,1)S(1)}, u32[]{:S(2)}, u32[]{:S(2)}) collective-permute-start(bf16[96,1,128]{0,1,2:T(2,128)(2,1)S(1)} %get-tuple-element.10), channel_id=1, source_target_pairs={{0,1},{1,2},{2,3},{3,0},{4,5},{5,6},{6,7},{7,4},{8,9},{9,10},{10,1... | collective-permute-start | bytes 73736 | tf_op jit(solution)/shard_map/ppermute | solution.py:23
  132.7 10.2 %collective-permute-start.15 = (bf16[96,1,128]{0,1,2:T(2,128)(2,1)S(1)}, bf16[96,1,128]{0,1,2:T(2,128)(2,1)S(1)}, u32[]{:S(2)}, u32[]{:S(2)}) collective-permute-start(bf16[96,1,128]{0,1,2:T(2,128)(2,1)S(1)} %get-tuple-element.11), channel_id=1, source_target_pairs={{1,0},{2,1},{3,2},{0,3},{5,4},{6,5},{7,6},{4,7},{9,8},{10,9},{11,1... | collective-permute-start | bytes 73736 | tf_op jit(solution)/shard_map/ppermute | solution.py:26
  151.3 19.4 %collective-permute-start.19 = (f32[2,16,128]{2,1,0:T(8,128)S(1)}, f32[2,16,128]{2,1,0:T(8,128)}, u32[]{:S(2)}, u32[]{:S(2)}) collective-permute-start(f32[2,16,128]{2,1,0:T(8,128)S(1)} %slice_bitcast_fusion.4), channel_id=1, source_target_pairs={{0,8},{4,12},{8,16},{12,20},{16,24},{20,28},{24,32},{28,36},{32,40... | collective-permute-start | bytes 49160 | tf_op jit(solution)/shard_map/ppermute | solution.py:14
  159.4 11.3 %collective-permute-start.18 = (f32[2,16,128]{2,1,0:T(8,128)}, f32[2,16,128]{2,1,0:T(8,128)}, u32[]{:S(2)}, u32[]{:S(2)}) collective-permute-start(f32[2,16,128]{2,1,0:T(8,128)} %slice_bitcast_fusion.5), channel_id=1, source_target_pairs={{0,4},{4,8},{8,12},{12,16},{16,20},{20,24},{24,28},{28,32},{32,36}... | collective-permute-start | bytes 49160 | tf_op jit(solution)/shard_map/ppermute | solution.py:14
  162.2 7.3 %copy-start.1 = (f32[16,8,17,2]{2,1,3,0:T(8,128)S(1)}, f32[16,8,17,2]{2,1,3,0:T(8,128)}, u32[]{:S(2)}) copy-start(f32[16,8,17,2]{2,1,3,0:T(8,128)} %get-tuple-element.18) | copy-start | bytes 52228
  162.4 9.6 %collective-permute-start.17 = (f32[2,16,128]{2,1,0:T(8,128)S(1)}, f32[2,16,128]{2,1,0:T(8,128)S(1)}, u32[]{:S(2)}, u32[]{:S(2)}) collective-permute-start(f32[2,16,128]{2,1,0:T(8,128)S(1)} %slice_bitcast_fusion.6), channel_id=1, source_target_pairs={{8,0},{12,4},{16,8},{20,12},{24,16},{28,20},{32,24},{36,28},{40,32... | collective-permute-start | bytes 49160 | tf_op jit(solution)/shard_map/ppermute | solution.py:14
  167.6 8.7 %collective-permute-start.16 = (f32[2,16,128]{2,1,0:T(8,128)S(1)}, f32[2,16,128]{2,1,0:T(8,128)S(1)}, u32[]{:S(2)}, u32[]{:S(2)}) collective-permute-start(f32[2,16,128]{2,1,0:T(8,128)S(1)} %slice_bitcast_fusion.7), channel_id=1, source_target_pairs={{4,0},{8,4},{12,8},{16,12},{20,16},{24,20},{28,24},{32,28},{36,32}... | collective-permute-start | bytes 49160 | tf_op jit(solution)/shard_map/ppermute | solution.py:14
where the time goes:
time: 179 us; the launch traced here: 178 us
  starting transfers between devices  64.3 us (36%)
  waiting for transfers between devices  46.3 us (26%)
  other arithmetic  23.8 us (13%)
  local copies, waits for them, and re-layouts  23.1 us (13%)
  matrix products  18.6 us (10%)
    ppermute x6, waiting for transfers between devices, extended(): lax.ppermute(lax.slice_in_dim(block, 0, width, axis=dim), axis, backward)  40.7 us
    ppermute x8, starting transfers between devices, from_behind(): lax.ppermute(value, axis, [(source, source + steps) for source in range(l...  27.6 us
    ppermute x6, starting transfers between devices, extended(): lax.ppermute(lax.slice_in_dim(block, block.shape[dim] - width, None, axis...  22.4 us
    conv_general_dilated x6, matrix products, conv_rows(): lax.conv_general_dilated(padded[None], weight, (1, 1), 'VALID', dimension...  18.6 us
    unnamed x4, other arithmetic  15.3 us
    conv_general_dilated x30, local copies, waits for them, and re-layouts, conv_rows(): lax.conv_general_dilated(padded[None], weight, (1, 1), 'VALID', dimension...  14.8 us
    ppermute x6, starting transfers between devices, extended(): lax.ppermute(lax.slice_in_dim(block, 0, width, axis=dim), axis, backward)  14.3 us
    ppermute x8, waiting for transfers between devices, from_behind(): lax.ppermute(value, axis, [(source, source + steps) for source in range(l...  5.58 us
  transfers between devices with their start and end apart: 20, of which 8 were waited for; matrix products, arithmetic and copies ran while one was open for 8% of the time, Pallas kernels for 0%

commit v1 on v0

v1 whole, which is shorter than its diff:
```python
import math

import jax
import jax.numpy as jnp
from jax import lax
from jax.experimental import pallas as pl
from jax.experimental.pallas import tpu as pltpu
from jax.sharding import PartitionSpec as P

NSTEPS = 256
HID = 96
WIDTH = 128
OWN = 16
REACH = 2
WINDOWS = 2 * REACH + 1
SPAN = 24
BLOCK = 6 * OWN
PULL = 4 * SPAN
ONE = BLOCK + PULL
THREE = 3 * BLOCK + PULL
F32 = jnp.float32
BF16 = jnp.bfloat16


def noise_level(step_index):
    phase_time = (step_index[0].astype(F32) + 0.5) / NSTEPS
    noise_alpha = jnp.cos(0.5 * math.pi * phase_time)
    noise_sigma = jnp.sin(0.5 * math.pi * phase_time)
    obs_kappa = 1.0 + (noise_sigma / noise_alpha) ** 2
    return noise_alpha, noise_sigma, obs_kappa


def station_kernel(first_ref, rows_ref, cols_ref, obs_ref, pull_ref, count_ref):
    stations = rows_ref.shape[1]
    offset = rows_ref[...] - first_ref[0]
    offset = jnp.where(offset < 0, offset + 64, offset)
    offset = jnp.where(offset >= 64, offset - 64, offset)
    place = lax.broadcasted_iota(jnp.int32, (SPAN, stations), 0)
    hit = place == jnp.broadcast_to(offset, (SPAN, stations))
    parts = []
    for f in range(2):
        values = obs_ref[f : f + 1, :]
        left = values
        for _ in range(3):
            part = left.astype(BF16).astype(F32)
            left = left - part
            parts.append(jnp.where(hit, jnp.broadcast_to(part, hit.shape), 0.0))
    parts.append(jnp.where(hit, 1.0, 0.0))
    left_side = jnp.concatenate(parts, axis=0).astype(BF16)
    column = lax.broadcasted_iota(jnp.int32, (WIDTH, stations), 0)
    at_column = jnp.where(
        column == jnp.broadcast_to(cols_ref[...], (WIDTH, stations)), 1.0, 0.0
    ).astype(BF16)
    sums = lax.dot_general(
        left_side, at_column, (((1,), (1,)), ((), ())), preferred_element_type=F32
    )
    total = jnp.concatenate(
        [
            sums[3 * SPAN * f : 3 * SPAN * f + SPAN]
            + sums[3 * SPAN * f + SPAN : 3 * SPAN * f + 2 * SPAN]
            + sums[3 * SPAN * f + 2 * SPAN : 3 * SPAN * f + 3 * SPAN]
            for f in range(2)
        ],
        axis=0,
    )
    high = total.astype(BF16)
    pull_ref[: 2 * SPAN, :] = high
    pull_ref[2 * SPAN :, :] = (total - high.astype(F32)).astype(BF16)
    count_ref[...] = sums[6 * SPAN : 7 * SPAN]


def logistic(values):
    return 0.5 + 0.5 * jnp.tanh(0.5 * values)


def rolled(values, shift):
    if shift == 0:
        return values
    return jnp.concatenate(
        [
            pltpu.roll(values[:, k : k + WIDTH], (-shift) % WIDTH, 1)
            for k in range(0, values.shape[1], WIDTH)
        ],
        axis=1,
    )


def store_shifted(ref, start, values):
    for b in range(3):
        moved = rolled(values, b - 1).astype(BF16)
        for k in range(2):
            ref[pl.ds(pl.multiple_of(start + (3 * k + b) * HID, 16), HID), :] = moved[
                :, k * WIDTH : (k + 1) * WIDTH
            ]


def two_rows(ref, start, slab, depth):
    return jnp.concatenate(
        [
            ref[pl.ds(pl.multiple_of(start + k * slab, 8), depth), :].astype(BF16)
            for k in range(2)
        ],
        axis=1,
    )


def dot(left, right):
    return lax.dot_general(
        left, right, (((1,), (0,)), ((), ())), preferred_element_type=F32
    )


def folded(product):
    return rolled(product[0:8], -1) + product[8:16] + rolled(product[16:24], 1)


def score_kernel(
    scalars_ref,
    own_ref,
    before_ref,
    after_ref,
    far_before_ref,
    far_after_ref,
    count_ref,
    bias_ref,
    w_in_ref,
    w_mid_ref,
    w_out_ref,
    w_out_adj_ref,
    w_back_ref,
    w_in_adj_ref,
    out_ref,
    moved,
    sums,
    blanket,
    hidden,
    slope_one,
    slope_two,
    folds,
    pull_slabs,
    back,
    grads,
    kept,
):
    noise_alpha = scalars_ref[0]
    noise_sigma = scalars_ref[1]
    obs_kappa = scalars_ref[2]
    over_alpha = 1.0 / noise_alpha
    over_kappa = 1.0 / obs_kappa

    blanket[...] = jnp.zeros_like(blanket)
    folds[...] = jnp.zeros_like(folds)
    pull_slabs[...] = jnp.zeros_like(pull_slabs)
    grads[...] = jnp.zeros_like(grads)

    places = (
        (far_before_ref, 0),
        (far_before_ref, BLOCK),
        (far_before_ref, 2 * BLOCK),
        (before_ref, 0),
        (own_ref, 0),
        (after_ref, 0),
        (far_after_ref, 0),
        (far_after_ref, BLOCK),
        (far_after_ref, 2 * BLOCK),
    )
    for s, (ref, start) in enumerate(places):
        inside = scalars_ref[3 + s]
        for f in range(2):
            rows = [
                ref[pl.ds(start + OWN * (2 * block + f), OWN), :].astype(F32)
                for block in range(3)
            ]
            field = inside * jnp.concatenate(
                [rows[0][8:], rows[1], rows[2][:8]], axis=0
            )
            for b in range(3):
                moved[b, 2 * s + f, :, :] = rolled(field, b - 1)

    for w, (ref, start) in enumerate(
        (
            (far_before_ref, 3 * BLOCK),
            (before_ref, BLOCK),
            (own_ref, BLOCK),
            (after_ref, BLOCK),
            (far_after_ref, 3 * BLOCK),
        )
    ):
        sums[w, :, :] = ref[pl.ds(start, 2 * SPAN), :].astype(F32) + ref[
            pl.ds(start + 2 * SPAN, 2 * SPAN), :
        ].astype(F32)

    def window(w, _):
        inside = scalars_ref[3 + REACH + w]
        for b in range(3):
            for channel in range(2 * WINDOWS):
                blanket[pl.ds(16 * b + channel, 32, stride=48), :] = moved[
                    b, 2 * w + channel, :, :
                ]

        def first_layer(p, _):
            bias = bias_ref[...]
            values = dot(w_in_ref[...], two_rows(blanket, 48 * (2 * p + 2), 48, 144))
            values = values + jnp.concatenate([bias, bias], axis=1)
            gate = logistic(values)
            result = values * gate
            slope = gate + result * (1.0 - gate)
            store_shifted(hidden, 6 * HID * p, result)
            for k in range(2):
                slope_one[pl.ds(pl.multiple_of(HID * (2 * p + k), 8), HID), :] = slope[
                    :, k * WIDTH : (k + 1) * WIDTH
                ]
            return 0

        lax.fori_loop(0, 13, first_layer, 0)

        def second_layer(q, _):
            values = dot(w_mid_ref[...], two_rows(hidden, 6 * HID * q, 3 * HID, 9 * HID))
            gate = logistic(values)
            result = values * gate
            slope = gate + result * (1.0 - gate)
            residual = jnp.concatenate(
                [
                    hidden[pl.ds(pl.multiple_of(3 * HID * (2 * q + 1 + k) + HID, 16), HID), :]
                    for k in range(2)
                ],
                axis=1,
            )
            high = (residual.astype(F32) + result).astype(BF16)
            fold = folded(dot(w_out_ref[...], high))
            for k in range(2):
                slope_two[pl.ds(pl.multiple_of(HID * (2 * q + k), 8), HID), :] = slope[
                    :, k * WIDTH : (k + 1) * WIDTH
                ]
                folds[pl.ds(pl.multiple_of(8 * (2 * q + k), 8), 8), :] = fold[
                    :, k * WIDTH : (k + 1) * WIDTH
                ]
            return 0

        lax.fori_loop(0, 12, second_layer, 0)

        for f in range(2):
            noise_pred = (
                folds[pl.ds(f, SPAN, stride=8), :]
                + folds[pl.ds(8 + 2 + f, SPAN, stride=8), :]
                + folds[pl.ds(16 + 4 + f, SPAN, stride=8), :]
            )
            state = moved[1, 2 * w + 2 * REACH + f, pl.ds(5, SPAN), :]
            denoised = (state - noise_sigma * noise_pred) * over_alpha
            pull = (
                sums[w, pl.ds(SPAN * f, SPAN), :] - count_ref[...] * denoised
            ) * over_kappa
            for b in range(3):
                pull_slabs[pl.ds(2 * b + f, SPAN, stride=16), :] = rolled(pull, b - 1)

            @pl.when(w == REACH)
            def _():
                kept[f, :, :] = noise_pred
                kept[2 + f, :, :] = pull

        def second_back(t, _):
            gradient = dot(w_out_adj_ref[...], two_rows(pull_slabs, 32 * t, 16, 48))
            slope = jnp.concatenate(
                [
                    slope_two[pl.ds(pl.multiple_of(HID * (2 * t + 2 + k), 8), HID), :]
                    for k in range(2)
                ],
                axis=1,
            )
            store_shifted(back, 6 * HID * t, gradient * slope)
            return 0

        lax.fori_loop(0, 10, second_back, 0)

        def first_back(u, _):
            operand = jnp.concatenate(
                [
                    two_rows(back, 6 * HID * u, 3 * HID, 9 * HID),
                    two_rows(pull_slabs, 16 * (2 * u + 1), 16, 48),
                ],
                axis=0,
            )
            gradient = dot(w_back_ref[...], operand)
            slope = jnp.concatenate(
                [
                    slope_one[pl.ds(pl.multiple_of(HID * (2 * u + 4 + k), 8), HID), :]
                    for k in range(2)
                ],
                axis=1,
            )
            fold = inside * folded(dot(w_in_adj_ref[w], (gradient * slope).astype(BF16)))
            for k in range(2):
                at = pl.ds(pl.multiple_of(8 * (2 * u + k), 8), 8)
                grads[at, :] = grads[at, :] + fold[:, k * WIDTH : (k + 1) * WIDTH]
            return 0

        lax.fori_loop(0, 9, first_back, 0)
        return 0

    lax.fori_loop(0, WINDOWS, window, 0)

    for f in range(2):
        summed = (
            grads[pl.ds(f, OWN, stride=8), :]
            + grads[pl.ds(8 + 2 + f, OWN, stride=8), :]
            + grads[pl.ds(16 + 4 + f, OWN, stride=8), :]
        )
        noise_pred = kept[f, pl.ds(3, OWN), :]
        pull = kept[2 + f, pl.ds(3, OWN), :]
        out_ref[f, :, :] = -noise_pred / noise_sigma + (
            pull - noise_sigma * summed
        ) * over_alpha


def padded(array, axis, size):
    pads = [(0, 0)] * array.ndim
    pads[axis] = (0, size - array.shape[axis])
    return jnp.pad(array, pads)


def matrices(w_in, w_mid, w_out):
    taps = w_mid.reshape(9, HID, HID)
    mid = jnp.transpose(taps, (1, 0, 2)).reshape(HID, 9 * HID)
    mid_adj = jnp.transpose(taps[::-1], (2, 0, 1)).reshape(HID, 9 * HID)
    first = padded(jnp.transpose(w_in, (0, 2, 3, 1)), 3, 16).reshape(HID, 144)
    last = padded(
        jnp.transpose(w_out, (3, 2, 0, 1)).reshape(3, 6, HID), 1, 8
    ).reshape(24, HID)
    flipped_out = w_out[:, :, ::-1, ::-1]
    last_adj = padded(
        jnp.transpose(flipped_out, (1, 2, 3, 0)).reshape(HID, 3, 6), 2, 16
    ).reshape(HID, 48)
    flipped_in = w_in[:, :, ::-1, ::-1].reshape(HID, WINDOWS, 2, 3, 3)[:, ::-1]
    first_adj = padded(
        jnp.transpose(flipped_in, (1, 4, 3, 2, 0)).reshape(WINDOWS, 3, 6, HID), 2, 8
    ).reshape(WINDOWS, 24, HID)
    return first, mid, last, last_adj, jnp.concatenate([mid_adj, last_adj], axis=1), first_adj


def on_device(
    trajectory, observed, station_rows, station_cols, step_index, w_in, w_mid, w_out, noise_gain
):
    place = lax.axis_index("tm")
    part = lax.axis_index("rows")
    count = lax.axis_size("tm")
    noise_alpha, noise_sigma, obs_kappa = noise_level(step_index)
    own_state = trajectory[0]

    far = lax.ppermute(own_state, "rows", [(1, 2), (2, 1), (3, 0), (0, 3)])
    near = lax.ppermute(own_state, "rows", [(0, 1), (1, 0), (2, 3), (3, 2)])

    vmem = pl.BlockSpec(memory_space=pltpu.VMEM)
    smem = pl.BlockSpec(memory_space=pltpu.SMEM)
    pulls, counts = pl.pallas_call(
        station_kernel,
        out_shape=(
            jax.ShapeDtypeStruct((PULL, WIDTH), BF16),
            jax.ShapeDtypeStruct((SPAN, WIDTH), F32),
        ),
        in_specs=[smem, vmem, vmem, vmem],
        out_specs=(vmem, vmem),
        cost_estimate=pl.CostEstimate(flops=40_000_000, bytes_accessed=50_000, transcendentals=0),
        name="stations",
    )(
        (part * OWN - 3).reshape(1).astype(jnp.int32),
        station_rows.reshape(1, -1),
        station_cols.reshape(1, -1),
        observed[0],
    )
    weights = matrices(w_in, w_mid, w_out)
    bias = jnp.broadcast_to((noise_sigma * noise_gain)[:, None], (HID, WIDTH))
    states = place + jnp.arange(-2 * REACH, 2 * REACH + 1)
    inside = ((states >= 0) & (states < count)).astype(F32)
    scalars = jnp.concatenate(
        [jnp.stack([noise_alpha, noise_sigma, obs_kappa]), inside, jnp.zeros(4, F32)]
    )

    even = part % 2 == 0
    above = jnp.where(even, far, near)
    below = jnp.where(even, near, far)
    own = jnp.concatenate([above, own_state, below], axis=0).reshape(BLOCK, WIDTH)
    own = jnp.concatenate([own, pulls], axis=0)

    def ring(value, steps):
        return lax.ppermute(value, "tm", [(k, (k + steps) % count) for k in range(count)])

    before = ring(own, 1)
    after = ring(own, -1)
    three = jnp.concatenate([before[:BLOCK], own[:BLOCK], after[:BLOCK]], axis=0)
    far_before = ring(jnp.concatenate([three, after[BLOCK:]], axis=0), 3)
    far_after = ring(jnp.concatenate([three, before[BLOCK:]], axis=0), -3)

    posterior = pl.pallas_call(
        score_kernel,
        out_shape=jax.ShapeDtypeStruct((2, OWN, WIDTH), F32),
        in_specs=[smem] + [vmem] * 13,
        out_specs=vmem,
        scratch_shapes=[
            pltpu.VMEM((3, 18, 32, WIDTH), F32),
            pltpu.VMEM((WINDOWS, 2 * SPAN, WIDTH), F32),
            pltpu.VMEM((32 * 48, WIDTH), F32),
            pltpu.VMEM((26 * 3 * HID, WIDTH), BF16),
            pltpu.VMEM((26 * HID, WIDTH), F32),
            pltpu.VMEM((24 * HID, WIDTH), F32),
            pltpu.VMEM((32 * 8, WIDTH), F32),
            pltpu.VMEM((SPAN * 16, WIDTH), F32),
            pltpu.VMEM((20 * 3 * HID, WIDTH), BF16),
            pltpu.VMEM((18 * 8, WIDTH), F32),
            pltpu.VMEM((4, SPAN, WIDTH), F32),
        ],
        compiler_params=pltpu.CompilerParams(vmem_limit_bytes=32 * 1024 * 1024),
        cost_estimate=pl.CostEstimate(
            flops=5_000_000_000, bytes_accessed=1_000_000, transcendentals=1_000_000
        ),
        name="score",
    )(
        scalars,
        own,
        before,
        after,
        far_before,
        far_after,
        counts,
        bias,
        *weights,
    )
    return posterior[None]


def solution(mesh):
    return jax.shard_map(
        on_device,
        mesh=mesh,
        in_specs=(
            P("tm", None, "rows", None),
            P("tm", None, None),
            P(),
            P(),
            P(),
            P(),
            P(),
            P(),
            P(),
        ),
        out_specs=P("tm", None, "rows", None),
        check_vma=False,
    )
```

time: 179 us -> 129 us (0.72)
  the two profiles are of different devices: /device:TPU:63 before, /device:TPU:1 now
where the time goes in v1:
time: 129 us; the launch traced here: 128 us
  Pallas kernels  78.5 us (61%)
  starting transfers between devices  39 us (30%)
  local copies, waits for them, and re-layouts  6.12 us (5%)
  waiting for transfers between devices  3.72 us (3%)
    pallas_call x1, Pallas kernels, on_device(): pl.pallas_call(score_kernel, out_shape=jax.ShapeDtypeStruct((2, OWN, WIDT...  76.8 us
    ppermute x4, starting transfers between devices, ring(): lax.ppermute(value, 'tm', [(k, (k + steps) % count) for k in range(count)])  25 us
    ppermute x1, starting transfers between devices, on_device(): far = lax.ppermute(own_state, 'rows', [(1, 2), (2, 1), (3, 0), (0, 3)])  12 us
    unnamed x13, local copies, waits for them, and re-layouts  3.86 us
    ppermute x4, waiting for transfers between devices, ring(): lax.ppermute(value, 'tm', [(k, (k + steps) % count) for k in range(count)])  3.71 us
  transfers between devices with their start and end apart: 6, of which 3 were waited for; matrix products, arithmetic and copies ran while one was open for 2% of the time, Pallas kernels for 1%

profile of v1, /device:TPU:1, one launch (start us, length us, event | category | flops | bytes accessed | tf_op | source)
XLA Modules:
  0.0 128.5 jit_solution(13816249681759840320)
XLA Ops:
  0.0 12.0 %collective-permute-start = (bf16[2,16,128]{2,1,0:T(8,128)(2,1)}, bf16[2,16,128]{2,1,0:T(8,128)(2,1)S(1)}, u32[]{:S(2)}, u32[]{:S(2)}) collective-permute-start(bf16[2,16,128]{2,1,0:T(8,128)(2,1)} %bitcast.42), channel_id=1, source_target_pairs={{1,2},{2,1},{3,0},{0,3},{5,6},{6,5},{7,4},{4,7},{9,10},{10,9},{11,... | collective-permute-start | bytes 24584 | tf_op jit(solution)/shard_map/ppermute | solution.py:349
  12.0 1.9 %collective-permute-start.1 = (bf16[2,16,128]{2,1,0:T(8,128)(2,1)}, bf16[2,16,128]{2,1,0:T(8,128)(2,1)S(1)}, u32[]{:S(2)}, u32[]{:S(2)}) collective-permute-start(bf16[2,16,128]{2,1,0:T(8,128)(2,1)} %bitcast.43), channel_id=1, source_target_pairs={{0,1},{1,0},{2,3},{3,2},{4,5},{5,4},{6,7},{7,6},{8,9},{9,8},{10,11... | collective-permute-start | bytes 24584 | tf_op jit(solution)/shard_map/ppermute | solution.py:350
  14.7 1.1 reshape.60
  15.9 0.0 copy-start.3
  15.9 0.2 copy.18
  16.0 0.5 copy-done.3
  16.6 0.1 copy.23.w_out_adj_ref
  16.7 0.6 copy-done.1
  17.3 0.1 rev.14
  17.5 0.0 copy-start.5
  17.5 0.6 copy-done.5
  18.2 0.1 pad_maximum_fusion.w_back_ref
  18.3 1.6 %stations.1 = (bf16[96,128]{1,0:T(8,128)(2,1)}, f32[24,128]{1,0:T(8,128)}) custom-call(s32[1]{0:T(128)} %bitcast.5.first_ref, s32[1,1024]{1,0:T(1,128)} %bitcast.46, s32[1,1024]{1,0:T(1,128)} %bitcast.47, f32[2,1024]{1,0:T(2,128)} %bitcast.45), custom_call_target="tpu_custom_call" | custom-call | flops 40000000 | bytes 50000 | tf_op jit(solution)/shard_map/stations/pallas_call | solution.py:354
  19.9 0.0 collective-permute-done
  19.9 0.0 collective-permute-done.1
  19.9 0.7 copy-done.4
  20.6 0.7 copy-done.2
  21.4 3.2 %collective-permute-start.2 = (bf16[192,128]{1,0:T(8,128)(2,1)S(1)}, bf16[192,128]{1,0:T(8,128)(2,1)S(1)}, u32[]{:S(2)}, u32[]{:S(2)}) collective-permute-start(bf16[192,128]{1,0:T(8,128)(2,1)S(1)} %pad_maximum_fusion.4.own_ref), channel_id=1, source_target_pairs={{0,4},{4,8},{8,12},{12,16},{16,20},{20,24},{24,28},{28,32},{32,36}... | collective-permute-start | bytes 147464 | tf_op jit(solution)/shard_map/ppermute | solution.py:385
  24.7 0.2 copy.16
  24.9 0.2 copy.22.w_mid_ref
  25.1 0.1 copy.21.w_in_ref
  25.2 0.1 concatenate.22.scalars_ref
  25.3 8.7 %collective-permute-start.3 = (bf16[192,128]{1,0:T(8,128)(2,1)S(1)}, bf16[192,128]{1,0:T(8,128)(2,1)S(1)}, u32[]{:S(2)}, u32[]{:S(2)}) collective-permute-start(bf16[192,128]{1,0:T(8,128)(2,1)S(1)} %pad_maximum_fusion.4.own_ref), channel_id=1, source_target_pairs={{0,508},{4,0},{8,4},{12,8},{16,12},{20,16},{24,20},{28,24},{32,28}... | collective-permute-start | bytes 147464 | tf_op jit(solution)/shard_map/ppermute | solution.py:385
  34.0 0.0 collective-permute-done.2.before_ref
  34.1 1.1 collective-permute-done.3.after_ref
  35.2 2.6 %collective-permute-start.4 = (bf16[384,128]{1,0:T(8,128)(2,1)S(1)}, bf16[384,128]{1,0:T(8,128)(2,1)S(1)}, u32[]{:S(2)}, u32[]{:S(2)}) collective-permute-start(bf16[384,128]{1,0:T(8,128)(2,1)S(1)} %get-tuple-element.10), channel_id=1, source_target_pairs={{0,12},{4,16},{8,20},{12,24},{16,28},{20,32},{24,36},{28,40},{32,4... | collective-permute-start | bytes 294920 | tf_op jit(solution)/shard_map/ppermute | solution.py:385
  37.8 10.5 %collective-permute-start.5 = (bf16[384,128]{1,0:T(8,128)(2,1)S(1)}, bf16[384,128]{1,0:T(8,128)(2,1)S(1)}, u32[]{:S(2)}, u32[]{:S(2)}) collective-permute-start(bf16[384,128]{1,0:T(8,128)(2,1)S(1)} %get-tuple-element.9), channel_id=1, source_target_pairs={{0,500},{4,504},{8,508},{12,0},{16,4},{20,8},{24,12},{28,16},{32,2... | collective-permute-start | bytes 294920 | tf_op jit(solution)/shard_map/ppermute | solution.py:385
  48.4 0.1 collective-permute-done.4.far_before_ref
  48.5 2.5 %collective-permute-done.5.far_after_ref = bf16[384,128]{1,0:T(8,128)(2,1)S(1)} collective-permute-done((bf16[384,128]{1,0:T(8,128)(2,1)S(1)}, bf16[384,128]{1,0:T(8,128)(2,1)S(1)}, u32[]{:S(2)}, u32[]{:S(2)}) %collective-permute-start.5) | collective-permute-done | bytes 98336 | tf_op jit(solution)/shard_map/ppermute | solution.py:385
  50.9 0.1 broadcast_in_dim.4.bias_ref
  51.0 0.6 copy-done
  51.6 76.8 %score.1 = f32[2,16,128]{2,1,0:T(8,128)} custom-call(f32[16]{0:T(128)S(1)} %concatenate.22.scalars_ref, bf16[192,128]{1,0:T(8,128)(2,1)S(1)} %pad_maximum_fusion.4.own_ref, bf16[192,128]{1,0:T(8,128)(2,1)S(1)} %collective-permute-done.2.before_ref, bf16[192,128]{1,0:T(8,128)(2,1)S(1)} %collective-permute-done.3.after_ref, ...), custom_call_target="tpu_custom_call" | custom-call | flops 5000000000 | bytes 1000000 | tf_op jit(solution)/shard_map/score/pallas_call | solution.py:393
  (26 shorter events, 0.3 us)
Async XLA Ops:
  0.0 19.9 %collective-permute-start = (bf16[2,16,128]{2,1,0:T(8,128)(2,1)}, bf16[2,16,128]{2,1,0:T(8,128)(2,1)S(1)}, u32[]{:S(2)}, u32[]{:S(2)}) collective-permute-start(bf16[2,16,128]{2,1,0:T(8,128)(2,1)} %bitcast.42), channel_id=1, source_target_pairs={{1,2},{2,1},{3,0},{0,3},{5,6},{6,5},{7,4},{4,7},{9,10},{10,9},{11,... | collective-permute-start | bytes 24584 | tf_op jit(solution)/shard_map/ppermute | solution.py:349
  12.0 7.9 %collective-permute-start.1 = (bf16[2,16,128]{2,1,0:T(8,128)(2,1)}, bf16[2,16,128]{2,1,0:T(8,128)(2,1)S(1)}, u32[]{:S(2)}, u32[]{:S(2)}) collective-permute-start(bf16[2,16,128]{2,1,0:T(8,128)(2,1)} %bitcast.43), channel_id=1, source_target_pairs={{0,1},{1,0},{2,3},{3,2},{4,5},{5,4},{6,7},{7,6},{8,9},{9,8},{10,11... | collective-permute-start | bytes 24584 | tf_op jit(solution)/shard_map/ppermute | solution.py:350
  15.9 0.7 copy-start.3
  16.6 0.8 copy-start.1
  17.5 0.7 copy-start.5
  19.9 0.7 copy-start.4
  20.6 0.7 copy-start.2
  21.4 12.7 %collective-permute-start.2 = (bf16[192,128]{1,0:T(8,128)(2,1)S(1)}, bf16[192,128]{1,0:T(8,128)(2,1)S(1)}, u32[]{:S(2)}, u32[]{:S(2)}) collective-permute-start(bf16[192,128]{1,0:T(8,128)(2,1)S(1)} %pad_maximum_fusion.4.own_ref), channel_id=1, source_target_pairs={{0,4},{4,8},{8,12},{12,16},{16,20},{20,24},{24,28},{28,32},{32,36}... | collective-permute-start | bytes 147464 | tf_op jit(solution)/shard_map/ppermute | solution.py:385
  25.3 9.9 %collective-permute-start.3 = (bf16[192,128]{1,0:T(8,128)(2,1)S(1)}, bf16[192,128]{1,0:T(8,128)(2,1)S(1)}, u32[]{:S(2)}, u32[]{:S(2)}) collective-permute-start(bf16[192,128]{1,0:T(8,128)(2,1)S(1)} %pad_maximum_fusion.4.own_ref), channel_id=1, source_target_pairs={{0,508},{4,0},{8,4},{12,8},{16,12},{20,16},{24,20},{28,24},{32,28}... | collective-permute-start | bytes 147464 | tf_op jit(solution)/shard_map/ppermute | solution.py:385
  35.2 13.3 %collective-permute-start.4 = (bf16[384,128]{1,0:T(8,128)(2,1)S(1)}, bf16[384,128]{1,0:T(8,128)(2,1)S(1)}, u32[]{:S(2)}, u32[]{:S(2)}) collective-permute-start(bf16[384,128]{1,0:T(8,128)(2,1)S(1)} %get-tuple-element.10), channel_id=1, source_target_pairs={{0,12},{4,16},{8,20},{12,24},{16,28},{20,32},{24,36},{28,40},{32,4... | collective-permute-start | bytes 294920 | tf_op jit(solution)/shard_map/ppermute | solution.py:385
  37.8 13.1 %collective-permute-start.5 = (bf16[384,128]{1,0:T(8,128)(2,1)S(1)}, bf16[384,128]{1,0:T(8,128)(2,1)S(1)}, u32[]{:S(2)}, u32[]{:S(2)}) collective-permute-start(bf16[384,128]{1,0:T(8,128)(2,1)S(1)} %get-tuple-element.9), channel_id=1, source_target_pairs={{0,500},{4,504},{8,508},{12,0},{16,4},{20,8},{24,12},{28,16},{32,2... | collective-permute-start | bytes 294920 | tf_op jit(solution)/shard_map/ppermute | solution.py:385
  50.9 0.7 copy-start

commit v2 on v1

v2 whole, which is shorter than its diff:
```python
import math

import jax
import jax.numpy as jnp
from jax import lax
from jax.experimental import pallas as pl
from jax.experimental.pallas import tpu as pltpu
from jax.sharding import PartitionSpec as P

NSTEPS = 256
HID = 96
WIDTH = 128
OWN = 16
REACH = 2
WINDOWS = 2 * REACH + 1
SPAN = 24
EDGE = 8
BLOCK = 2 * OWN + 4 * EDGE
STATIONS = 1024
SEEN = 4 * STATIONS // WIDTH
ONE = BLOCK + SEEN
THREE = 3 * BLOCK + SEEN
PLAN = ((2, 99), (24, 99), (2, 99), (18, 99))
F32 = jnp.float32
BF16 = jnp.bfloat16


def noise_level(step_index):
    phase_time = (step_index[0].astype(F32) + 0.5) / NSTEPS
    noise_alpha = jnp.cos(0.5 * math.pi * phase_time)
    noise_sigma = jnp.sin(0.5 * math.pi * phase_time)
    obs_kappa = 1.0 + (noise_sigma / noise_alpha) ** 2
    return noise_alpha, noise_sigma, obs_kappa


def station_sums(first, rows_ref, cols_ref, seen):
    left_side, at_column = [], []
    chunks = STATIONS // WIDTH
    for chunk in range(chunks):
        offset = rows_ref[chunk : chunk + 1, :] - first
        offset = jnp.where(offset < 0, offset + 64, offset)
        offset = jnp.where(offset >= 64, offset - 64, offset)
        place = lax.broadcasted_iota(jnp.int32, (SPAN, WIDTH), 0)
        hit = place == jnp.broadcast_to(offset, (SPAN, WIDTH))
        parts = [jnp.where(hit, 1.0, 0.0)]
        for values in seen:
            for part in range(4):
                row = values[chunks * part + chunk : chunks * part + chunk + 1, :]
                parts.append(jnp.where(hit, jnp.broadcast_to(row, (SPAN, WIDTH)), 0.0))
        left_side.append(jnp.concatenate(parts, axis=0).astype(BF16))
        column = lax.broadcasted_iota(jnp.int32, (WIDTH, WIDTH), 0)
        at = jnp.broadcast_to(cols_ref[chunk : chunk + 1, :], (WIDTH, WIDTH))
        at_column.append(jnp.where(column == at, 1.0, 0.0).astype(BF16))
    sums = lax.dot_general(
        jnp.concatenate(left_side, axis=1),
        jnp.concatenate(at_column, axis=1),
        (((1,), (1,)), ((), ())),
        preferred_element_type=F32,
    )
    results = []
    for k in range(len(seen)):
        start = SPAN * (4 * k + 1)
        results.append(
            sums[start : start + 2 * SPAN] + sums[start + 2 * SPAN : start + 4 * SPAN]
        )
    return results + [sums[:SPAN]]


def logistic(values):
    return 0.5 + 0.5 * jnp.tanh(0.5 * values)


def rolled(values, shift):
    if shift == 0:
        return values
    return jnp.concatenate(
        [
            pltpu.roll(values[:, k : k + WIDTH], (-shift) % WIDTH, 1)
            for k in range(0, values.shape[1], WIDTH)
        ],
        axis=1,
    )


def store_shifted(ref, start, values):
    low = values.astype(BF16)
    for b in range(3):
        moved = rolled(low, b - 1)
        for k in range(values.shape[1] // WIDTH):
            ref[pl.ds(pl.multiple_of(start + (3 * k + b) * HID, 16), HID), :] = moved[
                :, k * WIDTH : (k + 1) * WIDTH
            ]


def store_rows(ref, start, slab, values):
    for k in range(values.shape[1] // WIDTH):
        ref[pl.ds(pl.multiple_of(start + k * slab, 8), slab), :] = values[
            :, k * WIDTH : (k + 1) * WIDTH
        ]


def side_by_side(ref, start, slab, depth, rows):
    return jnp.concatenate(
        [
            ref[pl.ds(pl.multiple_of(start + k * slab, 8), depth), :].astype(BF16)
            for k in range(rows)
        ],
        axis=1,
    )


def wide(ref, start, slab, rows):
    return jnp.concatenate(
        [ref[pl.ds(pl.multiple_of(start + k * slab, 8), slab), :] for k in range(rows)], axis=1
    )


def over_rows(body, total, rows, unroll):
    steps = total // rows

    def step(k, carry):
        body(k * rows, rows)
        return carry

    if unroll >= steps:
        for k in range(steps):
            body(k * rows, rows)
    else:
        lax.fori_loop(0, steps, step, 0, unroll=unroll)
    if total % rows:
        body(steps * rows, total % rows)


def dot(left, right):
    return lax.dot_general(
        left, right, (((1,), (0,)), ((), ())), preferred_element_type=F32
    )


def folded(product):
    return rolled(product[0:8], -1) + product[8:16] + rolled(product[16:24], 1)


def score_kernel(
    scalars_ref,
    first_ref,
    rows_ref,
    cols_ref,
    seen_ref,
    near_after_ref,
    near_before_ref,
    far_before_ref,
    far_after_ref,
    bias_ref,
    w_in_ref,
    w_mid_ref,
    w_out_ref,
    w_out_adj_ref,
    w_back_ref,
    w_in_adj_ref,
    out_ref,
    moved,
    sums,
    count,
    blanket,
    hidden,
    slope_one,
    slope_two,
    folds,
    pull_slabs,
    back,
    grads,
    kept,
):
    noise_alpha = scalars_ref[0]
    noise_sigma = scalars_ref[1]
    obs_kappa = scalars_ref[2]
    over_alpha = 1.0 / noise_alpha
    over_kappa = 1.0 / obs_kappa

    blanket[...] = jnp.zeros_like(blanket)
    folds[...] = jnp.zeros_like(folds)
    pull_slabs[...] = jnp.zeros_like(pull_slabs)
    grads[...] = jnp.zeros_like(grads)

    places = (
        (far_before_ref, 0),
        (far_before_ref, BLOCK),
        (far_before_ref, 2 * BLOCK),
        (near_after_ref, 0),
        (near_after_ref, BLOCK),
        (near_after_ref, 2 * BLOCK),
        (far_after_ref, 0),
        (far_after_ref, BLOCK),
        (far_after_ref, 2 * BLOCK),
    )
    for s, (ref, start) in enumerate(places):
        inside = scalars_ref[3 + s]
        above = ref[pl.ds(start + 2 * OWN, 2 * EDGE), :].astype(F32)
        below = ref[pl.ds(start + 2 * OWN + 2 * EDGE, 2 * EDGE), :].astype(F32)
        for f in range(2):
            rows = ref[pl.ds(start + OWN * f, OWN), :].astype(F32)
            edge = slice(EDGE * f, EDGE * (f + 1))
            field = inside * jnp.concatenate([above[edge], rows, below[edge]], axis=0)
            for b in range(3):
                moved[b, 2 * s + f, :, :] = rolled(field, b - 1)

    seen = [
        ref[pl.ds(start, SEEN), :].astype(F32)
        for ref, start in (
            (far_before_ref, 3 * BLOCK),
            (near_before_ref, 3 * BLOCK),
            (seen_ref, 0),
            (near_after_ref, 3 * BLOCK),
            (far_after_ref, 3 * BLOCK),
        )
    ]
    *totals, stations = station_sums(first_ref[0], rows_ref, cols_ref, seen)
    for k in range(WINDOWS):
        sums[k, :, :] = totals[k]
    count[...] = stations

    def window(w, _):
        inside = scalars_ref[3 + REACH + w]
        for b in range(3):
            for channel in range(2 * WINDOWS):
                blanket[pl.ds(16 * b + channel, 32, stride=48), :] = moved[
                    b, 2 * w + channel, :, :
                ]

        def first_layer(p, rows):
            values = dot(w_in_ref[...], side_by_side(blanket, 48 * (p + 2), 48, 144, rows))
            values = values + jnp.concatenate([bias_ref[...]] * rows, axis=1)
            gate = logistic(values)
            result = values * gate
            store_shifted(hidden, 3 * HID * p, result)
            store_rows(slope_one, HID * p, HID, gate + result * (1.0 - gate))

        over_rows(first_layer, 26, *PLAN[0])

        def second_layer(q, rows):
            operand = side_by_side(hidden, 3 * HID * q, 3 * HID, 9 * HID, rows)
            values = dot(w_mid_ref[...], operand)
            gate = logistic(values)
            result = values * gate
            residual = side_by_side(hidden, 3 * HID * (q + 1) + HID, 3 * HID, HID, rows)
            high = (residual.astype(F32) + result).astype(BF16)
            store_rows(slope_two, HID * q, HID, gate + result * (1.0 - gate))
            store_rows(folds, 8 * q, 8, folded(dot(w_out_ref[...], high)))

        over_rows(second_layer, 24, *PLAN[1])

        for f in range(2):
            noise_pred = (
                folds[pl.ds(f, SPAN, stride=8), :]
                + folds[pl.ds(8 + 2 + f, SPAN, stride=8), :]
                + folds[pl.ds(16 + 4 + f, SPAN, stride=8), :]
            )
            state = moved[1, 2 * w + 2 * REACH + f, pl.ds(5, SPAN), :]
            denoised = (state - noise_sigma * noise_pred) * over_alpha
            pull = (
                sums[w, pl.ds(SPAN * f, SPAN), :] - count[...] * denoised
            ) * over_kappa
            for b in range(3):
                pull_slabs[pl.ds(2 * b + f, SPAN, stride=16), :] = rolled(pull, b - 1)

            @pl.when(w == REACH)
            def _():
                kept[f, :, :] = noise_pred
                kept[2 + f, :, :] = pull

        def second_back(t, rows):
            operand = side_by_side(pull_slabs, 16 * t, 16, 48, rows)
            slope = wide(slope_two, HID * (t + 2), HID, rows)
            store_shifted(back, 3 * HID * t, dot(w_out_adj_ref[...], operand) * slope)

        over_rows(second_back, 20, *PLAN[2])

        def first_back(u, rows):
            operand = jnp.concatenate(
                [
                    side_by_side(back, 3 * HID * u, 3 * HID, 9 * HID, rows),
                    side_by_side(pull_slabs, 16 * (u + 1), 16, 48, rows),
                ],
                axis=0,
            )
            slope = wide(slope_one, HID * (u + 4), HID, rows)
            low = (dot(w_back_ref[...], operand) * slope).astype(BF16)
            fold = inside * folded(dot(w_in_adj_ref[w], low))
            for k in range(rows):
                at = pl.ds(pl.multiple_of(8 * (u + k), 8), 8)
                grads[at, :] = grads[at, :] + fold[:, k * WIDTH : (k + 1) * WIDTH]

        over_rows(first_back, 18, *PLAN[3])
        return 0

    lax.fori_loop(0, WINDOWS, window, 0)

    for f in range(2):
        summed = (
            grads[pl.ds(f, OWN, stride=8), :]
            + grads[pl.ds(8 + 2 + f, OWN, stride=8), :]
            + grads[pl.ds(16 + 4 + f, OWN, stride=8), :]
        )
        noise_pred = kept[f, pl.ds(3, OWN), :]
        pull = kept[2 + f, pl.ds(3, OWN), :]
        out_ref[f, :, :] = -noise_pred / noise_sigma + (
            pull - noise_sigma * summed
        ) * over_alpha


def score(*operands):
    vmem = pl.BlockSpec(memory_space=pltpu.VMEM)
    smem = pl.BlockSpec(memory_space=pltpu.SMEM)
    return pl.pallas_call(
        score_kernel,
        out_shape=jax.ShapeDtypeStruct((2, OWN, WIDTH), F32),
        in_specs=[smem, smem] + [vmem] * 14,
        out_specs=vmem,
        scratch_shapes=[
            pltpu.VMEM((3, 18, 32, WIDTH), F32),
            pltpu.VMEM((WINDOWS, 2 * SPAN, WIDTH), F32),
            pltpu.VMEM((SPAN, WIDTH), F32),
            pltpu.VMEM((32 * 48, WIDTH), F32),
            pltpu.VMEM((26 * 3 * HID, WIDTH), BF16),
            pltpu.VMEM((26 * HID, WIDTH), F32),
            pltpu.VMEM((24 * HID, WIDTH), F32),
            pltpu.VMEM((32 * 8, WIDTH), F32),
            pltpu.VMEM((SPAN * 16, WIDTH), F32),
            pltpu.VMEM((20 * 3 * HID, WIDTH), BF16),
            pltpu.VMEM((18 * 8, WIDTH), F32),
            pltpu.VMEM((4, SPAN, WIDTH), F32),
        ],
        compiler_params=pltpu.CompilerParams(vmem_limit_bytes=32 * 1024 * 1024),
        cost_estimate=pl.CostEstimate(
            flops=5_000_000_000, bytes_accessed=1_000_000, transcendentals=1_000_000
        ),
        name="score",
    )(
        *operands
    )


def padded(array, axis, size):
    pads = [(0, 0)] * array.ndim
    pads[axis] = (0, size - array.shape[axis])
    return jnp.pad(array, pads)


def matrices(w_in, w_mid, w_out):
    taps = w_mid.reshape(9, HID, HID)
    mid = jnp.transpose(taps, (1, 0, 2)).reshape(HID, 9 * HID)
    mid_adj = jnp.transpose(taps[::-1], (2, 0, 1)).reshape(HID, 9 * HID)
    first = padded(jnp.transpose(w_in, (0, 2, 3, 1)), 3, 16).reshape(HID, 144)
    last = padded(
        jnp.transpose(w_out, (3, 2, 0, 1)).reshape(3, 6, HID), 1, 8
    ).reshape(24, HID)
    flipped_out = w_out[:, :, ::-1, ::-1]
    last_adj = padded(
        jnp.transpose(flipped_out, (1, 2, 3, 0)).reshape(HID, 3, 6), 2, 16
    ).reshape(HID, 48)
    flipped_in = w_in[:, :, ::-1, ::-1].reshape(HID, WINDOWS, 2, 3, 3)[:, ::-1]
    first_adj = padded(
        jnp.transpose(flipped_in, (1, 4, 3, 2, 0)).reshape(WINDOWS, 3, 6, HID), 2, 8
    ).reshape(WINDOWS, 24, HID)
    return first, mid, last, last_adj, jnp.concatenate([mid_adj, last_adj], axis=1), first_adj


def on_device(
    trajectory, observed, station_rows, station_cols, step_index, w_in, w_mid, w_out, noise_gain
):
    place = lax.axis_index("tm")
    part = lax.axis_index("rows")
    count = lax.axis_size("tm")
    noise_alpha, noise_sigma, obs_kappa = noise_level(step_index)
    own_state = trajectory[0]

    far = lax.ppermute(own_state, "rows", [(1, 2), (2, 1), (3, 0), (0, 3)])
    near = lax.ppermute(own_state, "rows", [(0, 1), (1, 0), (2, 3), (3, 2)])
    high = observed[0].astype(BF16)
    low = (observed[0] - high.astype(F32)).astype(BF16)
    seen = jnp.concatenate([high, low], axis=0).reshape(SEEN, WIDTH)
    even = part % 2 == 0
    above = jnp.where(even, far, near)[:, OWN - EDGE :].reshape(2 * EDGE, WIDTH)
    below = jnp.where(even, near, far)[:, :EDGE].reshape(2 * EDGE, WIDTH)
    own = jnp.concatenate([own_state.reshape(2 * OWN, WIDTH), above, below, seen], axis=0)

    def ring(value, steps):
        return lax.ppermute(value, "tm", [(k, (k + steps) % count) for k in range(count)])

    before = ring(own, 1)
    after = ring(own, -1)
    own, w_mid = lax.optimization_barrier((own, w_mid))
    first, mid, last, last_adj, back, first_adj = matrices(w_in, w_mid, w_out)
    bias = jnp.broadcast_to((noise_sigma * noise_gain)[:, None], (HID, WIDTH))
    states = place + jnp.arange(-2 * REACH, 2 * REACH + 1)
    inside = ((states >= 0) & (states < count)).astype(F32)
    scalars = jnp.concatenate(
        [jnp.stack([noise_alpha, noise_sigma, obs_kappa]), inside, jnp.zeros(4, F32)]
    )

    three = jnp.concatenate([before[:BLOCK], own[:BLOCK], after[:BLOCK]], axis=0)
    near_after = jnp.concatenate([three, after[BLOCK:]], axis=0)
    near_before = jnp.concatenate([three, before[BLOCK:]], axis=0)
    far_before = ring(near_after, 3)
    far_after = ring(near_before, -3)

    posterior = score(
        scalars,
        (part * OWN - 3).reshape(1).astype(jnp.int32),
        station_rows.reshape(-1, WIDTH),
        station_cols.reshape(-1, WIDTH),
        seen,
        near_after,
        near_before,
        far_before,
        far_after,
        bias,
        first,
        mid,
        last,
        last_adj,
        back,
        first_adj,
    )
    return posterior[None]


def solution(mesh):
    return jax.shard_map(
        on_device,
        mesh=mesh,
        in_specs=(
            P("tm", None, "rows", None),
            P("tm", None, None),
            P(),
            P(),
            P(),
            P(),
            P(),
            P(),
            P(),
        ),
        out_specs=P("tm", None, "rows", None),
        check_vma=False,
    )
```

time: 129 us -> 66.6 us (0.52)
  Pallas kernels: 78.5 us -> 18.2 us
  waiting for transfers between devices: 3.72 us -> 0.79 us
    pallas_call x2 -> x1, Pallas kernels: 78.5 us -> 18.2 us  [score(): pl.pallas_call(score_kernel, out_shape=jax.ShapeDtypeStruct((2, OWN, WIDT...]
    ppermute x4, waiting for transfers between devices: 3.71 us -> 0.79 us  [ring(): lax.ppermute(value, 'tm', [(k, (k + steps) % count) for k in range(count)])]
    unnamed x13 -> x17, local copies, waits for them, and re-layouts: 3.86 us -> 3.17 us
  transfers between devices with their start and end apart: 6 -> 6, of which waited for: 3 -> 1; matrix products, arithmetic and copies ran while one was open for 2% -> 4% of each run, Pallas kernels for 1% -> 0%
where the time goes in v2:
time: 66.6 us; the launch traced here: 65.9 us
  starting transfers between devices  39 us (59%)
  Pallas kernels  18.2 us (27%)
  local copies, waits for them, and re-layouts  5.96 us (9%)
  between operations  1.18 us (2%)
  other arithmetic  0.84 us (1%)
  waiting for transfers between devices  0.79 us (1%)
    ppermute x4, starting transfers between devices, ring(): lax.ppermute(value, 'tm', [(k, (k + steps) % count) for k in range(count)])  25 us
    pallas_call x1, Pallas kernels, score(): pl.pallas_call(score_kernel, out_shape=jax.ShapeDtypeStruct((2, OWN, WIDT...  18.2 us
    ppermute x1, starting transfers between devices, on_device(): far = lax.ppermute(own_state, 'rows', [(1, 2), (2, 1), (3, 0), (0, 3)])  12 us
    unnamed x17, local copies, waits for them, and re-layouts  3.17 us
    ppermute x1, starting transfers between devices, on_device(): near = lax.ppermute(own_state, 'rows', [(0, 1), (1, 0), (2, 3), (3, 2)])  1.92 us
  transfers between devices with their start and end apart: 6, of which 1 were waited for; matrix products, arithmetic and copies ran while one was open for 4% of the time, Pallas kernels for 0%

profile of v2, /device:TPU:1, one launch (start us, length us, event | category | flops | bytes accessed | tf_op | source)
XLA Modules:
  0.0 65.9 jit_solution(7306052118565757498)
XLA Ops:
  0.0 12.0 %collective-permute-start = (bf16[2,16,128]{2,1,0:T(8,128)(2,1)}, bf16[2,16,128]{2,1,0:T(8,128)(2,1)S(1)}, u32[]{:S(2)}, u32[]{:S(2)}) collective-permute-start(bf16[2,16,128]{2,1,0:T(8,128)(2,1)} %bitcast.51), channel_id=1, source_target_pairs={{1,2},{2,1},{3,0},{0,3},{5,6},{6,5},{7,4},{4,7},{9,10},{10,9},{11,... | collective-permute-start | bytes 24584 | tf_op jit(solution)/shard_map/ppermute | solution.py:378
  12.0 1.9 %collective-permute-start.1 = (bf16[2,16,128]{2,1,0:T(8,128)(2,1)}, bf16[2,16,128]{2,1,0:T(8,128)(2,1)S(1)}, u32[]{:S(2)}, u32[]{:S(2)}) collective-permute-start(bf16[2,16,128]{2,1,0:T(8,128)(2,1)} %bitcast.52), channel_id=1, source_target_pairs={{0,1},{1,0},{2,3},{3,2},{4,5},{5,4},{6,7},{7,6},{8,9},{9,8},{10,11... | collective-permute-start | bytes 24584 | tf_op jit(solution)/shard_map/ppermute | solution.py:379
  14.0 0.7 %fusion = (bf16[2,1024]{1,0:T(2,128)(2,1)S(1)}, bf16[2,1024]{1,0:T(2,128)(2,1)S(1)}) fusion(f32[1,2,1024]{2,1,0:T(2,128)} %param.10), kind=kLoop, calls=%fused_computation.11 | loop fusion | flops 8192 | bytes 16384 | tf_op jit(solution)/shard_map/convert_element_type | solution.py:381
  15.4 0.8 %rev.14 = bf16[96,10,3,3]{0,3,2,1:T(4,128)(2,1)S(1)} reverse(bf16[96,10,3,3]{0,3,2,1:T(4,128)(2,1)} %param.14), dimensions={2,3} | reverse | bytes 34560 | tf_op jit(solution)/shard_map/rev | solution.py:362
  16.3 0.0 copy-start.5
  16.3 0.7 copy-done.5
  17.1 0.0 copy-start.7
  17.1 0.6 copy-done.7
  17.7 0.0 copy-start.6
  17.7 0.0 copy-start.3
  17.8 0.0 copy-start.2
  17.8 0.0 collective-permute-done.1
  17.8 0.6 copy-done.6
  18.4 3.2 %collective-permute-start.2 = (bf16[96,128]{1,0:T(8,128)(2,1)S(1)}, bf16[96,128]{1,0:T(8,128)(2,1)S(1)}, u32[]{:S(2)}, u32[]{:S(2)}) collective-permute-start(bf16[96,128]{1,0:T(8,128)(2,1)S(1)} %pad_maximum_fusion.4), channel_id=1, source_target_pairs={{0,4},{4,8},{8,12},{12,16},{16,20},{20,24},{24,28},{28,32},{32,36}... | collective-permute-start | bytes 73736 | tf_op jit(solution)/shard_map/ppermute | solution.py:389
  21.6 8.7 %collective-permute-start.3 = (bf16[96,128]{1,0:T(8,128)(2,1)S(1)}, bf16[96,128]{1,0:T(8,128)(2,1)S(1)}, u32[]{:S(2)}, u32[]{:S(2)}) collective-permute-start(bf16[96,128]{1,0:T(8,128)(2,1)S(1)} %pad_maximum_fusion.4), channel_id=1, source_target_pairs={{0,508},{4,0},{8,4},{12,8},{16,12},{20,16},{24,20},{28,24},{32,28}... | collective-permute-start | bytes 73736 | tf_op jit(solution)/shard_map/ppermute | solution.py:389
  30.5 0.1 copy.23.w_out_adj_ref
  30.7 0.1 copy.21.w_in_ref
  30.8 0.1 concatenate.21.scalars_ref
  30.9 0.2 reshape.68
  31.2 0.2 copy.18
  31.4 0.6 copy-done.4
  32.0 0.7 %slice-done = bf16[64,128]{1,0:T(8,128)(2,1)S(1)} async-done(((bf16[96,128]{1,0:T(8,128)(2,1)}), bf16[64,128]{1,0:T(8,128)(2,1)S(1)}, s32[]{:S(2)}) %slice-start) | async-done | bytes 16408 | tf_op jit(solution)/shard_map/slice | solution.py:402
  32.7 1.9 %collective-permute-start.4 = (bf16[224,128]{1,0:T(8,128)(2,1)S(1)}, bf16[224,128]{1,0:T(8,128)(2,1)S(1)}, u32[]{:S(2)}, u32[]{:S(2)}) collective-permute-start(bf16[224,128]{1,0:T(8,128)(2,1)S(1)} %get-tuple-element.12.near_after_ref), channel_id=1, source_target_pairs={{0,12},{4,16},{8,20},{12,24},{16,28},{20,32},{24,36},{28,40},{32,4... | collective-permute-start | bytes 172040 | tf_op jit(solution)/shard_map/ppermute | solution.py:389
  34.6 11.2 %collective-permute-start.5 = (bf16[224,128]{1,0:T(8,128)(2,1)S(1)}, bf16[224,128]{1,0:T(8,128)(2,1)S(1)}, u32[]{:S(2)}, u32[]{:S(2)}) collective-permute-start(bf16[224,128]{1,0:T(8,128)(2,1)S(1)} %get-tuple-element.11.near_before_ref), channel_id=1, source_target_pairs={{0,500},{4,504},{8,508},{12,0},{16,4},{20,8},{24,12},{28,16},{32,2... | collective-permute-start | bytes 172040 | tf_op jit(solution)/shard_map/ppermute | solution.py:389
  45.8 0.1 pad_maximum_fusion.w_back_ref
  45.9 0.2 copy.16
  46.1 0.2 copy.22.w_mid_ref
  46.2 0.8 %collective-permute-done.5.far_after_ref = bf16[224,128]{1,0:T(8,128)(2,1)S(1)} collective-permute-done((bf16[224,128]{1,0:T(8,128)(2,1)S(1)}, bf16[224,128]{1,0:T(8,128)(2,1)S(1)}, u32[]{:S(2)}, u32[]{:S(2)}) %collective-permute-start.5) | collective-permute-done | bytes 57376 | tf_op jit(solution)/shard_map/ppermute | solution.py:389
  47.0 0.1 broadcast_in_dim.4.bias_ref
  47.1 0.6 copy-done
  47.7 0.0 copy-done.1
  47.7 18.2 %score.1 = f32[2,16,128]{2,1,0:T(8,128)} custom-call(f32[16]{0:T(128)S(1)} %concatenate.21.scalars_ref, s32[1]{0:T(128)} %bitcast.3.first_ref, s32[8,128]{1,0:T(8,128)S(1)} %bitcast.41, s32[8,128]{1,0:T(8,128)S(1)} %bitcast.42, bf16[32,128]{1,0:T(8,128)(2,1)S(1)} %reshape.64.seen_ref, bf16[224,128]{1,0:T(8,128)(2,1)S(1)} %get-tuple-element.12.near_after_ref, ...), custom_call_target="tpu_custom_call" | custom-call | flops 5000000000 | bytes 1000000 | tf_op jit(solution)/shard_map/score/pallas_call | solution.py:315
  (35 shorter events, 0.3 us)
Async XLA Ops:
  0.0 17.8 %collective-permute-start = (bf16[2,16,128]{2,1,0:T(8,128)(2,1)}, bf16[2,16,128]{2,1,0:T(8,128)(2,1)S(1)}, u32[]{:S(2)}, u32[]{:S(2)}) collective-permute-start(bf16[2,16,128]{2,1,0:T(8,128)(2,1)} %bitcast.51), channel_id=1, source_target_pairs={{1,2},{2,1},{3,0},{0,3},{5,6},{6,5},{7,4},{4,7},{9,10},{10,9},{11,... | collective-permute-start | bytes 24584 | tf_op jit(solution)/shard_map/ppermute | solution.py:378
  12.0 5.8 %collective-permute-start.1 = (bf16[2,16,128]{2,1,0:T(8,128)(2,1)}, bf16[2,16,128]{2,1,0:T(8,128)(2,1)S(1)}, u32[]{:S(2)}, u32[]{:S(2)}) collective-permute-start(bf16[2,16,128]{2,1,0:T(8,128)(2,1)} %bitcast.52), channel_id=1, source_target_pairs={{0,1},{1,0},{2,3},{3,2},{4,5},{5,4},{6,7},{7,6},{8,9},{9,8},{10,11... | collective-permute-start | bytes 24584 | tf_op jit(solution)/shard_map/ppermute | solution.py:379
  16.3 0.7 %copy-start.5 = (bf16[2,96,3,3]{1,0,3,2:T(2,128)(2,1)S(1)}, bf16[2,96,3,3]{1,0,3,2:T(2,128)(2,1)}, u32[]{:S(2)}) copy-start(bf16[2,96,3,3]{1,0,3,2:T(2,128)(2,1)} %param.16) | copy-start | bytes 10372
  17.1 0.7 copy-start.7
  17.7 0.7 %copy-start.6 = (bf16[1,2,16,128]{3,2,1,0:T(8,128)(2,1)S(1)}, bf16[1,2,16,128]{3,2,1,0:T(8,128)(2,1)}, u32[]{:S(2)}) copy-start(bf16[1,2,16,128]{3,2,1,0:T(8,128)(2,1)} %param.9) | copy-start | bytes 24580
  17.7 12.7 %copy-start.3 = (bf16[96,10,3,3]{0,3,2,1:T(4,128)(2,1)S(1)}, bf16[96,10,3,3]{0,3,2,1:T(4,128)(2,1)}, u32[]{:S(2)}) copy-start(bf16[96,10,3,3]{0,3,2,1:T(4,128)(2,1)} %param.14) | copy-start | bytes 51844
  17.8 13.2 %copy-start.2 = (bf16[3,3,9216]{2,1,0:T(4,128)(2,1)S(1)}, bf16[3,3,9216]{2,1,0:T(4,128)(2,1)}, u32[]{:S(2)}) copy-start(bf16[3,3,9216]{2,1,0:T(4,128)(2,1)} %param.15) | copy-start | bytes 497668
  18.4 12.9 %collective-permute-start.2 = (bf16[96,128]{1,0:T(8,128)(2,1)S(1)}, bf16[96,128]{1,0:T(8,128)(2,1)S(1)}, u32[]{:S(2)}, u32[]{:S(2)}) collective-permute-start(bf16[96,128]{1,0:T(8,128)(2,1)S(1)} %pad_maximum_fusion.4), channel_id=1, source_target_pairs={{0,4},{4,8},{8,12},{12,16},{16,20},{20,24},{24,28},{28,32},{32,36}... | collective-permute-start | bytes 73736 | tf_op jit(solution)/shard_map/ppermute | solution.py:389
  21.6 10.3 %collective-permute-start.3 = (bf16[96,128]{1,0:T(8,128)(2,1)S(1)}, bf16[96,128]{1,0:T(8,128)(2,1)S(1)}, u32[]{:S(2)}, u32[]{:S(2)}) collective-permute-start(bf16[96,128]{1,0:T(8,128)(2,1)S(1)} %pad_maximum_fusion.4), channel_id=1, source_target_pairs={{0,508},{4,0},{8,4},{12,8},{16,12},{20,16},{24,20},{28,24},{32,28}... | collective-permute-start | bytes 73736 | tf_op jit(solution)/shard_map/ppermute | solution.py:389
  31.3 0.6 copy-start.4
  31.9 0.7 %slice-start = ((bf16[96,128]{1,0:T(8,128)(2,1)}), bf16[64,128]{1,0:T(8,128)(2,1)S(1)}, s32[]{:S(2)}) async-start(bf16[96,128]{1,0:T(8,128)(2,1)} %copy-done.4), calls=%async_computation | async-start | bytes 32768 | tf_op jit(solution)/shard_map/slice | solution.py:402
  32.0 0.7 %slice-start.1 = ((bf16[96,128]{1,0:T(8,128)(2,1)}), bf16[32,128]{1,0:T(8,128)(2,1)S(1)}, s32[]{:S(2)}) async-start(bf16[96,128]{1,0:T(8,128)(2,1)} %copy-done.4), calls=%async_computation.1 | async-start | bytes 16384 | tf_op jit(solution)/shard_map/slice | solution.py:404
  32.7 13.6 %collective-permute-start.4 = (bf16[224,128]{1,0:T(8,128)(2,1)S(1)}, bf16[224,128]{1,0:T(8,128)(2,1)S(1)}, u32[]{:S(2)}, u32[]{:S(2)}) collective-permute-start(bf16[224,128]{1,0:T(8,128)(2,1)S(1)} %get-tuple-element.12.near_after_ref), channel_id=1, source_target_pairs={{0,12},{4,16},{8,20},{12,24},{16,28},{20,32},{24,36},{28,40},{32,4... | collective-permute-start | bytes 172040 | tf_op jit(solution)/shard_map/ppermute | solution.py:389
  34.6 12.4 %collective-permute-start.5 = (bf16[224,128]{1,0:T(8,128)(2,1)S(1)}, bf16[224,128]{1,0:T(8,128)(2,1)S(1)}, u32[]{:S(2)}, u32[]{:S(2)}) collective-permute-start(bf16[224,128]{1,0:T(8,128)(2,1)S(1)} %get-tuple-element.11.near_before_ref), channel_id=1, source_target_pairs={{0,500},{4,504},{8,508},{12,0},{16,4},{20,8},{24,12},{28,16},{32,2... | collective-permute-start | bytes 172040 | tf_op jit(solution)/shard_map/ppermute | solution.py:389
  47.0 0.7 %copy-start = (s32[1024]{0:T(1024)S(1)}, s32[1024]{0:T(1024)}, u32[]{:S(2)}) copy-start(s32[1024]{0:T(1024)} %param.11) | copy-start | bytes 12292
  47.0 0.7 %copy-start.1 = (s32[1024]{0:T(1024)S(1)}, s32[1024]{0:T(1024)}, u32[]{:S(2)}) copy-start(s32[1024]{0:T(1024)} %param.12) | copy-start | bytes 12292

commit v3 on v2

v3 whole, which is shorter than its diff:
```python
import math

import jax
import jax.numpy as jnp
from jax import lax
from jax.experimental import pallas as pl
from jax.experimental.pallas import tpu as pltpu
from jax.sharding import PartitionSpec as P

NSTEPS = 256
HID = 96
WIDTH = 128
OWN = 16
REACH = 2
WINDOWS = 2 * REACH + 1
SPAN = 24
EDGE = 8
BLOCK = 2 * OWN + 4 * EDGE
STATIONS = 1024
SEEN = 4 * STATIONS // WIDTH
ONE = BLOCK + SEEN
THREE = 3 * ONE
ORDER = tuple((step, at - step) for at in range(WINDOWS + 5) for step in range(5) if 0 <= at - step < WINDOWS)
F32 = jnp.float32
BF16 = jnp.bfloat16


def noise_level(step_index):
    phase_time = (step_index[0].astype(F32) + 0.5) / NSTEPS
    noise_alpha = jnp.cos(0.5 * math.pi * phase_time)
    noise_sigma = jnp.sin(0.5 * math.pi * phase_time)
    obs_kappa = 1.0 + (noise_sigma / noise_alpha) ** 2
    return noise_alpha, noise_sigma, obs_kappa


def station_sums(first, stations_ref, seen):
    left_side, at_column = [], []
    chunks = STATIONS // WIDTH
    for chunk in range(chunks):
        offset = stations_ref[chunk : chunk + 1, :] - first
        offset = jnp.where(offset < 0, offset + 64, offset)
        offset = jnp.where(offset >= 64, offset - 64, offset)
        place = lax.broadcasted_iota(jnp.int32, (SPAN, WIDTH), 0)
        hit = place == jnp.broadcast_to(offset, (SPAN, WIDTH))
        parts = [jnp.where(hit, 1.0, 0.0)]
        for values in seen:
            for part in range(4):
                row = values[chunks * part + chunk : chunks * part + chunk + 1, :]
                parts.append(jnp.where(hit, jnp.broadcast_to(row, (SPAN, WIDTH)), 0.0))
        left_side.append(jnp.concatenate(parts, axis=0).astype(BF16))
        column = lax.broadcasted_iota(jnp.int32, (WIDTH, WIDTH), 0)
        at = stations_ref[chunks + chunk : chunks + chunk + 1, :]
        at = jnp.broadcast_to(at, (WIDTH, WIDTH))
        at_column.append(jnp.where(column == at, 1.0, 0.0).astype(BF16))
    sums = lax.dot_general(
        jnp.concatenate(left_side, axis=1),
        jnp.concatenate(at_column, axis=1),
        (((1,), (1,)), ((), ())),
        preferred_element_type=F32,
    )
    results = []
    for k in range(len(seen)):
        start = SPAN * (4 * k + 1)
        results.append(
            sums[start : start + 2 * SPAN] + sums[start + 2 * SPAN : start + 4 * SPAN]
        )
    return results + [sums[:SPAN]]


def logistic(values):
    return 0.5 + 0.5 * jnp.tanh(0.5 * values)


def rolled(values, shift):
    if shift == 0:
        return values
    return jnp.concatenate(
        [
            pltpu.roll(values[:, k : k + WIDTH], (-shift) % WIDTH, 1)
            for k in range(0, values.shape[1], WIDTH)
        ],
        axis=1,
    )


def store_shifted(ref, start, step, values):
    low = values.astype(BF16)
    for b in range(3):
        moved = rolled(low, b - 1)
        for k in range(values.shape[1] // WIDTH):
            ref[pl.ds((3 * (start + step * k) + b) * HID, HID), :] = moved[
                :, k * WIDTH : (k + 1) * WIDTH
            ]


def side_by_side(ref, start, step, depth, count):
    return jnp.concatenate(
        [ref[pl.ds(start + k * step, depth), :] for k in range(count)], axis=1
    )


def dot(left, right):
    return lax.dot_general(
        left, right, (((1,), (0,)), ((), ())), preferred_element_type=F32
    )


def folded(product):
    return rolled(product[0:8], -1) + product[8:16] + rolled(product[16:24], 1)


def score_kernel(
    scalars_ref,
    first_ref,
    stations_ref,
    near_ref,
    far_before_ref,
    far_after_ref,
    end_ref,
    bias_ref,
    w_in_ref,
    w_mid_ref,
    w_out_ref,
    w_out_adj_ref,
    w_back_ref,
    w_in_adj_ref,
    out_ref,
    moved,
    sums,
    count,
    blanket,
    hidden,
    slope_one,
    slope_two,
    folds,
    pull_slabs,
    back,
    slopes,
    grads,
    kept,
):
    noise_alpha = scalars_ref[0]
    noise_sigma = scalars_ref[1]
    obs_kappa = scalars_ref[2]
    over_alpha = 1.0 / noise_alpha
    over_kappa = 1.0 / obs_kappa

    blanket[...] = jnp.zeros_like(blanket)
    folds[...] = jnp.zeros_like(folds)
    pull_slabs[...] = jnp.zeros_like(pull_slabs)

    def rows_of(ref, start):
        above = ref[pl.ds(start + 2 * OWN, 2 * EDGE), :].astype(F32)
        below = ref[pl.ds(start + 2 * OWN + 2 * EDGE, 2 * EDGE), :].astype(F32)
        return [
            jnp.concatenate(
                [
                    above[EDGE * f : EDGE * (f + 1)],
                    ref[pl.ds(start + OWN * f, OWN), :].astype(F32),
                    below[EDGE * f : EDGE * (f + 1)],
                ],
                axis=0,
            )
            for f in range(2)
        ]

    at_low, at_high = scalars_ref[3], scalars_ref[4]
    end = rows_of(end_ref, SEEN)
    for s in range(4 * REACH + 1):
        ref = (far_before_ref, near_ref, far_after_ref)[s // 3]
        fields = rows_of(ref, ONE * (s % 3) + SEEN)
        for f in range(2):
            field = fields[f]
            if s == REACH:
                field = field + at_low * end[f]
            if s == 3 * REACH:
                field = field + at_high * end[f]
            for b in range(3):
                moved[b, 2 * s + f, :, :] = rolled(field, b - 1)

    seen = [
        ref[pl.ds(ONE * k, SEEN), :].astype(F32)
        for ref, k in (
            (far_before_ref, 2),
            (near_ref, 0),
            (near_ref, 1),
            (near_ref, 2),
            (far_after_ref, 0),
        )
    ]
    end_seen = end_ref[pl.ds(0, SEEN), :].astype(F32)
    seen[0] = seen[0] + at_low * end_seen
    seen[-1] = seen[-1] + at_high * end_seen
    *totals, stations = station_sums(first_ref[0], stations_ref, seen)
    for k in range(WINDOWS):
        sums[k, :, :] = totals[k]
    count[...] = stations

    def first_layer(w):
        for b in range(3):
            for channel in range(2 * WINDOWS):
                blanket[w, pl.ds(16 * b + channel, 32, stride=48), :] = moved[
                    b, 2 * w + channel, :, :
                ]

        values = dot(w_in_ref[...], side_by_side(blanket.at[w], 96, 144, 240, 9).astype(BF16))
        for j in range(3):
            part = values[HID * j : HID * (j + 1)] + jnp.concatenate([bias_ref[...]] * 9, axis=1)
            gate = logistic(part)
            result = part * gate
            slope = gate + result * (1.0 - gate)
            store_shifted(hidden.at[w], j, 3, result)
            for k in range(9):
                slope_one[w, pl.ds(HID * (3 * k + j), HID), :] = slope[:, k * WIDTH : (k + 1) * WIDTH]

    def second_layer(w):
        values = dot(w_mid_ref[...], side_by_side(hidden.at[w], 0, 3 * HID, 9 * HID, 24))
        gate = logistic(values)
        result = values * gate
        slope = gate + result * (1.0 - gate)
        residual = side_by_side(hidden.at[w], 4 * HID, 3 * HID, HID, 24)
        high = (residual.astype(F32) + result).astype(BF16)
        for k in range(24):
            slope_two[w, pl.ds(HID * k, HID), :] = slope[:, k * WIDTH : (k + 1) * WIDTH]
        pairs = jnp.concatenate(
            [
                jnp.concatenate(
                    [high[:, (2 * k + j) * WIDTH : (2 * k + j + 1) * WIDTH] for j in range(2)],
                    axis=0,
                )
                for k in range(12)
            ],
            axis=1,
        )
        fold = folded(dot(w_out_ref[...], pairs))
        for k in range(12):
            folds[w, pl.ds(8 * k, 8), :] = fold[:, k * WIDTH : (k + 1) * WIDTH]

    def find_pull(w):
        half = SPAN // 2
        for f in range(2):
            for j in range(2):
                noise_pred = (
                    folds[w, pl.ds(4 + 2 * j + f, half, stride=8), :]
                    + folds[w, pl.ds(8 + 2 * j + f, half, stride=8), :]
                )
                state = moved[1, 2 * w + 2 * REACH + f, pl.ds(5 + j, half, stride=2), :]
                denoised = (state - noise_sigma * noise_pred) * over_alpha
                total = sums[w, pl.ds(SPAN * f + j, half, stride=2), :]
                stations = count[pl.ds(j, half, stride=2), :]
                pull = (total - stations * denoised) * over_kappa
                for b in range(3):
                    pull_slabs[w, pl.ds(16 * j + 2 * b + f, half, stride=32), :] = rolled(pull, b - 1)

                if w == REACH:
                    kept[f, pl.ds(j, half, stride=2), :] = noise_pred
                    kept[2 + f, pl.ds(j, half, stride=2), :] = pull

    def second_back(w):
        gradient = dot(w_out_adj_ref[...], side_by_side(pull_slabs.at[w], 0, 80, 112, 4).astype(BF16))
        for j in range(5):
            slope = side_by_side(slope_two.at[w], HID * (2 + j), 5 * HID, HID, 4)
            store_shifted(back.at[w], j, 5, gradient[HID * j : HID * (j + 1)] * slope)

    def first_back(w):
        operand = jnp.concatenate(
            [
                side_by_side(back.at[w], 0, 3 * HID, 9 * HID, 18),
                side_by_side(pull_slabs.at[w], 16, 16, 48, 18).astype(BF16),
            ],
            axis=0,
        )
        slope = side_by_side(slope_one.at[w], 4 * HID, HID, HID, 18)
        low = (dot(w_back_ref[...], operand) * slope).astype(BF16)
        for k in range(18):
            at = HID * (WINDOWS * k + w)
            slopes[pl.ds(at, HID), :] = low[:, k * WIDTH : (k + 1) * WIDTH]

    passes = (first_layer, second_layer, find_pull, second_back, first_back)
    for step, w in ORDER:
        passes[step](w)

    stacked = side_by_side(slopes, 0, WINDOWS * HID, WINDOWS * HID, 18)
    fold = folded(dot(w_in_adj_ref[...], stacked))
    for k in range(18):
        grads[pl.ds(8 * k, 8), :] = fold[:, k * WIDTH : (k + 1) * WIDTH]
    for f in range(2):
        summed = (
            grads[pl.ds(f, OWN, stride=8), :]
            + grads[pl.ds(8 + 2 + f, OWN, stride=8), :]
            + grads[pl.ds(16 + 4 + f, OWN, stride=8), :]
        )
        noise_pred = kept[f, pl.ds(3, OWN), :]
        pull = kept[2 + f, pl.ds(3, OWN), :]
        out_ref[f, :, :] = -noise_pred / noise_sigma + (
            pull - noise_sigma * summed
        ) * over_alpha


def score(*operands):
    vmem = pl.BlockSpec(memory_space=pltpu.VMEM)
    smem = pl.BlockSpec(memory_space=pltpu.SMEM)
    return pl.pallas_call(
        score_kernel,
        out_shape=jax.ShapeDtypeStruct((2, OWN, WIDTH), F32),
        in_specs=[smem, smem] + [vmem] * 12,
        out_specs=vmem,
        scratch_shapes=[
            pltpu.VMEM((3, 18, 32, WIDTH), F32),
            pltpu.VMEM((WINDOWS, 2 * SPAN, WIDTH), F32),
            pltpu.VMEM((SPAN, WIDTH), F32),
            pltpu.VMEM((WINDOWS, 32 * 48, WIDTH), F32),
            pltpu.VMEM((WINDOWS, 27 * 3 * HID, WIDTH), BF16),
            pltpu.VMEM((WINDOWS, 27 * HID, WIDTH), F32),
            pltpu.VMEM((WINDOWS, 24 * HID, WIDTH), F32),
            pltpu.VMEM((WINDOWS, 16 * 8, WIDTH), F32),
            pltpu.VMEM((WINDOWS, SPAN * 16, WIDTH), F32),
            pltpu.VMEM((WINDOWS, 20 * 3 * HID, WIDTH), BF16),
            pltpu.VMEM((18 * WINDOWS * HID, WIDTH), BF16),
            pltpu.VMEM((18 * 8, WIDTH), F32),
            pltpu.VMEM((4, SPAN, WIDTH), F32),
        ],
        compiler_params=pltpu.CompilerParams(vmem_limit_bytes=50 * 1024 * 1024),
        cost_estimate=pl.CostEstimate(
            flops=5_000_000_000, bytes_accessed=1_000_000, transcendentals=1_000_000
        ),
        name="score",
    )(
        *operands
    )


def padded(array, axis, size):
    pads = [(0, 0)] * array.ndim
    pads[axis] = (0, size - array.shape[axis])
    return jnp.pad(array, pads)


def stepped(matrix, step, rows, depth):
    width = matrix.shape[1]
    return jnp.concatenate(
        [
            jnp.pad(matrix, ((0, 0), (step * k, depth - width - step * k)))
            for k in range(rows)
        ],
        axis=0,
    )


def matrices(w_in, w_mid, w_out, inside):
    taps = w_mid.reshape(9, HID, HID)
    mid = jnp.transpose(taps, (1, 0, 2)).reshape(HID, 9 * HID)
    mid_adj = jnp.transpose(taps[::-1], (2, 0, 1)).reshape(HID, 9 * HID)
    first = padded(jnp.transpose(w_in, (0, 2, 3, 1)), 3, 16).reshape(HID, 144)
    by_tap = jnp.transpose(w_out, (3, 2, 0, 1))
    by_tap = jnp.concatenate([by_tap[:, k : k + 1] for k in (2, 1, 0)], axis=1)
    last = jnp.concatenate(
        [
            jnp.pad(by_tap, ((0, 0), (k, 1 - k), (0, 0), (0, 0))).reshape(24, HID)
            for k in range(2)
        ],
        axis=1,
    )
    flipped_out = w_out[:, :, ::-1, ::-1]
    last_adj = padded(
        jnp.transpose(flipped_out, (1, 2, 3, 0)).reshape(HID, 3, 6), 2, 16
    ).reshape(HID, 48)
    flipped_in = w_in[:, :, ::-1, ::-1].reshape(HID, WINDOWS, 2, 3, 3)[:, ::-1]
    first_adj = jnp.transpose(flipped_in, (4, 3, 2, 1, 0)) * inside.astype(BF16)[:, None]
    first_adj = padded(first_adj.reshape(3, 6, WINDOWS * HID), 1, 8).reshape(24, WINDOWS * HID)
    return (
        stepped(first, 48, 3, 240),
        mid,
        last,
        stepped(last_adj, 16, 5, 112),
        jnp.concatenate([mid_adj, last_adj], axis=1),
        first_adj,
    )


def on_device(
    trajectory, observed, station_rows, station_cols, step_index, w_in, w_mid, w_out, noise_gain
):
    place = lax.axis_index("tm")
    part = lax.axis_index("rows")
    count = lax.axis_size("tm")
    own_state = trajectory[0]

    far = lax.ppermute(own_state, "rows", [(1, 2), (2, 1), (3, 0), (0, 3)])
    near = lax.ppermute(own_state, "rows", [(0, 1), (1, 0), (2, 3), (3, 2)])
    high = observed[0].astype(BF16)
    low = (observed[0] - high.astype(F32)).astype(BF16)
    seen = jnp.concatenate([high, low], axis=0).reshape(SEEN, WIDTH)
    base = jnp.concatenate([seen, own_state.reshape(2 * OWN, WIDTH)], axis=0)
    base = lax.optimization_barrier(base)
    even = part % 2 == 0
    above = jnp.where(even, far, near)[:, OWN - EDGE :].reshape(2 * EDGE, WIDTH)
    below = jnp.where(even, near, far)[:, :EDGE].reshape(2 * EDGE, WIDTH)
    own = jnp.concatenate([base, above, below], axis=0)

    def passed(value, steps):
        pairs = [(k, k + steps) for k in range(count) if 0 <= k + steps < count]
        return lax.ppermute(value, "tm", pairs)

    before = passed(own, 1)
    after = passed(own, -1)
    end = lax.ppermute(own, "tm", [(0, 2), (count - 1, count - 3)])
    own, w_mid = lax.optimization_barrier((own, w_mid))
    near = jnp.concatenate([before, own, after], axis=0)
    near, w_in, w_out, noise_gain, step_index, station_rows, station_cols = (
        lax.optimization_barrier(
            (near, w_in, w_out, noise_gain, step_index, station_rows, station_cols)
        )
    )
    far_before = passed(near, 3)
    far_after = passed(near, -3)

    noise_alpha, noise_sigma, obs_kappa = noise_level(step_index)
    bias = jnp.broadcast_to((noise_sigma * noise_gain)[:, None], (HID, WIDTH))
    states = place + jnp.arange(-REACH, REACH + 1)
    inside = ((states >= 0) & (states < count)).astype(F32)
    weights = matrices(w_in, w_mid, w_out, inside)
    ends = jnp.stack([place == 2, place == count - 3]).astype(F32)
    scalars = jnp.concatenate([jnp.stack([noise_alpha, noise_sigma, obs_kappa]), ends])
    stations = jnp.concatenate([station_rows, station_cols]).reshape(-1, WIDTH)

    posterior = score(
        scalars,
        (part * OWN - 3).reshape(1).astype(jnp.int32),
        stations,
        near,
        far_before,
        far_after,
        end,
        bias,
        *weights,
    )
    return posterior[None]


def solution(mesh):
    return jax.shard_map(
        on_device,
        mesh=mesh,
        in_specs=(
            P("tm", None, "rows", None),
            P("tm", None, None),
            P(),
            P(),
            P(),
            P(),
            P(),
            P(),
            P(),
        ),
        out_specs=P("tm", None, "rows", None),
        check_vma=False,
    )
```

time: 66.6 us -> 57.9 us (0.87)
  the two profiles are of different devices: /device:TPU:1 before, /device:TPU:46 now
where the time goes in v3:
time: 57.9 us; the launch traced here: 57.4 us
  starting transfers between devices  28.4 us (49%)
  Pallas kernels  13.5 us (23%)
  waiting for transfers between devices  9.41 us (16%)
  local copies, waits for them, and re-layouts  2.93 us (5%)
  other arithmetic  1.96 us (3%)
  between operations  1.16 us (2%)
    ppermute x4, starting transfers between devices, passed(): return lax.ppermute(value, 'tm', pairs)  14.7 us
    pallas_call x1, Pallas kernels, score(): pl.pallas_call(score_kernel, out_shape=jax.ShapeDtypeStruct((2, OWN, WIDT...  13.5 us
    ppermute x1, starting transfers between devices, on_device(): far = lax.ppermute(own_state, 'rows', [(1, 2), (2, 1), (3, 0), (0, 3)])  10.5 us
    ppermute x4, waiting for transfers between devices, passed(): return lax.ppermute(value, 'tm', pairs)  9.41 us
    ppermute x1, starting transfers between devices, on_device(): near = lax.ppermute(own_state, 'rows', [(0, 1), (1, 0), (2, 3), (3, 2)])  2.59 us
    unnamed x16, local copies, waits for them, and re-layouts  1.54 us
  transfers between devices with their start and end apart: 7, of which 2 were waited for; matrix products, arithmetic and copies ran while one was open for 6% of the time, Pallas kernels for 0%

profile of v3, /device:TPU:46, one launch (start us, length us, event | category | flops | bytes accessed | tf_op | source)
XLA Modules:
  0.0 57.4 jit_solution(8214761417750810268)
XLA Ops:
  0.0 10.5 %collective-permute-start = (bf16[2,16,128]{2,1,0:T(8,128)(2,1)}, bf16[2,16,128]{2,1,0:T(8,128)(2,1)S(1)}, u32[]{:S(2)}, u32[]{:S(2)}) collective-permute-start(bf16[2,16,128]{2,1,0:T(8,128)(2,1)} %bitcast.53), channel_id=1, source_target_pairs={{1,2},{2,1},{3,0},{0,3},{5,6},{6,5},{7,4},{4,7},{9,10},{10,9},{11,... | collective-permute-start | bytes 24584 | tf_op jit(solution)/shard_map/ppermute | solution.py:389
  10.5 2.6 %collective-permute-start.1 = (bf16[2,16,128]{2,1,0:T(8,128)(2,1)}, bf16[2,16,128]{2,1,0:T(8,128)(2,1)S(1)}, u32[]{:S(2)}, u32[]{:S(2)}) collective-permute-start(bf16[2,16,128]{2,1,0:T(8,128)(2,1)} %bitcast.54), channel_id=1, source_target_pairs={{0,1},{1,0},{2,3},{3,2},{4,5},{5,4},{6,7},{7,6},{8,9},{9,8},{10,11... | collective-permute-start | bytes 24584 | tf_op jit(solution)/shard_map/ppermute | solution.py:390
  13.1 0.7 %fusion.6 = (bf16[2,1024]{1,0:T(2,128)(2,1)S(1)}, bf16[2,1024]{1,0:T(2,128)(2,1)S(1)}) fusion(f32[1,2,1024]{2,1,0:T(2,128)} %param.10), kind=kLoop, calls=%fused_computation.27 | loop fusion | flops 8192 | bytes 16384 | tf_op jit(solution)/shard_map/convert_element_type | solution.py:392
  13.8 0.7 %pad_maximum_fusion.3 = bf16[64,128]{1,0:T(8,128)(2,1)S(1)} fusion(bf16[32,128]{1,0:T(8,128)(2,1)} %bitcast.55, bf16[32,128]{1,0:T(8,128)(2,1)S(1)} %reshape.68), kind=kLoop, calls=%fused_computation.21 | loop fusion | flops 32768 | bytes 32768 | tf_op jit(solution)/shard_map/concatenate | solution.py:394
  14.6 0.1 add_convert_fusion
  15.5 2.6 %collective-permute-start.2 = (bf16[96,128]{1,0:T(8,128)(2,1)S(1)}, bf16[96,128]{1,0:T(8,128)(2,1)S(1)}, u32[]{:S(2)}, u32[]{:S(2)}) collective-permute-start(bf16[96,128]{1,0:T(8,128)(2,1)S(1)} %pad_maximum_fusion.2), channel_id=1, source_target_pairs={{0,4},{4,8},{8,12},{12,16},{16,20},{20,24},{24,28},{28,32},{32,36}... | collective-permute-start | bytes 73736 | tf_op jit(solution)/shard_map/ppermute | solution.py:403
  18.1 3.3 %collective-permute-start.3 = (bf16[96,128]{1,0:T(8,128)(2,1)S(1)}, bf16[96,128]{1,0:T(8,128)(2,1)S(1)}, u32[]{:S(2)}, u32[]{:S(2)}) collective-permute-start(bf16[96,128]{1,0:T(8,128)(2,1)S(1)} %pad_maximum_fusion.2), channel_id=1, source_target_pairs={{4,0},{8,4},{12,8},{16,12},{20,16},{24,20},{28,24},{32,28},{36,32}... | collective-permute-start | bytes 73736 | tf_op jit(solution)/shard_map/ppermute | solution.py:403
  21.4 0.1 pad_maximum_fusion.7.scalars_ref
  21.5 0.7 %collective-permute-start.6 = (bf16[96,128]{1,0:T(8,128)(2,1)S(1)}, bf16[96,128]{1,0:T(8,128)(2,1)S(1)}, u32[]{:S(2)}, u32[]{:S(2)}) collective-permute-start(bf16[96,128]{1,0:T(8,128)(2,1)S(1)} %pad_maximum_fusion.2), channel_id=1, source_target_pairs={{0,8},{508,500},{1,9},{509,501},{2,10},{510,502},{3,11},{511,503}} | collective-permute-start | bytes 73736 | tf_op jit(solution)/shard_map/ppermute | solution.py:407
  22.1 0.2 reshape.73
  22.4 0.2 copy.29
  22.5 0.2 copy.21
  22.7 0.2 copy.32.w_mid_ref
  22.9 0.9 %collective-permute-done.3 = bf16[96,128]{1,0:T(8,128)(2,1)S(1)} collective-permute-done((bf16[96,128]{1,0:T(8,128)(2,1)S(1)}, bf16[96,128]{1,0:T(8,128)(2,1)S(1)}, u32[]{:S(2)}, u32[]{:S(2)}) %collective-permute-start.3) | collective-permute-done | bytes 24608 | tf_op jit(solution)/shard_map/ppermute | solution.py:403
  24.0 6.7 %collective-permute-start.4 = (bf16[288,128]{1,0:T(8,128)(2,1)S(1)}, bf16[288,128]{1,0:T(8,128)(2,1)S(1)}, u32[]{:S(2)}, u32[]{:S(2)}) collective-permute-start(bf16[288,128]{1,0:T(8,128)(2,1)S(1)} %pad_maximum_fusion.1.near_ref), channel_id=1, source_target_pairs={{0,12},{4,16},{8,20},{12,24},{16,28},{20,32},{24,36},{28,40},{32,4... | collective-permute-start | bytes 221192 | tf_op jit(solution)/shard_map/ppermute | solution.py:403
  30.7 2.1 %collective-permute-start.5 = (bf16[288,128]{1,0:T(8,128)(2,1)S(1)}, bf16[288,128]{1,0:T(8,128)(2,1)S(1)}, u32[]{:S(2)}, u32[]{:S(2)}) collective-permute-start(bf16[288,128]{1,0:T(8,128)(2,1)S(1)} %pad_maximum_fusion.1.near_ref), channel_id=1, source_target_pairs={{12,0},{16,4},{20,8},{24,12},{28,16},{32,20},{36,24},{40,28},{44,3... | collective-permute-start | bytes 221192 | tf_op jit(solution)/shard_map/ppermute | solution.py:403
  32.9 0.1 copy.24
  33.0 0.1 pad_dynamic-update-slice_fusion.3
  33.1 0.1 pad_dynamic-update-slice_fusion.2
  33.2 0.1 pad_dynamic-update-slice_fusion.1
  33.3 0.1 pad_dynamic-update-slice_fusion.w_out_adj_ref
  33.4 0.1 pad_maximum_fusion.w_back_ref
  33.5 0.1 copy.18
  33.6 0.1 fusion.5.w_in_ref
  33.8 0.1 multiply_bitcast_fusion
  33.8 0.1 reshape.81
  34.0 0.6 %copy-done.5 = f32[96]{0:T(128)S(1)} copy-done((f32[96]{0:T(128)S(1)}, f32[96]{0:T(128)}, u32[]{:S(2)}) %copy-start.5) | copy-done | bytes 408
  34.7 0.1 pad_maximum_fusion.4.w_out_ref
  34.7 0.6 %copy-done.3 = s32[1024]{0:T(1024)S(1)} copy-done((s32[1024]{0:T(1024)S(1)}, s32[1024]{0:T(1024)}, u32[]{:S(2)}) %copy-start.3) | copy-done | bytes 4120
  35.3 8.5 %collective-permute-done.5.far_after_ref = bf16[288,128]{1,0:T(8,128)(2,1)S(1)} collective-permute-done((bf16[288,128]{1,0:T(8,128)(2,1)S(1)}, bf16[288,128]{1,0:T(8,128)(2,1)S(1)}, u32[]{:S(2)}, u32[]{:S(2)}) %collective-permute-start.5) | collective-permute-done | bytes 73760 | tf_op jit(solution)/shard_map/ppermute | solution.py:403
  43.8 0.1 broadcast_in_dim.4.bias_ref
  43.9 13.5 %score.1 = f32[2,16,128]{2,1,0:T(8,128)} custom-call(f32[5]{0:T(128)S(1)} %pad_maximum_fusion.7.scalars_ref, s32[1]{0:T(128)} %bitcast.10.first_ref, s32[16,128]{1,0:T(8,128)S(1)} %pad_add_fusion.stations_ref, bf16[288,128]{1,0:T(8,128)(2,1)S(1)} %pad_maximum_fusion.1.near_ref, bf16[288,128]{1,0:T(8,128)(2,1)S(1)} %collective-permute-done.4.far_before_ref, ...), custom_call_target="tpu_custom_call" | custom-call | flops 5000000000 | bytes 1000000 | tf_op jit(solution)/shard_map/score/pallas_call | solution.py:303
  (36 shorter events, 0.4 us)
Async XLA Ops:
  0.0 22.1 %copy-start = (bf16[3,3,9216]{2,1,0:T(4,128)(2,1)S(1)}, bf16[3,3,9216]{2,1,0:T(4,128)(2,1)}, u32[]{:S(2)}) copy-start(bf16[3,3,9216]{2,1,0:T(4,128)(2,1)} %param.15) | copy-start | bytes 497668
  0.0 15.5 %collective-permute-start = (bf16[2,16,128]{2,1,0:T(8,128)(2,1)}, bf16[2,16,128]{2,1,0:T(8,128)(2,1)S(1)}, u32[]{:S(2)}, u32[]{:S(2)}) collective-permute-start(bf16[2,16,128]{2,1,0:T(8,128)(2,1)} %bitcast.53), channel_id=1, source_target_pairs={{1,2},{2,1},{3,0},{0,3},{5,6},{6,5},{7,4},{4,7},{9,10},{10,9},{11,... | collective-permute-start | bytes 24584 | tf_op jit(solution)/shard_map/ppermute | solution.py:389
  10.5 5.0 %collective-permute-start.1 = (bf16[2,16,128]{2,1,0:T(8,128)(2,1)}, bf16[2,16,128]{2,1,0:T(8,128)(2,1)S(1)}, u32[]{:S(2)}, u32[]{:S(2)}) collective-permute-start(bf16[2,16,128]{2,1,0:T(8,128)(2,1)} %bitcast.54), channel_id=1, source_target_pairs={{0,1},{1,0},{2,3},{3,2},{4,5},{5,4},{6,7},{7,6},{8,9},{9,8},{10,11... | collective-permute-start | bytes 24584 | tf_op jit(solution)/shard_map/ppermute | solution.py:390
  15.5 7.4 %collective-permute-start.2 = (bf16[96,128]{1,0:T(8,128)(2,1)S(1)}, bf16[96,128]{1,0:T(8,128)(2,1)S(1)}, u32[]{:S(2)}, u32[]{:S(2)}) collective-permute-start(bf16[96,128]{1,0:T(8,128)(2,1)S(1)} %pad_maximum_fusion.2), channel_id=1, source_target_pairs={{0,4},{4,8},{8,12},{12,16},{16,20},{20,24},{24,28},{28,32},{32,36}... | collective-permute-start | bytes 73736 | tf_op jit(solution)/shard_map/ppermute | solution.py:403
  18.1 5.7 %collective-permute-start.3 = (bf16[96,128]{1,0:T(8,128)(2,1)S(1)}, bf16[96,128]{1,0:T(8,128)(2,1)S(1)}, u32[]{:S(2)}, u32[]{:S(2)}) collective-permute-start(bf16[96,128]{1,0:T(8,128)(2,1)S(1)} %pad_maximum_fusion.2), channel_id=1, source_target_pairs={{4,0},{8,4},{12,8},{16,12},{20,16},{24,20},{28,24},{32,28},{36,32}... | collective-permute-start | bytes 73736 | tf_op jit(solution)/shard_map/ppermute | solution.py:403
  21.5 13.9 %collective-permute-start.6 = (bf16[96,128]{1,0:T(8,128)(2,1)S(1)}, bf16[96,128]{1,0:T(8,128)(2,1)S(1)}, u32[]{:S(2)}, u32[]{:S(2)}) collective-permute-start(bf16[96,128]{1,0:T(8,128)(2,1)S(1)} %pad_maximum_fusion.2), channel_id=1, source_target_pairs={{0,8},{508,500},{1,9},{509,501},{2,10},{510,502},{3,11},{511,503}} | collective-permute-start | bytes 73736 | tf_op jit(solution)/shard_map/ppermute | solution.py:407
  22.9 1.0 %copy-start.1 = (bf16[96,10,3,3]{0,3,2,1:T(4,128)(2,1)S(1)}, bf16[96,10,3,3]{0,3,2,1:T(4,128)(2,1)}, u32[]{:S(2)}) copy-start(bf16[96,10,3,3]{0,3,2,1:T(4,128)(2,1)} %param.14) | copy-start | bytes 51844
  23.9 8.9 %copy-start.2 = (bf16[2,96,3,3]{1,0,3,2:T(2,128)(2,1)S(1)}, bf16[2,96,3,3]{1,0,3,2:T(2,128)(2,1)}, u32[]{:S(2)}) copy-start(bf16[2,96,3,3]{1,0,3,2:T(2,128)(2,1)} %param.16) | copy-start | bytes 10372
  24.0 11.4 %collective-permute-start.4 = (bf16[288,128]{1,0:T(8,128)(2,1)S(1)}, bf16[288,128]{1,0:T(8,128)(2,1)S(1)}, u32[]{:S(2)}, u32[]{:S(2)}) collective-permute-start(bf16[288,128]{1,0:T(8,128)(2,1)S(1)} %pad_maximum_fusion.1.near_ref), channel_id=1, source_target_pairs={{0,12},{4,16},{8,20},{12,24},{16,28},{20,32},{24,36},{28,40},{32,4... | collective-permute-start | bytes 221192 | tf_op jit(solution)/shard_map/ppermute | solution.py:403
  30.7 13.1 %collective-permute-start.5 = (bf16[288,128]{1,0:T(8,128)(2,1)S(1)}, bf16[288,128]{1,0:T(8,128)(2,1)S(1)}, u32[]{:S(2)}, u32[]{:S(2)}) collective-permute-start(bf16[288,128]{1,0:T(8,128)(2,1)S(1)} %pad_maximum_fusion.1.near_ref), channel_id=1, source_target_pairs={{12,0},{16,4},{20,8},{24,12},{28,16},{32,20},{36,24},{40,28},{44,3... | collective-permute-start | bytes 221192 | tf_op jit(solution)/shard_map/ppermute | solution.py:403
  34.0 0.7 %copy-start.5 = (f32[96]{0:T(128)S(1)}, f32[96]{0:T(128)}, u32[]{:S(2)}) copy-start(f32[96]{0:T(128)} %param.17) | copy-start | bytes 1156
  34.6 0.7 %copy-start.3 = (s32[1024]{0:T(1024)S(1)}, s32[1024]{0:T(1024)}, u32[]{:S(2)}) copy-start(s32[1024]{0:T(1024)} %param.12) | copy-start | bytes 12292
  34.6 0.7 %copy-start.4 = (s32[1024]{0:T(1024)S(1)}, s32[1024]{0:T(1024)}, u32[]{:S(2)}) copy-start(s32[1024]{0:T(1024)} %param.11) | copy-start | bytes 12292

commit v4 on v3

--- a/solution.py
+++ b/solution.py
@@ -20,7 +20,6 @@
 SEEN = 4 * STATIONS // WIDTH
 ONE = BLOCK + SEEN
 THREE = 3 * ONE
-ORDER = tuple((step, at - step) for at in range(WINDOWS + 5) for step in range(5) if 0 <= at - step < WINDOWS)
 F32 = jnp.float32
 BF16 = jnp.bfloat16
 
@@ -110,12 +109,14 @@
 
 
 def score_kernel(
+    chosen,
     scalars_ref,
     first_ref,
     stations_ref,
     near_ref,
     far_before_ref,
     far_after_ref,
+    earlier_ref,
     end_ref,
     bias_ref,
     w_in_ref,
@@ -166,7 +167,8 @@
 
     at_low, at_high = scalars_ref[3], scalars_ref[4]
     end = rows_of(end_ref, SEEN)
-    for s in range(4 * REACH + 1):
+    low = chosen[0]
+    for s in range(low, chosen[-1] + 2 * REACH + 1):
         ref = (far_before_ref, near_ref, far_after_ref)[s // 3]
         fields = rows_of(ref, ONE * (s % 3) + SEEN)
         for f in range(2):
@@ -176,24 +178,26 @@
             if s == 3 * REACH:
                 field = field + at_high * end[f]
             for b in range(3):
-                moved[b, 2 * s + f, :, :] = rolled(field, b - 1)
-
-    seen = [
-        ref[pl.ds(ONE * k, SEEN), :].astype(F32)
-        for ref, k in (
-            (far_before_ref, 2),
-            (near_ref, 0),
-            (near_ref, 1),
-            (near_ref, 2),
-            (far_after_ref, 0),
-        )
-    ]
-    end_seen = end_ref[pl.ds(0, SEEN), :].astype(F32)
-    seen[0] = seen[0] + at_low * end_seen
-    seen[-1] = seen[-1] + at_high * end_seen
+                moved[b, 2 * (s - low) + f, :, :] = rolled(field, b - 1)
+
+    places = (
+        (far_before_ref, 2),
+        (near_ref, 0),
+        (near_ref, 1),
+        (near_ref, 2),
+        (far_after_ref, 0),
+    )
+    seen = []
+    for k in chosen:
+        ref, packet = places[k]
+        values = ref[pl.ds(ONE * packet, SEEN), :].astype(F32)
+        at_end = {0: at_low, WINDOWS - 1: at_high}.get(k)
+        if at_end is not None:
+            values = values + at_end * end_ref[pl.ds(0, SEEN), :].astype(F32)
+        seen.append(values)
     *totals, stations = station_sums(first_ref[0], stations_ref, seen)
-    for k in range(WINDOWS):
-        sums[k, :, :] = totals[k]
+    for w in range(len(chosen)):
+        sums[w, :, :] = totals[w]
     count[...] = stations
 
     def first_layer(w):
@@ -214,24 +218,20 @@
                 slope_one[w, pl.ds(HID * (3 * k + j), HID), :] = slope[:, k * WIDTH : (k + 1) * WIDTH]
 
     def second_layer(w):
-        values = dot(w_mid_ref[...], side_by_side(hidden.at[w], 0, 3 * HID, 9 * HID, 24))
-        gate = logistic(values)
-        result = values * gate
-        slope = gate + result * (1.0 - gate)
-        residual = side_by_side(hidden.at[w], 4 * HID, 3 * HID, HID, 24)
-        high = (residual.astype(F32) + result).astype(BF16)
-        for k in range(24):
-            slope_two[w, pl.ds(HID * k, HID), :] = slope[:, k * WIDTH : (k + 1) * WIDTH]
-        pairs = jnp.concatenate(
-            [
-                jnp.concatenate(
-                    [high[:, (2 * k + j) * WIDTH : (2 * k + j + 1) * WIDTH] for j in range(2)],
-                    axis=0,
-                )
-                for k in range(12)
-            ],
-            axis=1,
-        )
+        values = dot(w_mid_ref[...], side_by_side(hidden.at[w], 0, 6 * HID, 12 * HID, 12))
+        pairs = []
+        for j in range(2):
+            part = values[HID * j : HID * (j + 1)]
+            gate = logistic(part)
+            result = part * gate
+            slope = gate + result * (1.0 - gate)
+            residual = side_by_side(hidden.at[w], (4 + 3 * j) * HID, 6 * HID, HID, 12)
+            pairs.append((residual.astype(F32) + result).astype(BF16))
+            for k in range(12):
+                slope_two[w, pl.ds(HID * (2 * k + j), HID), :] = slope[
+                    :, k * WIDTH : (k + 1) * WIDTH
+                ]
+        pairs = jnp.concatenate(pairs, axis=0)
         fold = folded(dot(w_out_ref[...], pairs))
         for k in range(12):
             folds[w, pl.ds(8 * k, 8), :] = fold[:, k * WIDTH : (k + 1) * WIDTH]
@@ -252,7 +252,7 @@
                 for b in range(3):
                     pull_slabs[w, pl.ds(16 * j + 2 * b + f, half, stride=32), :] = rolled(pull, b - 1)
 
-                if w == REACH:
+                if chosen[w] == REACH:
                     kept[f, pl.ds(j, half, stride=2), :] = noise_pred
                     kept[2 + f, pl.ds(j, half, stride=2), :] = pull
 
@@ -273,17 +273,25 @@
         slope = side_by_side(slope_one.at[w], 4 * HID, HID, HID, 18)
         low = (dot(w_back_ref[...], operand) * slope).astype(BF16)
         for k in range(18):
-            at = HID * (WINDOWS * k + w)
+            at = HID * (len(chosen) * k + w)
             slopes[pl.ds(at, HID), :] = low[:, k * WIDTH : (k + 1) * WIDTH]
 
     passes = (first_layer, second_layer, find_pull, second_back, first_back)
-    for step, w in ORDER:
-        passes[step](w)
-
-    stacked = side_by_side(slopes, 0, WINDOWS * HID, WINDOWS * HID, 18)
-    fold = folded(dot(w_in_adj_ref[...], stacked))
+    for at in range(len(chosen) + len(passes)):
+        for step, run in enumerate(passes):
+            if 0 <= at - step < len(chosen):
+                run(at - step)
+
+    width = len(chosen) * HID
+    fold = folded(dot(w_in_adj_ref[...], side_by_side(slopes, 0, width, width, 18)))
+    if REACH not in chosen:
+        for k in range(18):
+            out_ref[pl.ds(8 * k, 8), :] = fold[:, k * WIDTH : (k + 1) * WIDTH]
+        return
     for k in range(18):
-        grads[pl.ds(8 * k, 8), :] = fold[:, k * WIDTH : (k + 1) * WIDTH]
+        grads[pl.ds(8 * k, 8), :] = (
+            fold[:, k * WIDTH : (k + 1) * WIDTH] + earlier_ref[pl.ds(8 * k, 8), :]
+        )
     for f in range(2):
         summed = (
             grads[pl.ds(f, OWN, stride=8), :]
@@ -297,37 +305,45 @@
         ) * over_alpha
 
 
-def score(*operands):
+def score(chosen, *operands):
     vmem = pl.BlockSpec(memory_space=pltpu.VMEM)
     smem = pl.BlockSpec(memory_space=pltpu.SMEM)
+    last = REACH in chosen
+    windows = len(chosen)
+
+    def kernel(*refs):
+        refs = list(refs)
+        if not last:
+            refs.insert(5, None)
+            refs.insert(6, None)
+        score_kernel(chosen, *refs)
+
     return pl.pallas_call(
-        score_kernel,
-        out_shape=jax.ShapeDtypeStruct((2, OWN, WIDTH), F32),
-        in_specs=[smem, smem] + [vmem] * 12,
+        kernel,
+        out_shape=jax.ShapeDtypeStruct((2, OWN, WIDTH) if last else (18 * 8, WIDTH), F32),
+        in_specs=[smem, smem] + [vmem] * (len(operands) - 2),
         out_specs=vmem,
         scratch_shapes=[
-            pltpu.VMEM((3, 18, 32, WIDTH), F32),
-            pltpu.VMEM((WINDOWS, 2 * SPAN, WIDTH), F32),
+            pltpu.VMEM((3, 2 * (windows + 2 * REACH), 32, WIDTH), F32),
+            pltpu.VMEM((windows, 2 * SPAN, WIDTH), F32),
             pltpu.VMEM((SPAN, WIDTH), F32),
-            pltpu.VMEM((WINDOWS, 32 * 48, WIDTH), F32),
-            pltpu.VMEM((WINDOWS, 27 * 3 * HID, WIDTH), BF16),
-            pltpu.VMEM((WINDOWS, 27 * HID, WIDTH), F32),
-            pltpu.VMEM((WINDOWS, 24 * HID, WIDTH), F32),
-            pltpu.VMEM((WINDOWS, 16 * 8, WIDTH), F32),
-            pltpu.VMEM((WINDOWS, SPAN * 16, WIDTH), F32),
-            pltpu.VMEM((WINDOWS, 20 * 3 * HID, WIDTH), BF16),
-            pltpu.VMEM((18 * WINDOWS * HID, WIDTH), BF16),
+            pltpu.VMEM((windows, 32 * 48, WIDTH), F32),
+            pltpu.VMEM((windows, 27 * 3 * HID, WIDTH), BF16),
+            pltpu.VMEM((windows, 27 * HID, WIDTH), F32),
+            pltpu.VMEM((windows, 24 * HID, WIDTH), F32),
+            pltpu.VMEM((windows, 16 * 8, WIDTH), F32),
+            pltpu.VMEM((windows, SPAN * 16, WIDTH), F32),
+            pltpu.VMEM((windows, 20 * 3 * HID, WIDTH), BF16),
+            pltpu.VMEM((18 * windows * HID, WIDTH), BF16),
             pltpu.VMEM((18 * 8, WIDTH), F32),
             pltpu.VMEM((4, SPAN, WIDTH), F32),
         ],
-        compiler_params=pltpu.CompilerParams(vmem_limit_bytes=50 * 1024 * 1024),
+        compiler_params=pltpu.CompilerParams(vmem_limit_bytes=40 * 1024 * 1024),
         cost_estimate=pl.CostEstimate(
-            flops=5_000_000_000, bytes_accessed=1_000_000, transcendentals=1_000_000
+            flops=1_000_000_000 * windows, bytes_accessed=1_000_000, transcendentals=200_000 * windows
         ),
-        name="score",
-    )(
-        *operands
-    )
+        name="score" if last else "earlier",
+    )(*operands)
 
 
 def padded(array, axis, size):
@@ -370,7 +386,7 @@
     first_adj = padded(first_adj.reshape(3, 6, WINDOWS * HID), 1, 8).reshape(24, WINDOWS * HID)
     return (
         stepped(first, 48, 3, 240),
-        mid,
+        stepped(mid, 3 * HID, 2, 12 * HID),
         last,
         stepped(last_adj, 16, 5, 112),
         jnp.concatenate([mid_adj, last_adj], axis=1),
@@ -424,16 +440,25 @@
     scalars = jnp.concatenate([jnp.stack([noise_alpha, noise_sigma, obs_kappa]), ends])
     stations = jnp.concatenate([station_rows, station_cols]).reshape(-1, WIDTH)
 
+    first, mid, last, last_adj, back, first_adj = weights
+    start = (part * OWN - 3).reshape(1).astype(jnp.int32)
+    begun = REACH * HID
+    small = (bias, first, mid, last, last_adj, back)
+    earlier = score(
+        (0, 1), scalars, start, stations, near, far_before, end, *small, first_adj[:, :begun]
+    )
     posterior = score(
+        (2, 3, 4),
         scalars,
-        (part * OWN - 3).reshape(1).astype(jnp.int32),
+        start,
         stations,
         near,
         far_before,
         far_after,
+        earlier,
         end,
-        bias,
-        *weights,
+        *small,
+        first_adj[:, begun:],
     )
     return posterior[None]
 

time: 57.9 us -> 55.5 us (0.959)
  the two profiles are of different devices: /device:TPU:46 before, /device:TPU:64 now
where the time goes in v4:
time: 55.5 us; the launch traced here: 55.1 us
  starting transfers between devices  34.7 us (63%)
  Pallas kernels  14 us (25%)
  local copies, waits for them, and re-layouts  3.72 us (7%)
  other arithmetic  1.38 us (2%)
  between operations  1.18 us (2%)
    ppermute x4, starting transfers between devices, passed(): return lax.ppermute(value, 'tm', pairs)  21.9 us
    pallas_call x2, Pallas kernels, score(): pl.pallas_call(kernel, out_shape=jax.ShapeDtypeStruct((2, OWN, WIDTH) if...  14 us
    ppermute x1, starting transfers between devices, on_device(): far = lax.ppermute(own_state, 'rows', [(1, 2), (2, 1), (3, 0), (0, 3)])  9.58 us
    ppermute x1, starting transfers between devices, on_device(): near = lax.ppermute(own_state, 'rows', [(0, 1), (1, 0), (2, 3), (3, 2)])  2.59 us
    unnamed x18, local copies, waits for them, and re-layouts  2.25 us
  transfers between devices with their start and end apart: 7, of which 0 were waited for; matrix products, arithmetic and copies ran while one was open for 6% of the time, Pallas kernels for 10%

profile of v4, /device:TPU:64, one launch (start us, length us, event | category | flops | bytes accessed | tf_op | source)
XLA Modules:
  0.0 55.1 jit_solution(1197719163461594300)
XLA Ops:
  0.0 9.6 %collective-permute-start = (bf16[2,16,128]{2,1,0:T(8,128)(2,1)}, bf16[2,16,128]{2,1,0:T(8,128)(2,1)S(1)}, u32[]{:S(2)}, u32[]{:S(2)}) collective-permute-start(bf16[2,16,128]{2,1,0:T(8,128)(2,1)} %bitcast.53), channel_id=1, source_target_pairs={{1,2},{2,1},{3,0},{0,3},{5,6},{6,5},{7,4},{4,7},{9,10},{10,9},{11,... | collective-permute-start | bytes 24584 | tf_op jit(solution)/shard_map/ppermute | solution.py:405
  9.6 2.6 %collective-permute-start.1 = (bf16[2,16,128]{2,1,0:T(8,128)(2,1)}, bf16[2,16,128]{2,1,0:T(8,128)(2,1)S(1)}, u32[]{:S(2)}, u32[]{:S(2)}) collective-permute-start(bf16[2,16,128]{2,1,0:T(8,128)(2,1)} %bitcast.54), channel_id=1, source_target_pairs={{0,1},{1,0},{2,3},{3,2},{4,5},{5,4},{6,7},{7,6},{8,9},{9,8},{10,11... | collective-permute-start | bytes 24584 | tf_op jit(solution)/shard_map/ppermute | solution.py:406
  13.1 0.7 %pad_maximum_fusion.3 = bf16[64,128]{1,0:T(8,128)(2,1)S(1)} fusion(bf16[32,128]{1,0:T(8,128)(2,1)} %bitcast.55, bf16[32,128]{1,0:T(8,128)(2,1)S(1)} %reshape.68), kind=kLoop, calls=%fused_computation.26 | loop fusion | flops 32768 | bytes 32768 | tf_op jit(solution)/shard_map/concatenate | solution.py:410
  13.8 0.1 add_convert_fusion
  13.9 0.1 pad_maximum_fusion.7.refs_0_
  14.0 3.5 %collective-permute-start.2 = (bf16[96,128]{1,0:T(8,128)(2,1)S(1)}, bf16[96,128]{1,0:T(8,128)(2,1)S(1)}, u32[]{:S(2)}, u32[]{:S(2)}) collective-permute-start(bf16[96,128]{1,0:T(8,128)(2,1)S(1)} %pad_maximum_fusion.2), channel_id=1, source_target_pairs={{0,4},{4,8},{8,12},{12,16},{16,20},{20,24},{24,28},{28,32},{32,36}... | collective-permute-start | bytes 73736 | tf_op jit(solution)/shard_map/ppermute | solution.py:419
  17.5 6.6 %collective-permute-start.3 = (bf16[96,128]{1,0:T(8,128)(2,1)S(1)}, bf16[96,128]{1,0:T(8,128)(2,1)S(1)}, u32[]{:S(2)}, u32[]{:S(2)}) collective-permute-start(bf16[96,128]{1,0:T(8,128)(2,1)S(1)} %pad_maximum_fusion.2), channel_id=1, source_target_pairs={{4,0},{8,4},{12,8},{16,12},{20,16},{24,20},{28,24},{32,28},{36,32}... | collective-permute-start | bytes 73736 | tf_op jit(solution)/shard_map/ppermute | solution.py:419
  24.1 0.7 %collective-permute-start.6 = (bf16[96,128]{1,0:T(8,128)(2,1)S(1)}, bf16[96,128]{1,0:T(8,128)(2,1)S(1)}, u32[]{:S(2)}, u32[]{:S(2)}) collective-permute-start(bf16[96,128]{1,0:T(8,128)(2,1)S(1)} %pad_maximum_fusion.2), channel_id=1, source_target_pairs={{0,8},{508,500},{1,9},{509,501},{2,10},{510,502},{3,11},{511,503}} | collective-permute-start | bytes 73736 | tf_op jit(solution)/shard_map/ppermute | solution.py:423
  24.8 0.2 reshape.73
  25.0 0.2 copy.21
  25.2 0.2 copy.22
  25.3 0.1 fusion.2.refs_8_.refs_10_
  25.5 0.2 copy.31
  25.7 0.7 %copy-done.1 = bf16[96,10,3,3]{0,3,2,1:T(4,128)(2,1)S(1)} copy-done((bf16[96,10,3,3]{0,3,2,1:T(4,128)(2,1)S(1)}, bf16[96,10,3,3]{0,3,2,1:T(4,128)(2,1)}, u32[]{:S(2)}) %copy-start.1) | copy-done | bytes 17304
  26.5 4.8 %collective-permute-start.4 = (bf16[288,128]{1,0:T(8,128)(2,1)S(1)}, bf16[288,128]{1,0:T(8,128)(2,1)S(1)}, u32[]{:S(2)}, u32[]{:S(2)}) collective-permute-start(bf16[288,128]{1,0:T(8,128)(2,1)S(1)} %pad_maximum_fusion.1.refs_3_), channel_id=1, source_target_pairs={{0,12},{4,16},{8,20},{12,24},{16,28},{20,32},{24,36},{28,40},{32,4... | collective-permute-start | bytes 221192 | tf_op jit(solution)/shard_map/ppermute | solution.py:419
  31.3 7.1 %collective-permute-start.5 = (bf16[288,128]{1,0:T(8,128)(2,1)S(1)}, bf16[288,128]{1,0:T(8,128)(2,1)S(1)}, u32[]{:S(2)}, u32[]{:S(2)}) collective-permute-start(bf16[288,128]{1,0:T(8,128)(2,1)S(1)} %pad_maximum_fusion.1.refs_3_), channel_id=1, source_target_pairs={{12,0},{16,4},{20,8},{24,12},{28,16},{32,20},{36,24},{40,28},{44,3... | collective-permute-start | bytes 221192 | tf_op jit(solution)/shard_map/ppermute | solution.py:419
  38.4 0.1 copy.26
  38.5 0.1 pad_dynamic-update-slice_fusion.3
  38.6 0.1 pad_dynamic-update-slice_fusion.2
  38.7 0.1 pad_dynamic-update-slice_fusion.1
  38.8 0.1 pad_dynamic-update-slice_fusion.refs_10_.refs_12_
  38.9 0.1 pad_maximum_fusion.refs_11_.refs_13_
  39.0 0.1 copy.18
  39.1 0.1 fusion.8.refs_7_.refs_9_
  39.3 0.1 multiply_bitcast_fusion
  39.4 0.1 reshape.81
  39.5 0.6 %copy-done.6 = f32[96]{0:T(128)S(1)} copy-done((f32[96]{0:T(128)S(1)}, f32[96]{0:T(128)}, u32[]{:S(2)}) %copy-start.6) | copy-done | bytes 408
  40.2 0.1 pad_maximum_fusion.4.refs_9_.refs_11_
  40.3 0.6 %copy-done.4 = s32[1024]{0:T(1024)S(1)} copy-done((s32[1024]{0:T(1024)S(1)}, s32[1024]{0:T(1024)}, u32[]{:S(2)}) %copy-start.4) | copy-done | bytes 4120
  40.9 0.1 slice.36.refs_14_
  41.0 5.5 %earlier.1.refs_6_ = f32[144,128]{1,0:T(8,128)S(1)} custom-call(f32[5]{0:T(128)S(1)} %pad_maximum_fusion.7.refs_0_, s32[1]{0:T(128)} %bitcast.10.refs_1_, s32[16,128]{1,0:T(8,128)S(1)} %pad_add_fusion.refs_2_, bf16[288,128]{1,0:T(8,128)(2,1)S(1)} %pad_maximum_fusion.1.refs_3_, bf16[288,128]{1,0:T(8,128)(2,1)S(1)} %collective-permute-done.4.refs_4_, ...), custom_call_target="tpu_custom_call" | custom-call | flops 2000000000 | bytes 1000000 | tf_op jit(solution)/shard_map/earlier/pallas_call | solution.py:321
  46.6 8.5 %score.1 = f32[2,16,128]{2,1,0:T(8,128)} custom-call(f32[5]{0:T(128)S(1)} %pad_maximum_fusion.7.refs_0_, s32[1]{0:T(128)} %bitcast.10.refs_1_, s32[16,128]{1,0:T(8,128)S(1)} %pad_add_fusion.refs_2_, bf16[288,128]{1,0:T(8,128)(2,1)S(1)} %pad_maximum_fusion.1.refs_3_, bf16[288,128]{1,0:T(8,128)(2,1)S(1)} %collective-permute-done.4.refs_4_, ...), custom_call_target="tpu_custom_call" | custom-call | flops 3000000000 | bytes 1000000 | tf_op jit(solution)/shard_map/score/pallas_call | solution.py:321
  (42 shorter events, 0.4 us)
Async XLA Ops:
  0.0 13.0 %copy-start.3 = (f32[1,2,1024]{2,1,0:T(2,128)S(1)}, f32[1,2,1024]{2,1,0:T(2,128)}, u32[]{:S(2)}) copy-start(f32[1,2,1024]{2,1,0:T(2,128)} %param.10) | copy-start | bytes 24580
  0.0 24.8 %copy-start = (bf16[3,3,9216]{2,1,0:T(4,128)(2,1)S(1)}, bf16[3,3,9216]{2,1,0:T(4,128)(2,1)}, u32[]{:S(2)}) copy-start(bf16[3,3,9216]{2,1,0:T(4,128)(2,1)} %param.15) | copy-start | bytes 497668
  0.0 14.0 %collective-permute-start = (bf16[2,16,128]{2,1,0:T(8,128)(2,1)}, bf16[2,16,128]{2,1,0:T(8,128)(2,1)S(1)}, u32[]{:S(2)}, u32[]{:S(2)}) collective-permute-start(bf16[2,16,128]{2,1,0:T(8,128)(2,1)} %bitcast.53), channel_id=1, source_target_pairs={{1,2},{2,1},{3,0},{0,3},{5,6},{6,5},{7,4},{4,7},{9,10},{10,9},{11,... | collective-permute-start | bytes 24584 | tf_op jit(solution)/shard_map/ppermute | solution.py:405
  9.6 4.4 %collective-permute-start.1 = (bf16[2,16,128]{2,1,0:T(8,128)(2,1)}, bf16[2,16,128]{2,1,0:T(8,128)(2,1)S(1)}, u32[]{:S(2)}, u32[]{:S(2)}) collective-permute-start(bf16[2,16,128]{2,1,0:T(8,128)(2,1)} %bitcast.54), channel_id=1, source_target_pairs={{0,1},{1,0},{2,3},{3,2},{4,5},{5,4},{6,7},{7,6},{8,9},{9,8},{10,11... | collective-permute-start | bytes 24584 | tf_op jit(solution)/shard_map/ppermute | solution.py:406
  14.0 11.6 %collective-permute-start.2 = (bf16[96,128]{1,0:T(8,128)(2,1)S(1)}, bf16[96,128]{1,0:T(8,128)(2,1)S(1)}, u32[]{:S(2)}, u32[]{:S(2)}) collective-permute-start(bf16[96,128]{1,0:T(8,128)(2,1)S(1)} %pad_maximum_fusion.2), channel_id=1, source_target_pairs={{0,4},{4,8},{8,12},{12,16},{16,20},{20,24},{24,28},{28,32},{32,36}... | collective-permute-start | bytes 73736 | tf_op jit(solution)/shard_map/ppermute | solution.py:419
  17.5 8.2 %collective-permute-start.3 = (bf16[96,128]{1,0:T(8,128)(2,1)S(1)}, bf16[96,128]{1,0:T(8,128)(2,1)S(1)}, u32[]{:S(2)}, u32[]{:S(2)}) collective-permute-start(bf16[96,128]{1,0:T(8,128)(2,1)S(1)} %pad_maximum_fusion.2), channel_id=1, source_target_pairs={{4,0},{8,4},{12,8},{16,12},{20,16},{24,20},{28,24},{32,28},{36,32}... | collective-permute-start | bytes 73736 | tf_op jit(solution)/shard_map/ppermute | solution.py:419
  24.1 16.9 %collective-permute-start.6 = (bf16[96,128]{1,0:T(8,128)(2,1)S(1)}, bf16[96,128]{1,0:T(8,128)(2,1)S(1)}, u32[]{:S(2)}, u32[]{:S(2)}) collective-permute-start(bf16[96,128]{1,0:T(8,128)(2,1)S(1)} %pad_maximum_fusion.2), channel_id=1, source_target_pairs={{0,8},{508,500},{1,9},{509,501},{2,10},{510,502},{3,11},{511,503}} | collective-permute-start | bytes 73736 | tf_op jit(solution)/shard_map/ppermute | solution.py:423
  25.6 0.8 %copy-start.1 = (bf16[96,10,3,3]{0,3,2,1:T(4,128)(2,1)S(1)}, bf16[96,10,3,3]{0,3,2,1:T(4,128)(2,1)}, u32[]{:S(2)}) copy-start(bf16[96,10,3,3]{0,3,2,1:T(4,128)(2,1)} %param.14) | copy-start | bytes 51844
  26.4 12.0 %copy-start.2 = (bf16[2,96,3,3]{1,0,3,2:T(2,128)(2,1)S(1)}, bf16[2,96,3,3]{1,0,3,2:T(2,128)(2,1)}, u32[]{:S(2)}) copy-start(bf16[2,96,3,3]{1,0,3,2:T(2,128)(2,1)} %param.16) | copy-start | bytes 10372
  26.5 14.5 %collective-permute-start.4 = (bf16[288,128]{1,0:T(8,128)(2,1)S(1)}, bf16[288,128]{1,0:T(8,128)(2,1)S(1)}, u32[]{:S(2)}, u32[]{:S(2)}) collective-permute-start(bf16[288,128]{1,0:T(8,128)(2,1)S(1)} %pad_maximum_fusion.1.refs_3_), channel_id=1, source_target_pairs={{0,12},{4,16},{8,20},{12,24},{16,28},{20,32},{24,36},{28,40},{32,4... | collective-permute-start | bytes 221192 | tf_op jit(solution)/shard_map/ppermute | solution.py:419
  31.3 15.3 %collective-permute-start.5 = (bf16[288,128]{1,0:T(8,128)(2,1)S(1)}, bf16[288,128]{1,0:T(8,128)(2,1)S(1)}, u32[]{:S(2)}, u32[]{:S(2)}) collective-permute-start(bf16[288,128]{1,0:T(8,128)(2,1)S(1)} %pad_maximum_fusion.1.refs_3_), channel_id=1, source_target_pairs={{12,0},{16,4},{20,8},{24,12},{28,16},{32,20},{36,24},{40,28},{44,3... | collective-permute-start | bytes 221192 | tf_op jit(solution)/shard_map/ppermute | solution.py:419
  39.5 0.7 %copy-start.6 = (f32[96]{0:T(128)S(1)}, f32[96]{0:T(128)}, u32[]{:S(2)}) copy-start(f32[96]{0:T(128)} %param.17) | copy-start | bytes 1156
  40.2 0.7 %copy-start.4 = (s32[1024]{0:T(1024)S(1)}, s32[1024]{0:T(1024)}, u32[]{:S(2)}) copy-start(s32[1024]{0:T(1024)} %param.12) | copy-start | bytes 12292
  40.2 0.7 %copy-start.5 = (s32[1024]{0:T(1024)S(1)}, s32[1024]{0:T(1024)}, u32[]{:S(2)}) copy-start(s32[1024]{0:T(1024)} %param.11) | copy-start | bytes 12292

commit v5 on v4

--- a/solution.py
+++ b/solution.py
@@ -20,6 +20,7 @@
 SEEN = 4 * STATIONS // WIDTH
 ONE = BLOCK + SEEN
 THREE = 3 * ONE
+LIMIT = 50
 F32 = jnp.float32
 BF16 = jnp.bfloat16
 
@@ -108,6 +109,82 @@
     return rolled(product[0:8], -1) + product[8:16] + rolled(product[16:24], 1)
 
 
+def arrange(
+    place,
+    states,
+    rows_ref,
+    cols_ref,
+    w_in_ref,
+    w_out_ref,
+    gain_ref,
+    mid_adj_ref,
+    stations_ref,
+    gains_ref,
+    first_ref,
+    last_ref,
+    last_adj_ref,
+    back_ref,
+    first_adj_ref,
+    first_adj_later_ref,
+    rows,
+):
+    def turned(start):
+        return jnp.transpose(rows[pl.ds(start, 256), :])
+
+    rows[...] = jnp.zeros_like(rows)
+
+    for channel in range(2 * WINDOWS):
+        for a in range(3):
+            taps = w_in_ref[channel, a].astype(F32)
+            for b in range(3):
+                at = 96 + 48 * a + 16 * b + channel
+                rows[at : at + 1, :HID] = taps[b : b + 1]
+    for j in range(3):
+        first_ref[HID * j : HID * (j + 1), :] = turned(96 - 48 * j)[:HID, :240].astype(BF16)
+
+    parts = []
+    for w in range(WINDOWS):
+        state = place + (w - REACH)
+        inside = jnp.where((state >= 0) & (state < states), 1.0, 0.0)
+        rows[0:24, :] = jnp.zeros((24, WIDTH), F32)
+        for f in range(2):
+            for a in range(3):
+                taps = w_in_ref[2 * (WINDOWS - 1 - w) + f, 2 - a].astype(F32)
+                for b in range(3):
+                    at = 8 * b + 2 * a + f
+                    rows[at : at + 1, :HID] = taps[2 - b : 3 - b]
+        parts.append(inside * rows[0:24, :HID])
+    first_adj_ref[...] = jnp.concatenate(parts[:REACH], axis=1).astype(BF16)
+    first_adj_later_ref[...] = jnp.concatenate(parts[REACH:], axis=1).astype(BF16)
+
+    taps = [[w_out_ref[a, b].astype(F32) for b in range(3)] for a in range(3)]
+    parts = []
+    for j in range(2):
+        rows[0:24, :] = jnp.zeros((24, WIDTH), F32)
+        for o in range(j, j + 3):
+            for b in range(3):
+                at = 8 * b + 2 * o
+                rows[at : at + 2, :HID] = taps[2 + j - o][b]
+        parts.append(rows[0:24, :HID])
+    last_ref[...] = jnp.concatenate(parts, axis=1).astype(BF16)
+
+    rows[...] = jnp.zeros_like(rows)
+    for a in range(3):
+        for b in range(3):
+            at = 64 + 16 * a + 2 * b
+            rows[at : at + 2, :HID] = taps[2 - a][2 - b]
+    for j in range(5):
+        last_adj_ref[HID * j : HID * (j + 1), :] = turned(64 - 16 * j)[:HID, :112].astype(BF16)
+
+    back_ref[...] = jnp.concatenate([mid_adj_ref[...], last_adj_ref[:HID, :48]], axis=1)
+
+    gain = jnp.broadcast_to(gain_ref[...], (WIDTH, HID))
+    gain = jnp.concatenate([gain, jnp.zeros((WIDTH, WIDTH - HID), F32)], axis=1)
+    gains_ref[...] = jnp.transpose(gain)[:HID]
+    stations_ref[:8, :] = rows_ref[...]
+    stations_ref[8:, :] = cols_ref[...]
+
+
 def score_kernel(
     chosen,
     scalars_ref,
@@ -118,7 +195,7 @@
     far_after_ref,
     earlier_ref,
     end_ref,
-    bias_ref,
+    gains_ref,
     w_in_ref,
     w_mid_ref,
     w_out_ref,
@@ -209,7 +286,7 @@
 
         values = dot(w_in_ref[...], side_by_side(blanket.at[w], 96, 144, 240, 9).astype(BF16))
         for j in range(3):
-            part = values[HID * j : HID * (j + 1)] + jnp.concatenate([bias_ref[...]] * 9, axis=1)
+            part = values[HID * j : HID * (j + 1)] + jnp.concatenate([noise_sigma * gains_ref[...]] * 9, axis=1)
             gate = logistic(part)
             result = part * gate
             slope = gate + result * (1.0 - gate)
@@ -305,51 +382,79 @@
         ) * over_alpha
 
 
-def score(chosen, *operands):
+def buffers(windows):
+    return [
+        pltpu.VMEM((3, 2 * (windows + 2 * REACH), 32, WIDTH), F32),
+        pltpu.VMEM((windows, 2 * SPAN, WIDTH), F32),
+        pltpu.VMEM((SPAN, WIDTH), F32),
+        pltpu.VMEM((windows, 32 * 48, WIDTH), F32),
+        pltpu.VMEM((windows, 27 * 3 * HID, WIDTH), BF16),
+        pltpu.VMEM((windows, 27 * HID, WIDTH), F32),
+        pltpu.VMEM((windows, 24 * HID, WIDTH), F32),
+        pltpu.VMEM((windows, 16 * 8, WIDTH), F32),
+        pltpu.VMEM((windows, SPAN * 16, WIDTH), F32),
+        pltpu.VMEM((windows, 20 * 3 * HID, WIDTH), BF16),
+        pltpu.VMEM((18 * windows * HID, WIDTH), BF16),
+        pltpu.VMEM((18 * 8, WIDTH), F32),
+        pltpu.VMEM((4, SPAN, WIDTH), F32),
+    ]
+
+
+def call(kernel, name, windows, out_shape, scratch, operands):
     vmem = pl.BlockSpec(memory_space=pltpu.VMEM)
     smem = pl.BlockSpec(memory_space=pltpu.SMEM)
-    last = REACH in chosen
-    windows = len(chosen)
-
-    def kernel(*refs):
-        refs = list(refs)
-        if not last:
-            refs.insert(5, None)
-            refs.insert(6, None)
-        score_kernel(chosen, *refs)
-
     return pl.pallas_call(
         kernel,
-        out_shape=jax.ShapeDtypeStruct((2, OWN, WIDTH) if last else (18 * 8, WIDTH), F32),
+        out_shape=out_shape,
         in_specs=[smem, smem] + [vmem] * (len(operands) - 2),
-        out_specs=vmem,
-        scratch_shapes=[
-            pltpu.VMEM((3, 2 * (windows + 2 * REACH), 32, WIDTH), F32),
-            pltpu.VMEM((windows, 2 * SPAN, WIDTH), F32),
-            pltpu.VMEM((SPAN, WIDTH), F32),
-            pltpu.VMEM((windows, 32 * 48, WIDTH), F32),
-            pltpu.VMEM((windows, 27 * 3 * HID, WIDTH), BF16),
-            pltpu.VMEM((windows, 27 * HID, WIDTH), F32),
-            pltpu.VMEM((windows, 24 * HID, WIDTH), F32),
-            pltpu.VMEM((windows, 16 * 8, WIDTH), F32),
-            pltpu.VMEM((windows, SPAN * 16, WIDTH), F32),
-            pltpu.VMEM((windows, 20 * 3 * HID, WIDTH), BF16),
-            pltpu.VMEM((18 * windows * HID, WIDTH), BF16),
-            pltpu.VMEM((18 * 8, WIDTH), F32),
-            pltpu.VMEM((4, SPAN, WIDTH), F32),
-        ],
-        compiler_params=pltpu.CompilerParams(vmem_limit_bytes=40 * 1024 * 1024),
+        out_specs=jax.tree.map(lambda _: vmem, out_shape),
+        scratch_shapes=scratch,
+        compiler_params=pltpu.CompilerParams(vmem_limit_bytes=LIMIT * 1024 * 1024),
         cost_estimate=pl.CostEstimate(
             flops=1_000_000_000 * windows, bytes_accessed=1_000_000, transcendentals=200_000 * windows
         ),
-        name="score" if last else "earlier",
+        name=name,
     )(*operands)
 
 
-def padded(array, axis, size):
-    pads = [(0, 0)] * array.ndim
-    pads[axis] = (0, size - array.shape[axis])
-    return jnp.pad(array, pads)
+def begin(states, scalars, start, rows, cols, near, far_before, end, w_in, w_out, gain, mid, mid_adj):
+    def kernel(
+        scalars_ref, first_ref, rows_ref, cols_ref, near_ref, far_before_ref, end_ref, w_in_ref, w_out_ref,
+        gain_ref, mid_ref, mid_adj_ref, out_ref, stations_ref, gains_ref, layer_ref, last_ref, last_adj_ref,
+        back_ref, adj_later_ref, adj_ref, rows_buffer, *scratch,
+    ):
+        arrange(
+            scalars_ref[5], states, rows_ref, cols_ref, w_in_ref, w_out_ref, gain_ref, mid_adj_ref, stations_ref,
+            gains_ref, layer_ref, last_ref, last_adj_ref, back_ref, adj_ref, adj_later_ref, rows_buffer,
+        )
+        score_kernel(
+            tuple(range(REACH)), scalars_ref, first_ref, stations_ref, near_ref, far_before_ref, None, None, end_ref,
+            gains_ref, layer_ref, mid_ref, last_ref, last_adj_ref, back_ref, adj_ref, out_ref, *scratch,
+        )
+
+    out_shape = (
+        jax.ShapeDtypeStruct((18 * 8, WIDTH), F32),
+        jax.ShapeDtypeStruct((2 * STATIONS // WIDTH, WIDTH), jnp.int32),
+        jax.ShapeDtypeStruct((HID, WIDTH), F32),
+        jax.ShapeDtypeStruct((3 * HID, 240), BF16),
+        jax.ShapeDtypeStruct((24, 2 * HID), BF16),
+        jax.ShapeDtypeStruct((5 * HID, 112), BF16),
+        jax.ShapeDtypeStruct((HID, 9 * HID + 48), BF16),
+        jax.ShapeDtypeStruct((24, (WINDOWS - REACH) * HID), BF16),
+    )
+    scratch = [pltpu.VMEM((24, REACH * HID), BF16), pltpu.VMEM((352, WIDTH), F32)] + buffers(REACH)
+    operands = (scalars, start, rows, cols, near, far_before, end, w_in, w_out, gain, mid, mid_adj)
+    return call(kernel, "begin", REACH, out_shape, scratch, operands)
+
+
+def finish(*operands):
+    chosen = tuple(range(REACH, WINDOWS))
+
+    def kernel(*refs):
+        score_kernel(chosen, *refs)
+
+    out_shape = jax.ShapeDtypeStruct((2, OWN, WIDTH), F32)
+    return call(kernel, "score", len(chosen), out_shape, buffers(len(chosen)), operands)
 
 
 def stepped(matrix, step, rows, depth):
@@ -360,37 +465,6 @@
             for k in range(rows)
         ],
         axis=0,
-    )
-
-
-def matrices(w_in, w_mid, w_out, inside):
-    taps = w_mid.reshape(9, HID, HID)
-    mid = jnp.transpose(taps, (1, 0, 2)).reshape(HID, 9 * HID)
-    mid_adj = jnp.transpose(taps[::-1], (2, 0, 1)).reshape(HID, 9 * HID)
-    first = padded(jnp.transpose(w_in, (0, 2, 3, 1)), 3, 16).reshape(HID, 144)
-    by_tap = jnp.transpose(w_out, (3, 2, 0, 1))
-    by_tap = jnp.concatenate([by_tap[:, k : k + 1] for k in (2, 1, 0)], axis=1)
-    last = jnp.concatenate(
-        [
-            jnp.pad(by_tap, ((0, 0), (k, 1 - k), (0, 0), (0, 0))).reshape(24, HID)
-            for k in range(2)
-        ],
-        axis=1,
-    )
-    flipped_out = w_out[:, :, ::-1, ::-1]
-    last_adj = padded(
-        jnp.transpose(flipped_out, (1, 2, 3, 0)).reshape(HID, 3, 6), 2, 16
-    ).reshape(HID, 48)
-    flipped_in = w_in[:, :, ::-1, ::-1].reshape(HID, WINDOWS, 2, 3, 3)[:, ::-1]
-    first_adj = jnp.transpose(flipped_in, (4, 3, 2, 1, 0)) * inside.astype(BF16)[:, None]
-    first_adj = padded(first_adj.reshape(3, 6, WINDOWS * HID), 1, 8).reshape(24, WINDOWS * HID)
-    return (
-        stepped(first, 48, 3, 240),
-        stepped(mid, 3 * HID, 2, 12 * HID),
-        last,
-        stepped(last_adj, 16, 5, 112),
-        jnp.concatenate([mid_adj, last_adj], axis=1),
-        first_adj,
     )
 
 
@@ -422,33 +496,34 @@
     after = passed(own, -1)
     end = lax.ppermute(own, "tm", [(0, 2), (count - 1, count - 3)])
     own, w_mid = lax.optimization_barrier((own, w_mid))
+    taps = w_mid.reshape(9, HID, HID)
+    mid = jnp.transpose(taps, (1, 0, 2)).reshape(HID, 9 * HID)
+    mid = stepped(mid, 3 * HID, 2, 12 * HID)
+    mid_adj = jnp.transpose(taps[::-1], (2, 0, 1)).reshape(HID, 9 * HID)
     near = jnp.concatenate([before, own, after], axis=0)
-    near, w_in, w_out, noise_gain, step_index, station_rows, station_cols = (
-        lax.optimization_barrier(
-            (near, w_in, w_out, noise_gain, step_index, station_rows, station_cols)
-        )
-    )
     far_before = passed(near, 3)
     far_after = passed(near, -3)
 
     noise_alpha, noise_sigma, obs_kappa = noise_level(step_index)
-    bias = jnp.broadcast_to((noise_sigma * noise_gain)[:, None], (HID, WIDTH))
-    states = place + jnp.arange(-REACH, REACH + 1)
-    inside = ((states >= 0) & (states < count)).astype(F32)
-    weights = matrices(w_in, w_mid, w_out, inside)
-    ends = jnp.stack([place == 2, place == count - 3]).astype(F32)
+    ends = jnp.stack([place == 2, place == count - 3, place]).astype(F32)
     scalars = jnp.concatenate([jnp.stack([noise_alpha, noise_sigma, obs_kappa]), ends])
-    stations = jnp.concatenate([station_rows, station_cols]).reshape(-1, WIDTH)
-
-    first, mid, last, last_adj, back, first_adj = weights
     start = (part * OWN - 3).reshape(1).astype(jnp.int32)
-    begun = REACH * HID
-    small = (bias, first, mid, last, last_adj, back)
-    earlier = score(
-        (0, 1), scalars, start, stations, near, far_before, end, *small, first_adj[:, :begun]
-    )
-    posterior = score(
-        (2, 3, 4),
+    earlier, stations, gains, first, last, last_adj, back, first_adj = begin(
+        count,
+        scalars,
+        start,
+        station_rows.reshape(-1, WIDTH),
+        station_cols.reshape(-1, WIDTH),
+        near,
+        far_before,
+        end,
+        jnp.transpose(w_in, (1, 2, 3, 0)),
+        jnp.transpose(w_out, (2, 3, 0, 1)),
+        noise_gain.reshape(1, HID),
+        mid,
+        mid_adj,
+    )
+    posterior = finish(
         scalars,
         start,
         stations,
@@ -457,8 +532,13 @@
         far_after,
         earlier,
         end,
-        *small,
-        first_adj[:, begun:],
+        gains,
+        first,
+        mid,
+        last,
+        last_adj,
+        back,
+        first_adj,
     )
     return posterior[None]
 

time: 55.5 us -> 54.7 us (0.986)
  local copies, waits for them, and re-layouts: 3.72 us -> 1.45 us
  waiting for transfers between devices: 0.02 us -> 1.03 us
    unnamed x18 -> x14, local copies, waits for them, and re-layouts: 2.25 us -> 0.72 us
    ppermute x4, waiting for transfers between devices: 0.01 us -> 1.02 us  [passed(): return lax.ppermute(value, 'tm', pairs)]
    convert_element_type x1, other arithmetic: 0.01 us -> 0.7 us  [on_device(): low = (observed[0] - high.astype(F32)).astype(BF16)]
  transfers between devices with their start and end apart: 7 -> 7, of which waited for: 0 -> 2; matrix products, arithmetic and copies ran while one was open for 6% -> 4% of each run, Pallas kernels for 10% -> 11%
where the time goes in v5:
time: 54.7 us; the launch traced here: 54.3 us
  starting transfers between devices  34.7 us (63%)
  Pallas kernels  14.3 us (26%)
  other arithmetic  1.7 us (3%)
  local copies, waits for them, and re-layouts  1.45 us (3%)
  between operations  1.06 us (2%)
  waiting for transfers between devices  1.03 us (2%)
    ppermute x4, starting transfers between devices, passed(): return lax.ppermute(value, 'tm', pairs)  21.9 us
    pallas_call x2, Pallas kernels, call(): pl.pallas_call(kernel, out_shape=out_shape, in_specs=[smem, smem] + [vmem...  14.3 us
    ppermute x1, starting transfers between devices, on_device(): far = lax.ppermute(own_state, 'rows', [(1, 2), (2, 1), (3, 0), (0, 3)])  9.58 us
    ppermute x1, starting transfers between devices, on_device(): near = lax.ppermute(own_state, 'rows', [(0, 1), (1, 0), (2, 3), (3, 2)])  2.59 us
  transfers between devices with their start and end apart: 7, of which 2 were waited for; matrix products, arithmetic and copies ran while one was open for 4% of the time, Pallas kernels for 11%

profile of v5, /device:TPU:64, one launch (start us, length us, event | category | flops | bytes accessed | tf_op | source)
XLA Modules:
  0.0 54.3 jit_solution(5607294535208142174)
XLA Ops:
  0.0 9.6 %collective-permute-start = (bf16[2,16,128]{2,1,0:T(8,128)(2,1)}, bf16[2,16,128]{2,1,0:T(8,128)(2,1)S(1)}, u32[]{:S(2)}, u32[]{:S(2)}) collective-permute-start(bf16[2,16,128]{2,1,0:T(8,128)(2,1)} %bitcast.35), channel_id=1, source_target_pairs={{1,2},{2,1},{3,0},{0,3},{5,6},{6,5},{7,4},{4,7},{9,10},{10,9},{11,... | collective-permute-start | bytes 24584 | tf_op jit(solution)/shard_map/ppermute | solution.py:479
  9.6 2.6 %collective-permute-start.1 = (bf16[2,16,128]{2,1,0:T(8,128)(2,1)}, bf16[2,16,128]{2,1,0:T(8,128)(2,1)S(1)}, u32[]{:S(2)}, u32[]{:S(2)}) collective-permute-start(bf16[2,16,128]{2,1,0:T(8,128)(2,1)} %bitcast.36), channel_id=1, source_target_pairs={{0,1},{1,0},{2,3},{3,2},{4,5},{5,4},{6,7},{7,6},{8,9},{9,8},{10,11... | collective-permute-start | bytes 24584 | tf_op jit(solution)/shard_map/ppermute | solution.py:480
  12.2 0.7 %fusion.3 = (bf16[2,1024]{1,0:T(2,128)(2,1)S(1)}, bf16[2,1024]{1,0:T(2,128)(2,1)S(1)}) fusion(f32[1,2,1024]{2,1,0:T(2,128)} %param.10), kind=kLoop, calls=%fused_computation.13 | loop fusion | flops 8192 | bytes 16384 | tf_op jit(solution)/shard_map/convert_element_type | solution.py:482
  12.9 0.7 %pad_maximum_fusion.1 = bf16[64,128]{1,0:T(8,128)(2,1)S(1)} fusion(bf16[32,128]{1,0:T(8,128)(2,1)} %bitcast.37, bf16[32,128]{1,0:T(8,128)(2,1)S(1)} %reshape.42), kind=kLoop, calls=%fused_computation.6 | loop fusion | flops 32768 | bytes 32768 | tf_op jit(solution)/shard_map/concatenate | solution.py:484
  13.6 0.1 add_convert_fusion
  14.6 0.0 collective-permute-done
  14.6 0.0 collective-permute-done.1
  14.6 3.5 %collective-permute-start.2 = (bf16[96,128]{1,0:T(8,128)(2,1)S(1)}, bf16[96,128]{1,0:T(8,128)(2,1)S(1)}, u32[]{:S(2)}, u32[]{:S(2)}) collective-permute-start(bf16[96,128]{1,0:T(8,128)(2,1)S(1)} %pad_maximum_fusion), channel_id=1, source_target_pairs={{0,4},{4,8},{8,12},{12,16},{16,20},{20,24},{24,28},{28,32},{32,36}... | collective-permute-start | bytes 73736 | tf_op jit(solution)/shard_map/ppermute | solution.py:493
  18.1 0.1 pad_maximum_fusion.3.scalars_ref.refs_0_
  18.2 6.6 %collective-permute-start.3 = (bf16[96,128]{1,0:T(8,128)(2,1)S(1)}, bf16[96,128]{1,0:T(8,128)(2,1)S(1)}, u32[]{:S(2)}, u32[]{:S(2)}) collective-permute-start(bf16[96,128]{1,0:T(8,128)(2,1)S(1)} %pad_maximum_fusion), channel_id=1, source_target_pairs={{4,0},{8,4},{12,8},{16,12},{20,16},{24,20},{28,24},{32,28},{36,32}... | collective-permute-start | bytes 73736 | tf_op jit(solution)/shard_map/ppermute | solution.py:493
  24.8 0.7 %collective-permute-start.5 = (bf16[96,128]{1,0:T(8,128)(2,1)S(1)}, bf16[96,128]{1,0:T(8,128)(2,1)S(1)}, u32[]{:S(2)}, u32[]{:S(2)}) collective-permute-start(bf16[96,128]{1,0:T(8,128)(2,1)S(1)} %pad_maximum_fusion), channel_id=1, source_target_pairs={{0,8},{508,500},{1,9},{509,501},{2,10},{510,502},{3,11},{511,503}} | collective-permute-start | bytes 73736 | tf_op jit(solution)/shard_map/ppermute | solution.py:497
  25.4 0.0 copy-done.5
  25.4 0.2 reshape.46
  25.7 0.2 copy.12
  25.8 0.2 copy.13
  26.0 0.0 collective-permute-done.2
  26.0 0.2 collective-permute-done.3
  26.3 5.6 %collective-permute-start.4 = (bf16[288,128]{1,0:T(8,128)(2,1)S(1)}, bf16[288,128]{1,0:T(8,128)(2,1)S(1)}, u32[]{:S(2)}, u32[]{:S(2)}) collective-permute-start(bf16[288,128]{1,0:T(8,128)(2,1)S(1)} %constant_dynamic-update-slice_fusion.near_ref.refs_3_), channel_id=1, source_target_pairs={{0,12},{4,16},{8,20},{12,24},{16,28},{20,32},{24,36},{28,40},{32,4... | collective-permute-start | bytes 221192 | tf_op jit(solution)/shard_map/ppermute | solution.py:493
  31.8 0.1 fusion.2.mid_ref.refs_10_
  32.0 0.0 copy-start
  32.0 0.0 copy-start.3
  32.0 0.2 copy.15.mid_adj_ref
  32.2 6.3 %collective-permute-start.6 = (bf16[288,128]{1,0:T(8,128)(2,1)S(1)}, bf16[288,128]{1,0:T(8,128)(2,1)S(1)}, u32[]{:S(2)}, u32[]{:S(2)}) collective-permute-start(bf16[288,128]{1,0:T(8,128)(2,1)S(1)} %constant_dynamic-update-slice_fusion.near_ref.refs_3_), channel_id=1, source_target_pairs={{12,0},{16,4},{20,8},{24,12},{28,16},{32,20},{36,24},{40,28},{44,3... | collective-permute-start | bytes 221192 | tf_op jit(solution)/shard_map/ppermute | solution.py:493
  38.5 0.0 collective-permute-done.5.end_ref.refs_7_
  38.5 0.8 %collective-permute-done.4.far_before_ref.refs_4_ = bf16[288,128]{1,0:T(8,128)(2,1)S(1)} collective-permute-done((bf16[288,128]{1,0:T(8,128)(2,1)S(1)}, bf16[288,128]{1,0:T(8,128)(2,1)S(1)}, u32[]{:S(2)}, u32[]{:S(2)}) %collective-permute-start.4) | collective-permute-done | bytes 73760 | tf_op jit(solution)/shard_map/ppermute | solution.py:493
  39.3 0.0 copy-done
  39.3 0.0 copy-done.3
  39.3 0.7 %copy-done.1 = bf16[2,96,3,3]{1,0,3,2:T(2,128)(2,1)S(1)} copy-done((bf16[2,96,3,3]{1,0,3,2:T(2,128)(2,1)S(1)}, bf16[2,96,3,3]{1,0,3,2:T(2,128)(2,1)}, u32[]{:S(2)}) %copy-start.1) | copy-done | bytes 3480
  39.9 0.0 copy-done.2
  40.0 5.8 %begin.1 = (f32[144,128]{1,0:T(8,128)S(1)}, s32[16,128]{1,0:T(8,128)S(1)}, f32[96,128]{1,0:T(8,128)S(1)}, bf16[288,240]{1,0:T(8,128)(2,1)S(1)}, bf16[24,192]{1,0...) custom-call(f32[6]{0:T(128)S(1)} %pad_maximum_fusion.3.scalars_ref.refs_0, ...), custom_call_target="tpu_custom_call" | custom-call | flops 2000000000 | bytes 1000000 | tf_op jit(solution)/shard_map/begin/pallas_call | solution.py:406
  45.8 0.0 collective-permute-done.6.refs_5_
  45.8 8.5 %score.1 = f32[2,16,128]{2,1,0:T(8,128)} custom-call(f32[6]{0:T(128)S(1)} %pad_maximum_fusion.3.scalars_ref.refs_0_, s32[1]{0:T(128)} %bitcast.3.first_ref.refs_1_, s32[16,128]{1,0:T(8,128)S(1)} %get-tuple-element.17.refs_2_, bf16[288,128]{1,0:T(8,128)(2,1)S(1)} %constant_dynamic-update-slice_fusion.near_ref.refs_3_, ...), custom_call_target="tpu_custom_call" | custom-call | flops 3000000000 | bytes 1000000 | tf_op jit(solution)/shard_map/score/pallas_call | solution.py:406
  (13 shorter events, 0.1 us)
Async XLA Ops:
  0.0 25.4 %copy-start.5 = (bf16[3,3,9216]{2,1,0:T(4,128)(2,1)S(1)}, bf16[3,3,9216]{2,1,0:T(4,128)(2,1)}, u32[]{:S(2)}) copy-start(bf16[3,3,9216]{2,1,0:T(4,128)(2,1)} %param.15) | copy-start | bytes 497668
  0.0 14.6 %collective-permute-start = (bf16[2,16,128]{2,1,0:T(8,128)(2,1)}, bf16[2,16,128]{2,1,0:T(8,128)(2,1)S(1)}, u32[]{:S(2)}, u32[]{:S(2)}) collective-permute-start(bf16[2,16,128]{2,1,0:T(8,128)(2,1)} %bitcast.35), channel_id=1, source_target_pairs={{1,2},{2,1},{3,0},{0,3},{5,6},{6,5},{7,4},{4,7},{9,10},{10,9},{11,... | collective-permute-start | bytes 24584 | tf_op jit(solution)/shard_map/ppermute | solution.py:479
  9.6 5.0 %collective-permute-start.1 = (bf16[2,16,128]{2,1,0:T(8,128)(2,1)}, bf16[2,16,128]{2,1,0:T(8,128)(2,1)S(1)}, u32[]{:S(2)}, u32[]{:S(2)}) collective-permute-start(bf16[2,16,128]{2,1,0:T(8,128)(2,1)} %bitcast.36), channel_id=1, source_target_pairs={{0,1},{1,0},{2,3},{3,2},{4,5},{5,4},{6,7},{7,6},{8,9},{9,8},{10,11... | collective-permute-start | bytes 24584 | tf_op jit(solution)/shard_map/ppermute | solution.py:480
  14.6 11.4 %collective-permute-start.2 = (bf16[96,128]{1,0:T(8,128)(2,1)S(1)}, bf16[96,128]{1,0:T(8,128)(2,1)S(1)}, u32[]{:S(2)}, u32[]{:S(2)}) collective-permute-start(bf16[96,128]{1,0:T(8,128)(2,1)S(1)} %pad_maximum_fusion), channel_id=1, source_target_pairs={{0,4},{4,8},{8,12},{12,16},{16,20},{20,24},{24,28},{28,32},{32,36}... | collective-permute-start | bytes 73736 | tf_op jit(solution)/shard_map/ppermute | solution.py:493
  18.2 8.1 %collective-permute-start.3 = (bf16[96,128]{1,0:T(8,128)(2,1)S(1)}, bf16[96,128]{1,0:T(8,128)(2,1)S(1)}, u32[]{:S(2)}, u32[]{:S(2)}) collective-permute-start(bf16[96,128]{1,0:T(8,128)(2,1)S(1)} %pad_maximum_fusion), channel_id=1, source_target_pairs={{4,0},{8,4},{12,8},{16,12},{20,16},{24,20},{28,24},{32,28},{36,32}... | collective-permute-start | bytes 73736 | tf_op jit(solution)/shard_map/ppermute | solution.py:493
  24.8 13.7 %collective-permute-start.5 = (bf16[96,128]{1,0:T(8,128)(2,1)S(1)}, bf16[96,128]{1,0:T(8,128)(2,1)S(1)}, u32[]{:S(2)}, u32[]{:S(2)}) collective-permute-start(bf16[96,128]{1,0:T(8,128)(2,1)S(1)} %pad_maximum_fusion), channel_id=1, source_target_pairs={{0,8},{508,500},{1,9},{509,501},{2,10},{510,502},{3,11},{511,503}} | collective-permute-start | bytes 73736 | tf_op jit(solution)/shard_map/ppermute | solution.py:497
  26.3 13.0 %collective-permute-start.4 = (bf16[288,128]{1,0:T(8,128)(2,1)S(1)}, bf16[288,128]{1,0:T(8,128)(2,1)S(1)}, u32[]{:S(2)}, u32[]{:S(2)}) collective-permute-start(bf16[288,128]{1,0:T(8,128)(2,1)S(1)} %constant_dynamic-update-slice_fusion.near_ref.refs_3_), channel_id=1, source_target_pairs={{0,12},{4,16},{8,20},{12,24},{16,28},{20,32},{24,36},{28,40},{32,4... | collective-permute-start | bytes 221192 | tf_op jit(solution)/shard_map/ppermute | solution.py:493
  32.0 7.3 %copy-start = (bf16[96,10,3,3]{0,3,2,1:T(4,128)(2,1)S(1)}, bf16[96,10,3,3]{0,3,2,1:T(4,128)(2,1)}, u32[]{:S(2)}) copy-start(bf16[96,10,3,3]{0,3,2,1:T(4,128)(2,1)} %param.14) | copy-start | bytes 51844
  32.0 7.3 %copy-start.3 = (s32[1024]{0:T(1024)S(1)}, s32[1024]{0:T(1024)}, u32[]{:S(2)}) copy-start(s32[1024]{0:T(1024)} %param.12) | copy-start | bytes 12292
  32.2 13.6 %collective-permute-start.6 = (bf16[288,128]{1,0:T(8,128)(2,1)S(1)}, bf16[288,128]{1,0:T(8,128)(2,1)S(1)}, u32[]{:S(2)}, u32[]{:S(2)}) collective-permute-start(bf16[288,128]{1,0:T(8,128)(2,1)S(1)} %constant_dynamic-update-slice_fusion.near_ref.refs_3_), channel_id=1, source_target_pairs={{12,0},{16,4},{20,8},{24,12},{28,16},{32,20},{36,24},{40,28},{44,3... | collective-permute-start | bytes 221192 | tf_op jit(solution)/shard_map/ppermute | solution.py:493
  39.3 0.7 %copy-start.1 = (bf16[2,96,3,3]{1,0,3,2:T(2,128)(2,1)S(1)}, bf16[2,96,3,3]{1,0,3,2:T(2,128)(2,1)}, u32[]{:S(2)}) copy-start(bf16[2,96,3,3]{1,0,3,2:T(2,128)(2,1)} %param.16) | copy-start | bytes 10372
  39.3 0.7 %copy-start.2 = (s32[1024]{0:T(1024)S(1)}, s32[1024]{0:T(1024)}, u32[]{:S(2)}) copy-start(s32[1024]{0:T(1024)} %param.11) | copy-start | bytes 12292
  39.3 0.7 %copy-start.4 = (f32[96]{0:T(128)S(1)}, f32[96]{0:T(128)}, u32[]{:S(2)}) copy-start(f32[96]{0:T(128)} %param.17) | copy-start | bytes 1156

commit v6 on v5

--- a/solution.py
+++ b/solution.py
@@ -255,7 +255,7 @@
             if s == 3 * REACH:
                 field = field + at_high * end[f]
             for b in range(3):
-                moved[b, 2 * (s - low) + f, :, :] = rolled(field, b - 1)
+                moved[b, 2 * (s - low) + f, pl.ds(0, 32), :] = rolled(field, b - 1)
 
     places = (
         (far_before_ref, 2),
@@ -274,14 +274,14 @@
         seen.append(values)
     *totals, stations = station_sums(first_ref[0], stations_ref, seen)
     for w in range(len(chosen)):
-        sums[w, :, :] = totals[w]
-    count[...] = stations
+        sums[w, pl.ds(0, 2 * SPAN), :] = totals[w]
+    count[pl.ds(0, SPAN), :] = stations
 
     def first_layer(w):
         for b in range(3):
             for channel in range(2 * WINDOWS):
                 blanket[w, pl.ds(16 * b + channel, 32, stride=48), :] = moved[
-                    b, 2 * w + channel, :, :
+                    b, 2 * w + channel, pl.ds(0, 32), :
                 ]
 
         values = dot(w_in_ref[...], side_by_side(blanket.at[w], 96, 144, 240, 9).astype(BF16))
@@ -384,19 +384,19 @@
 
 def buffers(windows):
     return [
-        pltpu.VMEM((3, 2 * (windows + 2 * REACH), 32, WIDTH), F32),
-        pltpu.VMEM((windows, 2 * SPAN, WIDTH), F32),
-        pltpu.VMEM((SPAN, WIDTH), F32),
+        pltpu.VMEM((3, 2 * (windows + 2 * REACH), 40, WIDTH), F32),
+        pltpu.VMEM((windows, 64, WIDTH), F32),
+        pltpu.VMEM((32, WIDTH), F32),
         pltpu.VMEM((windows, 32 * 48, WIDTH), F32),
         pltpu.VMEM((windows, 27 * 3 * HID, WIDTH), BF16),
         pltpu.VMEM((windows, 27 * HID, WIDTH), F32),
         pltpu.VMEM((windows, 24 * HID, WIDTH), F32),
-        pltpu.VMEM((windows, 16 * 8, WIDTH), F32),
-        pltpu.VMEM((windows, SPAN * 16, WIDTH), F32),
+        pltpu.VMEM((windows, 20 * 8, WIDTH), F32),
+        pltpu.VMEM((windows, 32 * 16, WIDTH), F32),
         pltpu.VMEM((windows, 20 * 3 * HID, WIDTH), BF16),
         pltpu.VMEM((18 * windows * HID, WIDTH), BF16),
         pltpu.VMEM((18 * 8, WIDTH), F32),
-        pltpu.VMEM((4, SPAN, WIDTH), F32),
+        pltpu.VMEM((4, 32, WIDTH), F32),
     ]
 
 
@@ -501,6 +501,7 @@
     mid = stepped(mid, 3 * HID, 2, 12 * HID)
     mid_adj = jnp.transpose(taps[::-1], (2, 0, 1)).reshape(HID, 9 * HID)
     near = jnp.concatenate([before, own, after], axis=0)
+    near, w_out = lax.optimization_barrier((near, w_out))
     far_before = passed(near, 3)
     far_after = passed(near, -3)
 
@@ -518,7 +519,7 @@
         far_before,
         end,
         jnp.transpose(w_in, (1, 2, 3, 0)),
-        jnp.transpose(w_out, (2, 3, 0, 1)),
+        jnp.transpose(w_out, (2, 3, 0, 1)).astype(F32),
         noise_gain.reshape(1, HID),
         mid,
         mid_adj,

time: 54.7 us -> 54.5 us (level)
  other arithmetic: 1.7 us -> 1.02 us
    convert_element_type x1, other arithmetic: 0.7 us -> 0.01 us  [on_device(): low = (observed[0] - high.astype(F32)).astype(BF16)]
  transfers between devices with their start and end apart: 7 -> 7, of which waited for: 2 -> 1; matrix products, arithmetic and copies ran while one was open for 4% -> 3% of each run, Pallas kernels for 11% -> 11%
where the time goes in v6:
time: 54.5 us; the launch traced here: 54.1 us
  starting transfers between devices  34.7 us (64%)
  Pallas kernels  14.4 us (26%)
  local copies, waits for them, and re-layouts  1.44 us (3%)
  waiting for transfers between devices  1.41 us (3%)
  between operations  1.06 us (2%)
  other arithmetic  1.02 us (2%)
    ppermute x4, starting transfers between devices, passed(): return lax.ppermute(value, 'tm', pairs)  21.9 us
    pallas_call x2, Pallas kernels, call(): pl.pallas_call(kernel, out_shape=out_shape, in_specs=[smem, smem] + [vmem...  14.4 us
    ppermute x1, starting transfers between devices, on_device(): far = lax.ppermute(own_state, 'rows', [(1, 2), (2, 1), (3, 0), (0, 3)])  9.58 us
    ppermute x1, starting transfers between devices, on_device(): near = lax.ppermute(own_state, 'rows', [(0, 1), (1, 0), (2, 3), (3, 2)])  2.59 us
    ppermute x4, waiting for transfers between devices, passed(): return lax.ppermute(value, 'tm', pairs)  1.4 us
  transfers between devices with their start and end apart: 7, of which 1 were waited for; matrix products, arithmetic and copies ran while one was open for 3% of the time, Pallas kernels for 11%

profile of v6, /device:TPU:64, one launch (start us, length us, event | category | flops | bytes accessed | tf_op | source)
XLA Modules:
  0.0 54.1 jit_solution(7755398849161321199)
XLA Ops:
  0.0 9.6 %collective-permute-start = (bf16[2,16,128]{2,1,0:T(8,128)(2,1)}, bf16[2,16,128]{2,1,0:T(8,128)(2,1)S(1)}, u32[]{:S(2)}, u32[]{:S(2)}) collective-permute-start(bf16[2,16,128]{2,1,0:T(8,128)(2,1)} %bitcast.35), channel_id=1, source_target_pairs={{1,2},{2,1},{3,0},{0,3},{5,6},{6,5},{7,4},{4,7},{9,10},{10,9},{11,... | collective-permute-start | bytes 24584 | tf_op jit(solution)/shard_map/ppermute | solution.py:479
  9.6 2.6 %collective-permute-start.1 = (bf16[2,16,128]{2,1,0:T(8,128)(2,1)}, bf16[2,16,128]{2,1,0:T(8,128)(2,1)S(1)}, u32[]{:S(2)}, u32[]{:S(2)}) collective-permute-start(bf16[2,16,128]{2,1,0:T(8,128)(2,1)} %bitcast.36), channel_id=1, source_target_pairs={{0,1},{1,0},{2,3},{3,2},{4,5},{5,4},{6,7},{7,6},{8,9},{9,8},{10,11... | collective-permute-start | bytes 24584 | tf_op jit(solution)/shard_map/ppermute | solution.py:480
  13.0 0.0 copy-done.5
  13.1 0.7 %pad_maximum_fusion.2 = bf16[64,128]{1,0:T(8,128)(2,1)S(1)} fusion(bf16[32,128]{1,0:T(8,128)(2,1)} %bitcast.37, bf16[32,128]{1,0:T(8,128)(2,1)S(1)} %reshape.42), kind=kLoop, calls=%fused_computation.7 | loop fusion | flops 32768 | bytes 32768 | tf_op jit(solution)/shard_map/concatenate | solution.py:484
  13.8 0.1 add_convert_fusion
  13.9 0.1 pad_maximum_fusion.4.scalars_ref.refs_0_
  14.0 0.0 collective-permute-done
  14.0 0.0 collective-permute-done.1
  14.0 3.5 %collective-permute-start.2 = (bf16[96,128]{1,0:T(8,128)(2,1)S(1)}, bf16[96,128]{1,0:T(8,128)(2,1)S(1)}, u32[]{:S(2)}, u32[]{:S(2)}) collective-permute-start(bf16[96,128]{1,0:T(8,128)(2,1)S(1)} %pad_maximum_fusion.1), channel_id=1, source_target_pairs={{0,4},{4,8},{8,12},{12,16},{16,20},{20,24},{24,28},{28,32},{32,36}... | collective-permute-start | bytes 73736 | tf_op jit(solution)/shard_map/ppermute | solution.py:493
  17.5 6.6 %collective-permute-start.3 = (bf16[96,128]{1,0:T(8,128)(2,1)S(1)}, bf16[96,128]{1,0:T(8,128)(2,1)S(1)}, u32[]{:S(2)}, u32[]{:S(2)}) collective-permute-start(bf16[96,128]{1,0:T(8,128)(2,1)S(1)} %pad_maximum_fusion.1), channel_id=1, source_target_pairs={{4,0},{8,4},{12,8},{16,12},{20,16},{24,20},{28,24},{32,28},{36,32}... | collective-permute-start | bytes 73736 | tf_op jit(solution)/shard_map/ppermute | solution.py:493
  24.1 0.7 %collective-permute-start.5 = (bf16[96,128]{1,0:T(8,128)(2,1)S(1)}, bf16[96,128]{1,0:T(8,128)(2,1)S(1)}, u32[]{:S(2)}, u32[]{:S(2)}) collective-permute-start(bf16[96,128]{1,0:T(8,128)(2,1)S(1)} %pad_maximum_fusion.1), channel_id=1, source_target_pairs={{0,8},{508,500},{1,9},{509,501},{2,10},{510,502},{3,11},{511,503}} | collective-permute-start | bytes 73736 | tf_op jit(solution)/shard_map/ppermute | solution.py:497
  24.7 0.0 copy-done.4
  24.8 0.2 reshape.46
  25.0 0.2 copy.12
  25.1 0.2 copy.13
  25.3 0.1 fusion.2.mid_ref.refs_10_
  25.4 0.2 copy.15.mid_adj_ref
  25.6 0.0 copy-start.6
  25.6 0.0 copy-start
  25.6 0.0 collective-permute-done.2
  25.6 0.0 collective-permute-done.3
  25.7 5.5 %collective-permute-start.4 = (bf16[288,128]{1,0:T(8,128)(2,1)S(1)}, bf16[288,128]{1,0:T(8,128)(2,1)S(1)}, u32[]{:S(2)}, u32[]{:S(2)}) collective-permute-start(bf16[288,128]{1,0:T(8,128)(2,1)S(1)} %pad_maximum_fusion.near_ref.refs_3_), channel_id=1, source_target_pairs={{0,12},{4,16},{8,20},{12,24},{16,28},{20,32},{24,36},{28,40},{32,4... | collective-permute-start | bytes 221192 | tf_op jit(solution)/shard_map/ppermute | solution.py:493
  31.1 6.4 %collective-permute-start.6 = (bf16[288,128]{1,0:T(8,128)(2,1)S(1)}, bf16[288,128]{1,0:T(8,128)(2,1)S(1)}, u32[]{:S(2)}, u32[]{:S(2)}) collective-permute-start(bf16[288,128]{1,0:T(8,128)(2,1)S(1)} %pad_maximum_fusion.near_ref.refs_3_), channel_id=1, source_target_pairs={{12,0},{16,4},{20,8},{24,12},{28,16},{32,20},{36,24},{40,28},{44,3... | collective-permute-start | bytes 221192 | tf_op jit(solution)/shard_map/ppermute | solution.py:493
  37.5 0.0 copy-done.6
  37.6 0.0 collective-permute-done.5.end_ref.refs_7_
  37.6 1.4 %collective-permute-done.4.far_before_ref.refs_4_ = bf16[288,128]{1,0:T(8,128)(2,1)S(1)} collective-permute-done((bf16[288,128]{1,0:T(8,128)(2,1)S(1)}, bf16[288,128]{1,0:T(8,128)(2,1)S(1)}, u32[]{:S(2)}, u32[]{:S(2)}) %collective-permute-start.4) | collective-permute-done | bytes 73760 | tf_op jit(solution)/shard_map/ppermute | solution.py:493
  39.0 0.0 copy-done
  39.0 0.7 %copy-done.2 = s32[1024]{0:T(1024)S(1)} copy-done((s32[1024]{0:T(1024)S(1)}, s32[1024]{0:T(1024)}, u32[]{:S(2)}) %copy-start.2) | copy-done | bytes 4120
  39.7 0.0 copy-done.1
  39.7 5.9 %begin.1 = (f32[144,128]{1,0:T(8,128)S(1)}, s32[16,128]{1,0:T(8,128)S(1)}, f32[96,128]{1,0:T(8,128)S(1)}, bf16[288,240]{1,0:T(8,128)(2,1)S(1)}, bf16[24,192]{1,0...) custom-call(f32[6]{0:T(128)S(1)} %pad_maximum_fusion.4.scalars_ref.refs_0, ...), custom_call_target="tpu_custom_call" | custom-call | flops 2000000000 | bytes 1000000 | tf_op jit(solution)/shard_map/begin/pallas_call | solution.py:406
  45.5 0.0 collective-permute-done.6.refs_5_
  45.5 8.6 %score.1 = f32[2,16,128]{2,1,0:T(8,128)} custom-call(f32[6]{0:T(128)S(1)} %pad_maximum_fusion.4.scalars_ref.refs_0_, s32[1]{0:T(128)} %bitcast.3.first_ref.refs_1_, s32[16,128]{1,0:T(8,128)S(1)} %get-tuple-element.21.refs_2_, bf16[288,128]{1,0:T(8,128)(2,1)S(1)} %pad_maximum_fusion.near_ref.refs_3_, ...), custom_call_target="tpu_custom_call" | custom-call | flops 3000000000 | bytes 1000000 | tf_op jit(solution)/shard_map/score/pallas_call | solution.py:406
  (14 shorter events, 0.1 us)
Async XLA Ops:
  0.0 13.0 %copy-start.5 = (f32[1,2,1024]{2,1,0:T(2,128)S(1)}, f32[1,2,1024]{2,1,0:T(2,128)}, u32[]{:S(2)}) copy-start(f32[1,2,1024]{2,1,0:T(2,128)} %param.10) | copy-start | bytes 24580
  0.0 24.7 %copy-start.4 = (bf16[3,3,9216]{2,1,0:T(4,128)(2,1)S(1)}, bf16[3,3,9216]{2,1,0:T(4,128)(2,1)}, u32[]{:S(2)}) copy-start(bf16[3,3,9216]{2,1,0:T(4,128)(2,1)} %param.15) | copy-start | bytes 497668
  0.0 14.0 %collective-permute-start = (bf16[2,16,128]{2,1,0:T(8,128)(2,1)}, bf16[2,16,128]{2,1,0:T(8,128)(2,1)S(1)}, u32[]{:S(2)}, u32[]{:S(2)}) collective-permute-start(bf16[2,16,128]{2,1,0:T(8,128)(2,1)} %bitcast.35), channel_id=1, source_target_pairs={{1,2},{2,1},{3,0},{0,3},{5,6},{6,5},{7,4},{4,7},{9,10},{10,9},{11,... | collective-permute-start | bytes 24584 | tf_op jit(solution)/shard_map/ppermute | solution.py:479
  9.6 4.4 %collective-permute-start.1 = (bf16[2,16,128]{2,1,0:T(8,128)(2,1)}, bf16[2,16,128]{2,1,0:T(8,128)(2,1)S(1)}, u32[]{:S(2)}, u32[]{:S(2)}) collective-permute-start(bf16[2,16,128]{2,1,0:T(8,128)(2,1)} %bitcast.36), channel_id=1, source_target_pairs={{0,1},{1,0},{2,3},{3,2},{4,5},{5,4},{6,7},{7,6},{8,9},{9,8},{10,11... | collective-permute-start | bytes 24584 | tf_op jit(solution)/shard_map/ppermute | solution.py:480
  14.0 11.6 %collective-permute-start.2 = (bf16[96,128]{1,0:T(8,128)(2,1)S(1)}, bf16[96,128]{1,0:T(8,128)(2,1)S(1)}, u32[]{:S(2)}, u32[]{:S(2)}) collective-permute-start(bf16[96,128]{1,0:T(8,128)(2,1)S(1)} %pad_maximum_fusion.1), channel_id=1, source_target_pairs={{0,4},{4,8},{8,12},{12,16},{16,20},{20,24},{24,28},{28,32},{32,36}... | collective-permute-start | bytes 73736 | tf_op jit(solution)/shard_map/ppermute | solution.py:493
  17.5 8.2 %collective-permute-start.3 = (bf16[96,128]{1,0:T(8,128)(2,1)S(1)}, bf16[96,128]{1,0:T(8,128)(2,1)S(1)}, u32[]{:S(2)}, u32[]{:S(2)}) collective-permute-start(bf16[96,128]{1,0:T(8,128)(2,1)S(1)} %pad_maximum_fusion.1), channel_id=1, source_target_pairs={{4,0},{8,4},{12,8},{16,12},{20,16},{24,20},{28,24},{32,28},{36,32}... | collective-permute-start | bytes 73736 | tf_op jit(solution)/shard_map/ppermute | solution.py:493
  24.1 13.5 %collective-permute-start.5 = (bf16[96,128]{1,0:T(8,128)(2,1)S(1)}, bf16[96,128]{1,0:T(8,128)(2,1)S(1)}, u32[]{:S(2)}, u32[]{:S(2)}) collective-permute-start(bf16[96,128]{1,0:T(8,128)(2,1)S(1)} %pad_maximum_fusion.1), channel_id=1, source_target_pairs={{0,8},{508,500},{1,9},{509,501},{2,10},{510,502},{3,11},{511,503}} | collective-permute-start | bytes 73736 | tf_op jit(solution)/shard_map/ppermute | solution.py:497
  25.6 11.9 %copy-start.6 = (bf16[2,96,3,3]{1,0,3,2:T(2,128)(2,1)S(1)}, bf16[2,96,3,3]{1,0,3,2:T(2,128)(2,1)}, u32[]{:S(2)}) copy-start(bf16[2,96,3,3]{1,0,3,2:T(2,128)(2,1)} %param.16) | copy-start | bytes 10372
  25.6 13.4 %copy-start = (bf16[96,10,3,3]{0,3,2,1:T(4,128)(2,1)S(1)}, bf16[96,10,3,3]{0,3,2,1:T(4,128)(2,1)}, u32[]{:S(2)}) copy-start(bf16[96,10,3,3]{0,3,2,1:T(4,128)(2,1)} %param.14) | copy-start | bytes 51844
  25.7 13.3 %collective-permute-start.4 = (bf16[288,128]{1,0:T(8,128)(2,1)S(1)}, bf16[288,128]{1,0:T(8,128)(2,1)S(1)}, u32[]{:S(2)}, u32[]{:S(2)}) collective-permute-start(bf16[288,128]{1,0:T(8,128)(2,1)S(1)} %pad_maximum_fusion.near_ref.refs_3_), channel_id=1, source_target_pairs={{0,12},{4,16},{8,20},{12,24},{16,28},{20,32},{24,36},{28,40},{32,4... | collective-permute-start | bytes 221192 | tf_op jit(solution)/shard_map/ppermute | solution.py:493
  31.1 14.4 %collective-permute-start.6 = (bf16[288,128]{1,0:T(8,128)(2,1)S(1)}, bf16[288,128]{1,0:T(8,128)(2,1)S(1)}, u32[]{:S(2)}, u32[]{:S(2)}) collective-permute-start(bf16[288,128]{1,0:T(8,128)(2,1)S(1)} %pad_maximum_fusion.near_ref.refs_3_), channel_id=1, source_target_pairs={{12,0},{16,4},{20,8},{24,12},{28,16},{32,20},{36,24},{40,28},{44,3... | collective-permute-start | bytes 221192 | tf_op jit(solution)/shard_map/ppermute | solution.py:493
  39.0 0.7 %copy-start.2 = (s32[1024]{0:T(1024)S(1)}, s32[1024]{0:T(1024)}, u32[]{:S(2)}) copy-start(s32[1024]{0:T(1024)} %param.12) | copy-start | bytes 12292
  39.0 0.7 %copy-start.1 = (s32[1024]{0:T(1024)S(1)}, s32[1024]{0:T(1024)}, u32[]{:S(2)}) copy-start(s32[1024]{0:T(1024)} %param.11) | copy-start | bytes 12292
  39.0 0.7 %copy-start.3 = (f32[96]{0:T(128)S(1)}, f32[96]{0:T(128)}, u32[]{:S(2)}) copy-start(f32[96]{0:T(128)} %param.17) | copy-start | bytes 1156

commit v7 on v6

--- a/solution.py
+++ b/solution.py
@@ -112,13 +112,10 @@
 def arrange(
     place,
     states,
-    rows_ref,
-    cols_ref,
     w_in_ref,
     w_out_ref,
     gain_ref,
     mid_adj_ref,
-    stations_ref,
     gains_ref,
     first_ref,
     last_ref,
@@ -181,8 +178,6 @@
     gain = jnp.broadcast_to(gain_ref[...], (WIDTH, HID))
     gain = jnp.concatenate([gain, jnp.zeros((WIDTH, WIDTH - HID), F32)], axis=1)
     gains_ref[...] = jnp.transpose(gain)[:HID]
-    stations_ref[:8, :] = rows_ref[...]
-    stations_ref[8:, :] = cols_ref[...]
 
 
 def score_kernel(
@@ -417,14 +412,14 @@
     )(*operands)
 
 
-def begin(states, scalars, start, rows, cols, near, far_before, end, w_in, w_out, gain, mid, mid_adj):
+def begin(states, scalars, start, stations, near, far_before, end, w_in, w_out, gain, mid, mid_adj):
     def kernel(
-        scalars_ref, first_ref, rows_ref, cols_ref, near_ref, far_before_ref, end_ref, w_in_ref, w_out_ref,
-        gain_ref, mid_ref, mid_adj_ref, out_ref, stations_ref, gains_ref, layer_ref, last_ref, last_adj_ref,
+        scalars_ref, first_ref, stations_ref, near_ref, far_before_ref, end_ref, w_in_ref, w_out_ref,
+        gain_ref, mid_ref, mid_adj_ref, out_ref, gains_ref, layer_ref, last_ref, last_adj_ref,
         back_ref, adj_later_ref, adj_ref, rows_buffer, *scratch,
     ):
         arrange(
-            scalars_ref[5], states, rows_ref, cols_ref, w_in_ref, w_out_ref, gain_ref, mid_adj_ref, stations_ref,
+            scalars_ref[5], states, w_in_ref, w_out_ref, gain_ref, mid_adj_ref,
             gains_ref, layer_ref, last_ref, last_adj_ref, back_ref, adj_ref, adj_later_ref, rows_buffer,
         )
         score_kernel(
@@ -434,7 +429,6 @@
 
     out_shape = (
         jax.ShapeDtypeStruct((18 * 8, WIDTH), F32),
-        jax.ShapeDtypeStruct((2 * STATIONS // WIDTH, WIDTH), jnp.int32),
         jax.ShapeDtypeStruct((HID, WIDTH), F32),
         jax.ShapeDtypeStruct((3 * HID, 240), BF16),
         jax.ShapeDtypeStruct((24, 2 * HID), BF16),
@@ -443,7 +437,7 @@
         jax.ShapeDtypeStruct((24, (WINDOWS - REACH) * HID), BF16),
     )
     scratch = [pltpu.VMEM((24, REACH * HID), BF16), pltpu.VMEM((352, WIDTH), F32)] + buffers(REACH)
-    operands = (scalars, start, rows, cols, near, far_before, end, w_in, w_out, gain, mid, mid_adj)
+    operands = (scalars, start, stations, near, far_before, end, w_in, w_out, gain, mid, mid_adj)
     return call(kernel, "begin", REACH, out_shape, scratch, operands)
 
 
@@ -501,7 +495,10 @@
     mid = stepped(mid, 3 * HID, 2, 12 * HID)
     mid_adj = jnp.transpose(taps[::-1], (2, 0, 1)).reshape(HID, 9 * HID)
     near = jnp.concatenate([before, own, after], axis=0)
-    near, w_out = lax.optimization_barrier((near, w_out))
+    near, w_out, station_rows, station_cols = lax.optimization_barrier(
+        (near, w_out, station_rows, station_cols)
+    )
+    stations = jnp.concatenate([station_rows, station_cols]).reshape(-1, WIDTH)
     far_before = passed(near, 3)
     far_after = passed(near, -3)
 
@@ -509,12 +506,11 @@
     ends = jnp.stack([place == 2, place == count - 3, place]).astype(F32)
     scalars = jnp.concatenate([jnp.stack([noise_alpha, noise_sigma, obs_kappa]), ends])
     start = (part * OWN - 3).reshape(1).astype(jnp.int32)
-    earlier, stations, gains, first, last, last_adj, back, first_adj = begin(
+    earlier, gains, first, last, last_adj, back, first_adj = begin(
         count,
         scalars,
         start,
-        station_rows.reshape(-1, WIDTH),
-        station_cols.reshape(-1, WIDTH),
+        stations,
         near,
         far_before,
         end,

time: 54.5 us -> 54.4 us (level)
  no operation moved by 1% of the time
where the time goes in v7:
time: 54.4 us; the launch traced here: 54 us
  starting transfers between devices  34.7 us (64%)
  Pallas kernels  14.5 us (27%)
  local copies, waits for them, and re-layouts  1.41 us (3%)
  waiting for transfers between devices  1.27 us (2%)
  between operations  1.09 us (2%)
  other arithmetic  1.03 us (2%)
    ppermute x4, starting transfers between devices, passed(): return lax.ppermute(value, 'tm', pairs)  21.9 us
    pallas_call x2, Pallas kernels, call(): pl.pallas_call(kernel, out_shape=out_shape, in_specs=[smem, smem] + [vmem...  14.5 us
    ppermute x1, starting transfers between devices, on_device(): far = lax.ppermute(own_state, 'rows', [(1, 2), (2, 1), (3, 0), (0, 3)])  9.58 us
    ppermute x1, starting transfers between devices, on_device(): near = lax.ppermute(own_state, 'rows', [(0, 1), (1, 0), (2, 3), (3, 2)])  2.59 us
    ppermute x4, waiting for transfers between devices, passed(): return lax.ppermute(value, 'tm', pairs)  1.27 us
  transfers between devices with their start and end apart: 7, of which 1 were waited for; matrix products, arithmetic and copies ran while one was open for 3% of the time, Pallas kernels for 11%

profile of v7, /device:TPU:64, one launch (start us, length us, event | category | flops | bytes accessed | tf_op | source)
XLA Modules:
  0.0 54.0 jit_solution(18007369768782948129)
XLA Ops:
  0.0 9.6 %collective-permute-start = (bf16[2,16,128]{2,1,0:T(8,128)(2,1)}, bf16[2,16,128]{2,1,0:T(8,128)(2,1)S(1)}, u32[]{:S(2)}, u32[]{:S(2)}) collective-permute-start(bf16[2,16,128]{2,1,0:T(8,128)(2,1)} %bitcast.33), channel_id=1, source_target_pairs={{1,2},{2,1},{3,0},{0,3},{5,6},{6,5},{7,4},{4,7},{9,10},{10,9},{11,... | collective-permute-start | bytes 24584 | tf_op jit(solution)/shard_map/ppermute | solution.py:473
  9.6 2.6 %collective-permute-start.1 = (bf16[2,16,128]{2,1,0:T(8,128)(2,1)}, bf16[2,16,128]{2,1,0:T(8,128)(2,1)S(1)}, u32[]{:S(2)}, u32[]{:S(2)}) collective-permute-start(bf16[2,16,128]{2,1,0:T(8,128)(2,1)} %bitcast.34), channel_id=1, source_target_pairs={{0,1},{1,0},{2,3},{3,2},{4,5},{5,4},{6,7},{7,6},{8,9},{9,8},{10,11... | collective-permute-start | bytes 24584 | tf_op jit(solution)/shard_map/ppermute | solution.py:474
  13.1 0.7 %pad_maximum_fusion.2 = bf16[64,128]{1,0:T(8,128)(2,1)S(1)} fusion(bf16[32,128]{1,0:T(8,128)(2,1)} %bitcast.35, bf16[32,128]{1,0:T(8,128)(2,1)S(1)} %reshape.37), kind=kLoop, calls=%fused_computation.7 | loop fusion | flops 32768 | bytes 32768 | tf_op jit(solution)/shard_map/concatenate | solution.py:478
  13.8 0.1 add_convert_fusion
  13.9 0.1 pad_maximum_fusion.4.scalars_ref.refs_0_
  14.0 0.0 collective-permute-done
  14.0 0.0 collective-permute-done.1
  14.0 3.5 %collective-permute-start.2 = (bf16[96,128]{1,0:T(8,128)(2,1)S(1)}, bf16[96,128]{1,0:T(8,128)(2,1)S(1)}, u32[]{:S(2)}, u32[]{:S(2)}) collective-permute-start(bf16[96,128]{1,0:T(8,128)(2,1)S(1)} %pad_maximum_fusion.1), channel_id=1, source_target_pairs={{0,4},{4,8},{8,12},{12,16},{16,20},{20,24},{24,28},{28,32},{32,36}... | collective-permute-start | bytes 73736 | tf_op jit(solution)/shard_map/ppermute | solution.py:487
  17.5 6.6 %collective-permute-start.3 = (bf16[96,128]{1,0:T(8,128)(2,1)S(1)}, bf16[96,128]{1,0:T(8,128)(2,1)S(1)}, u32[]{:S(2)}, u32[]{:S(2)}) collective-permute-start(bf16[96,128]{1,0:T(8,128)(2,1)S(1)} %pad_maximum_fusion.1), channel_id=1, source_target_pairs={{4,0},{8,4},{12,8},{16,12},{20,16},{24,20},{28,24},{32,28},{36,32}... | collective-permute-start | bytes 73736 | tf_op jit(solution)/shard_map/ppermute | solution.py:487
  24.1 0.7 %collective-permute-start.6 = (bf16[96,128]{1,0:T(8,128)(2,1)S(1)}, bf16[96,128]{1,0:T(8,128)(2,1)S(1)}, u32[]{:S(2)}, u32[]{:S(2)}) collective-permute-start(bf16[96,128]{1,0:T(8,128)(2,1)S(1)} %pad_maximum_fusion.1), channel_id=1, source_target_pairs={{0,8},{508,500},{1,9},{509,501},{2,10},{510,502},{3,11},{511,503}} | collective-permute-start | bytes 73736 | tf_op jit(solution)/shard_map/ppermute | solution.py:491
  24.8 0.2 reshape.41
  25.0 0.2 copy.12
  25.1 0.2 copy.13
  25.3 0.1 fusion.2.mid_ref.refs_10_
  25.4 0.2 copy.15.mid_adj_ref
  25.6 0.0 copy-start.4
  25.6 0.0 collective-permute-done.2
  25.6 0.0 collective-permute-done.3
  25.6 0.0 copy-start.5
  25.6 0.0 copy-start.6
  25.7 0.0 copy-start
  25.7 5.6 %collective-permute-start.4 = (bf16[288,128]{1,0:T(8,128)(2,1)S(1)}, bf16[288,128]{1,0:T(8,128)(2,1)S(1)}, u32[]{:S(2)}, u32[]{:S(2)}) collective-permute-start(bf16[288,128]{1,0:T(8,128)(2,1)S(1)} %pad_maximum_fusion.near_ref.refs_3_), channel_id=1, source_target_pairs={{0,12},{4,16},{8,20},{12,24},{16,28},{20,32},{24,36},{28,40},{32,4... | collective-permute-start | bytes 221192 | tf_op jit(solution)/shard_map/ppermute | solution.py:487
  31.3 6.3 %collective-permute-start.5 = (bf16[288,128]{1,0:T(8,128)(2,1)S(1)}, bf16[288,128]{1,0:T(8,128)(2,1)S(1)}, u32[]{:S(2)}, u32[]{:S(2)}) collective-permute-start(bf16[288,128]{1,0:T(8,128)(2,1)S(1)} %pad_maximum_fusion.near_ref.refs_3_), channel_id=1, source_target_pairs={{12,0},{16,4},{20,8},{24,12},{28,16},{32,20},{36,24},{40,28},{44,3... | collective-permute-start | bytes 221192 | tf_op jit(solution)/shard_map/ppermute | solution.py:487
  37.6 0.0 copy-done.4
  37.6 0.0 copy-done.5
  37.6 0.0 copy-done.6
  37.6 0.0 collective-permute-done.6.end_ref.refs_7_
  37.6 1.3 %collective-permute-done.4.far_before_ref.refs_4_ = bf16[288,128]{1,0:T(8,128)(2,1)S(1)} collective-permute-done((bf16[288,128]{1,0:T(8,128)(2,1)S(1)}, bf16[288,128]{1,0:T(8,128)(2,1)S(1)}, u32[]{:S(2)}, u32[]{:S(2)}) %collective-permute-start.4) | collective-permute-done | bytes 73760 | tf_op jit(solution)/shard_map/ppermute | solution.py:487
  38.9 0.7 %copy-done.1 = f32[96]{0:T(128)S(1)} copy-done((f32[96]{0:T(128)S(1)}, f32[96]{0:T(128)}, u32[]{:S(2)}) %copy-start.1) | copy-done | bytes 408
  39.5 5.9 %begin.1 = (f32[144,128]{1,0:T(8,128)S(1)}, f32[96,128]{1,0:T(8,128)S(1)}, bf16[288,240]{1,0:T(8,128)(2,1)S(1)}, bf16[24,192]{1,0:T(8,128)(2,1)S(1)}, bf16[480,1...) custom-call(f32[6]{0:T(128)S(1)} %pad_maximum_fusion.4.scalars_ref.refs_0_, ...), custom_call_target="tpu_custom_call" | custom-call | flops 2000000000 | bytes 1000000 | tf_op jit(solution)/shard_map/begin/pallas_call | solution.py:401
  45.4 0.0 collective-permute-done.5.refs_5_
  45.4 8.6 %score.1 = f32[2,16,128]{2,1,0:T(8,128)} custom-call(f32[6]{0:T(128)S(1)} %pad_maximum_fusion.4.scalars_ref.refs_0_, s32[1]{0:T(128)} %bitcast.3.first_ref.refs_1_, s32[16,128]{1,0:T(8,128)S(1)} %pad_add_fusion.stations_ref.refs_2_, bf16[288,128]{1,0:T(8,128)(2,1)S(1)} %pad_maximum_fusion.near_ref.refs_3_, ...), custom_call_target="tpu_custom_call" | custom-call | flops 3000000000 | bytes 1000000 | tf_op jit(solution)/shard_map/score/pallas_call | solution.py:401
  (15 shorter events, 0.1 us)
Async XLA Ops:
  0.0 13.0 %copy-start.3 = (f32[1,2,1024]{2,1,0:T(2,128)S(1)}, f32[1,2,1024]{2,1,0:T(2,128)}, u32[]{:S(2)}) copy-start(f32[1,2,1024]{2,1,0:T(2,128)} %param.10) | copy-start | bytes 24580
  0.0 24.7 %copy-start.2 = (bf16[3,3,9216]{2,1,0:T(4,128)(2,1)S(1)}, bf16[3,3,9216]{2,1,0:T(4,128)(2,1)}, u32[]{:S(2)}) copy-start(bf16[3,3,9216]{2,1,0:T(4,128)(2,1)} %param.15) | copy-start | bytes 497668
  0.0 14.0 %collective-permute-start = (bf16[2,16,128]{2,1,0:T(8,128)(2,1)}, bf16[2,16,128]{2,1,0:T(8,128)(2,1)S(1)}, u32[]{:S(2)}, u32[]{:S(2)}) collective-permute-start(bf16[2,16,128]{2,1,0:T(8,128)(2,1)} %bitcast.33), channel_id=1, source_target_pairs={{1,2},{2,1},{3,0},{0,3},{5,6},{6,5},{7,4},{4,7},{9,10},{10,9},{11,... | collective-permute-start | bytes 24584 | tf_op jit(solution)/shard_map/ppermute | solution.py:473
  9.6 4.4 %collective-permute-start.1 = (bf16[2,16,128]{2,1,0:T(8,128)(2,1)}, bf16[2,16,128]{2,1,0:T(8,128)(2,1)S(1)}, u32[]{:S(2)}, u32[]{:S(2)}) collective-permute-start(bf16[2,16,128]{2,1,0:T(8,128)(2,1)} %bitcast.34), channel_id=1, source_target_pairs={{0,1},{1,0},{2,3},{3,2},{4,5},{5,4},{6,7},{7,6},{8,9},{9,8},{10,11... | collective-permute-start | bytes 24584 | tf_op jit(solution)/shard_map/ppermute | solution.py:474
  14.0 11.6 %collective-permute-start.2 = (bf16[96,128]{1,0:T(8,128)(2,1)S(1)}, bf16[96,128]{1,0:T(8,128)(2,1)S(1)}, u32[]{:S(2)}, u32[]{:S(2)}) collective-permute-start(bf16[96,128]{1,0:T(8,128)(2,1)S(1)} %pad_maximum_fusion.1), channel_id=1, source_target_pairs={{0,4},{4,8},{8,12},{12,16},{16,20},{20,24},{24,28},{28,32},{32,36}... | collective-permute-start | bytes 73736 | tf_op jit(solution)/shard_map/ppermute | solution.py:487
  17.5 8.1 %collective-permute-start.3 = (bf16[96,128]{1,0:T(8,128)(2,1)S(1)}, bf16[96,128]{1,0:T(8,128)(2,1)S(1)}, u32[]{:S(2)}, u32[]{:S(2)}) collective-permute-start(bf16[96,128]{1,0:T(8,128)(2,1)S(1)} %pad_maximum_fusion.1), channel_id=1, source_target_pairs={{4,0},{8,4},{12,8},{16,12},{20,16},{24,20},{28,24},{32,28},{36,32}... | collective-permute-start | bytes 73736 | tf_op jit(solution)/shard_map/ppermute | solution.py:487
  24.1 13.6 %collective-permute-start.6 = (bf16[96,128]{1,0:T(8,128)(2,1)S(1)}, bf16[96,128]{1,0:T(8,128)(2,1)S(1)}, u32[]{:S(2)}, u32[]{:S(2)}) collective-permute-start(bf16[96,128]{1,0:T(8,128)(2,1)S(1)} %pad_maximum_fusion.1), channel_id=1, source_target_pairs={{0,8},{508,500},{1,9},{509,501},{2,10},{510,502},{3,11},{511,503}} | collective-permute-start | bytes 73736 | tf_op jit(solution)/shard_map/ppermute | solution.py:491
  25.6 12.0 %copy-start.4 = (bf16[2,96,3,3]{1,0,3,2:T(2,128)(2,1)S(1)}, bf16[2,96,3,3]{1,0,3,2:T(2,128)(2,1)}, u32[]{:S(2)}) copy-start(bf16[2,96,3,3]{1,0,3,2:T(2,128)(2,1)} %param.16) | copy-start | bytes 10372
  25.6 12.0 %copy-start.5 = (s32[1024]{0:T(1024)S(1)}, s32[1024]{0:T(1024)}, u32[]{:S(2)}) copy-start(s32[1024]{0:T(1024)} %param.12) | copy-start | bytes 12292
  25.6 12.0 %copy-start.6 = (s32[1024]{0:T(1024)S(1)}, s32[1024]{0:T(1024)}, u32[]{:S(2)}) copy-start(s32[1024]{0:T(1024)} %param.11) | copy-start | bytes 12292
  25.7 13.2 %copy-start = (bf16[96,10,3,3]{0,3,2,1:T(4,128)(2,1)S(1)}, bf16[96,10,3,3]{0,3,2,1:T(4,128)(2,1)}, u32[]{:S(2)}) copy-start(bf16[96,10,3,3]{0,3,2,1:T(4,128)(2,1)} %param.14) | copy-start | bytes 51844
  25.7 13.2 %collective-permute-start.4 = (bf16[288,128]{1,0:T(8,128)(2,1)S(1)}, bf16[288,128]{1,0:T(8,128)(2,1)S(1)}, u32[]{:S(2)}, u32[]{:S(2)}) collective-permute-start(bf16[288,128]{1,0:T(8,128)(2,1)S(1)} %pad_maximum_fusion.near_ref.refs_3_), channel_id=1, source_target_pairs={{0,12},{4,16},{8,20},{12,24},{16,28},{20,32},{24,36},{28,40},{32,4... | collective-permute-start | bytes 221192 | tf_op jit(solution)/shard_map/ppermute | solution.py:487
  31.3 14.1 %collective-permute-start.5 = (bf16[288,128]{1,0:T(8,128)(2,1)S(1)}, bf16[288,128]{1,0:T(8,128)(2,1)S(1)}, u32[]{:S(2)}, u32[]{:S(2)}) collective-permute-start(bf16[288,128]{1,0:T(8,128)(2,1)S(1)} %pad_maximum_fusion.near_ref.refs_3_), channel_id=1, source_target_pairs={{12,0},{16,4},{20,8},{24,12},{28,16},{32,20},{36,24},{40,28},{44,3... | collective-permute-start | bytes 221192 | tf_op jit(solution)/shard_map/ppermute | solution.py:487
  38.9 0.7 %copy-start.1 = (f32[96]{0:T(128)S(1)}, f32[96]{0:T(128)}, u32[]{:S(2)}) copy-start(f32[96]{0:T(128)} %param.17) | copy-start | bytes 1156
